TPU v7x, 32 devices: a whole 2x2x4 slice. The times are simulated.
32 devices in a mesh: seq: 32 (over z, y, x, core), head: 1.
Axes of the slice: x: 2, y: 2, z: 4, core: 2. Of those that a mesh axis runs over, the one named last changes fastest.
Arguments:
- query_feat: bfloat16 [16384, 512], P('seq', 'head'), may hold values from -6 to 6
- key_feat: bfloat16 [16384, 512], P('seq', 'head'), may hold values from -6 to 6
- values: bfloat16 [16384, 4096], P('seq', 'head'), may hold values from -6 to 6
- conv_query: float32 [3, 512], P(None, 'head'), may hold values from -3 to 3
- conv_key: float32 [3, 512], P(None, 'head'), may hold values from -3 to 3
- conv_value: float32 [3, 4096], P(None, 'head'), may hold values from -3 to 3
- norm_gain: float32 [4096], P('head'), may hold values from 0.1 to 1.9
- out_weight: bfloat16 [4096, 4096], P('head', 'seq'), may hold values from -0.09375 to 0.09375
- stream_ids: int32 [32], replicated, may hold values from 0 to 3, never falling along the last dimension, each value on 1 to 16 neighbouring positions
Outputs:
- mixed: bfloat16 [16384, 4096], P('seq', 'head')
Inputs may be any that keep to these rules, and one draw needn't show every extreme that they name: `stream_ids`: stream ids never fall along the shards; each stream holds 1 to 16 consecutive shards, and one stream holds exactly 16.
All inputs are finite; a program needn't handle non-finite values.
Results may differ from a plain program's by a relative error of at most 0.018.
Values may be sent and summed in bfloat16 or wider, within the bound.
No kernel may reach another device: no remote copies, remote signals or barrier semaphores. Data moves between devices by JAX's collectives and lax.ppermute only.
A program may use at most 320 MiB of HBM per device.

v0:
```python
import jax
import jax.numpy as jnp
from jax import lax
from jax.sharding import PartitionSpec as P

HD = 128
FEAT = 16
TAYLOR = 273


def from_behind(block, axis, distance):
    devices = range(lax.axis_size(axis))
    route = [(i - distance, i) for i in devices if i - distance in devices]
    return lax.ppermute(block, axis, route)


def entering(value, axis, join, neutral):
    count, mine = (lax.axis_size(axis), lax.axis_index(axis))
    pieces = jax.tree.map(lambda part: lax.all_gather(part, axis), value)
    so_far = jax.tree.map(
        lambda part, zero: jnp.full_like(part, 0) + jnp.asarray(zero, part.dtype), value, neutral
    )

    def lap(position, so_far):
        longer = join(so_far, jax.tree.map(lambda part: part[position], pieces))
        return jax.tree.map(lambda new, old: jnp.where(position < mine, new, old), longer, so_far)

    return lax.fori_loop(0, count - 1, lap, so_far)


def taylor(feats):
    scaled = feats * FEAT ** (-0.25)
    outer = (scaled[..., :, None] * scaled[..., None, :]).reshape(
        scaled.shape[:-1] + (FEAT * FEAT,)
    ) * 0.5**0.5
    ones = jnp.ones(scaled.shape[:-1] + (1,), jnp.float32)
    return jnp.concatenate([ones, scaled, outer], axis=-1)


def convolve(inputs, rim_rows, kernel, keep):
    padded = jnp.concatenate(
        [rim_rows.astype(jnp.float32) * keep, inputs.astype(jnp.float32)], axis=0
    )
    return (kernel[0] * padded[:-2] + kernel[1] * padded[1:-1] + kernel[2] * padded[2:]).astype(
        jnp.bfloat16
    )


def segment_combine(earlier, later):
    return (jnp.maximum(earlier[0], later[0]), later[1] + (1.0 - later[0]) * earlier[1])


def on_device(
    query_feat,
    key_feat,
    values,
    conv_query,
    conv_key,
    conv_value,
    norm_gain,
    out_weight,
    stream_ids,
):
    rows = query_feat.shape[0]
    heads = values.shape[1] // HD
    position = lax.axis_index("seq")
    own_stream = stream_ids[position]
    prior_stream = stream_ids[jnp.maximum(position - 1, 0)]
    start_flag = jnp.logical_or(position == 0, own_stream != prior_stream).astype(jnp.float32)
    keep = 1.0 - start_flag
    rim_query, rim_key, rim_value = from_behind(
        (query_feat[-2:], key_feat[-2:], values[-2:]), "seq", 1
    )
    qconv = convolve(query_feat, rim_query, conv_query, keep)
    kconv = convolve(key_feat, rim_key, conv_key, keep)
    vconv = convolve(values, rim_value, conv_value, keep)
    block = min(512, rows)
    nblocks = rows // block
    phq = taylor(qconv.reshape(rows, heads, FEAT).transpose(1, 0, 2).astype(jnp.float32)).astype(
        jnp.bfloat16
    )
    phk = taylor(kconv.reshape(rows, heads, FEAT).transpose(1, 0, 2).astype(jnp.float32)).astype(
        jnp.bfloat16
    )
    phq = phq.reshape(heads, nblocks, block, TAYLOR)
    phk = phk.reshape(heads, nblocks, block, TAYLOR)
    vblock = vconv.reshape(rows, heads, HD).transpose(1, 0, 2).reshape(heads, nblocks, block, HD)
    causal = jnp.tril(jnp.ones((block, block), jnp.float32))
    scores = (
        jnp.einsum("hbif,hbjf->hbij", phq, phk, preferred_element_type=jnp.float32) * causal
    ).astype(jnp.bfloat16)
    local = jnp.einsum("hbij,hbjd->hbid", scores, vblock, preferred_element_type=jnp.float32)
    kvsum = jnp.einsum("hbjf,hbjd->hbfd", phk, vblock, preferred_element_type=jnp.float32)
    running_sum = jnp.cumsum(kvsum, axis=1)
    earlier_blocks = jnp.concatenate([jnp.zeros_like(kvsum), running_sum[:, :-1]], axis=1)
    shard_total = running_sum[:, -1]
    identity = (jnp.zeros((), jnp.float32), jnp.zeros_like(shard_total))
    scanned = entering((start_flag, shard_total), "seq", segment_combine, identity)
    incoming = scanned[1] * keep
    states = incoming[:, None] + earlier_blocks
    carried = jnp.einsum(
        "hbif,hbfd->hbid", phq.astype(jnp.float32), states, precision=lax.Precision.HIGHEST
    )
    result = (local + carried).reshape(heads, rows, HD)
    gains = norm_gain.reshape(heads, HD)
    normed = (
        result
        * lax.rsqrt(jnp.mean(result * result, axis=-1, keepdims=True) + 1e-05)
        * gains[:, None, :]
    )
    hidden = normed.astype(jnp.bfloat16).transpose(1, 0, 2).reshape(rows, heads * HD)
    terms = jnp.dot(
        hidden,
        lax.all_gather(out_weight, "seq", axis=1, tiled=True),
        preferred_element_type=jnp.float32,
    )
    return lax.psum_scatter(terms.astype(jnp.bfloat16), "head", scatter_dimension=1, tiled=True)


def solution(mesh):
    placed = (
        P("seq", "head"),
        P("seq", "head"),
        P("seq", "head"),
        P(None, "head"),
        P(None, "head"),
        P(None, "head"),
        P("head"),
        P("head", "seq"),
        P(),
    )
    return jax.shard_map(
        on_device, mesh=mesh, in_specs=placed, out_specs=P("seq", "head"), check_vma=False
    )
```

profile of v0, /device:TPU:11, one launch (start us, length us, event | category | flops | bytes accessed | tf_op | source)
XLA Modules:
  0.0 1332.0 jit_solution(7529190640488780606)
XLA Ops:
  39.6 9.5 fusion.14
  55.4 46.1 %all-reduce = f32[32]{0:T(128)S(1)} all-reduce(f32[32]{0:T(128)S(1)} %dynamic-update-slice), channel_id=1, replica_groups=mesh['seq'=32,'head'=1] {'seq'}, use_global_device_ids=true, to_apply=%add | all-reduce | flops 32 | bytes 256
  108.7 10.0 fusion.47
  122.0 678.2 %all-gather.6.cloned.1.call-done = f32[1024,273,128]{2,0,1:T(8,128)} async-done(((f32[32,273,128]{2,0,1:T(8,128)}), f32[1024,273,128]{2,0,1:T(8,128)}) %all-gather.6.cloned.1.call-update) | async-done | bytes 143130640 | tf_op jit(solution)/shard_map/all_gather | solution.py:19
  800.2 451.6 %while.14 = (s32[]{:T(128)}, f32[32,273,128]{2,1,0:T(8,128)}, s32[]{:T(128)}, f32[32,32,273,128]{3,1,0,2:T(8,128)}, f32[32]{0:T(128)S(1)}, /*index=5*/s32[]{:T(128)}, f32[1]{0:T(128)}, s32[]{:T(128)}) while((s32[]{:T(128)}, f32[32,273,128]{2,1,0:T(8,128)}, s32[]{:T(128)}, f32[32,32,273,128]{3,1,0,2:T(8,128)}, f32[32]{0:T(128)S(1)}, ...), condition=%wide.region_1.2_spmd.clone, body=%wide.region_0.1_spmd.clone.sunk | while | flops 4472837 | bytes 22364296 | solution.py:28
  819.4 8.5 fusion.52
  833.9 8.9 fusion.52
  848.9 8.6 fusion.52
  863.7 8.6 fusion.52
  878.4 8.5 fusion.52
  893.0 9.0 fusion.52
  908.4 8.5 fusion.52
  923.0 8.9 fusion.52
  938.0 8.6 fusion.52
  952.9 8.5 fusion.52
  982.0 8.6 fusion.52
  996.6 8.5 fusion.52
  1011.2 8.5 fusion.52
  1025.7 8.5 fusion.52
  1069.2 8.5 fusion.52
  1083.7 8.5 fusion.52
  1098.2 8.5 fusion.52
  1112.8 8.5 fusion.52
  1156.3 8.5 fusion.52
  1170.8 8.5 fusion.52
  1185.3 8.5 fusion.52
  1199.8 8.5 fusion.52
  1243.4 8.5 fusion.52
  1251.9 18.1 %fusion.15 = f32[32,512,128]{1,2,0:T(8,128)} fusion(bf16[32,512,256]{1,2,0:T(8,128)(2,1)} %bitcast.65, bf16[32,512,16]{1,2,0:T(8,128)(2,1)S(1)} %bitcast_convert_fusion.1, bf16[273]{0:T(512)(128)(2,1)S(1)} %pad.7.clone, f32[32,273,128]{2,1,0:T(8,128)} %get-tuple-element.99, f32[]{:T(128)S(6)} %sub.17), kind=kOutput, calls=%fused_computation.27 | convolution fusion | flops 6898225152 | bytes 21774886 | tf_op jit(solution)/shard_map/hbif,hbfd->hbid/dot_general | solution.py:101
  1270.0 22.6 %multiply_reduce_fusion = (f32[32,512]{1,0:T(8,128)S(1)}, f32[32,512,128]{1,2,0:T(8,128)}) fusion(f32[32,512,128]{1,2,0:T(8,128)} %fusion.15, bf16[32,512,128]{2,0,1:T(8,128)(2,1)} %bitcast.67, f32[512,512]{1,0:T(8,128)S(1)} %fusion.36, bf16[32,512,256]{1,2,0:T(8,128)(2,1)} %bitcast.64, bf16[32,512,16]{1,2,0:T(8,128)(2,1)S(1)} %copy-done.2, ...), kind=kOutput, calls=%fused_computation.24 | convolution fusion | flops 6804389888 | bytes 39911968 | tf_op jit(solution)/shard_map/hbij,hbjd->hbid/dot_general | solution.py:92
  1292.6 8.8 fusion.13
  1301.3 23.8 %convolution_convert_fusion = bf16[512,4096]{1,0:T(8,128)(2,1)} fusion(bf16[512,4096]{0,1:T(8,128)(2,1)} %bitcast.68, bf16[4096,4096]{1,0:T(8,128)(2,1)} %all-gather.4.cloned.1.call-done), kind=kOutput, calls=%fused_computation.25 | convolution fusion | flops 17181966336 | bytes 41943040 | tf_op jit(solution)/shard_map/dot_general | solution.py:112
  (121 shorter events, 285.1 us)
Async XLA Ops:
  6.5 20.9 %copy-start.5 = (s32[32]{0:T(128)S(1)}, s32[32]{0:T(128)}, u32[]{:S(2)}) copy-start(s32[32]{0:T(128)} %param.19) | copy-start | bytes 388
  6.5 793.7 %all-gather.6.cloned.1.call-start = ((), (), s32[]{:S(2)}) async-start(), calls=%async_computation.1 | async-start | bytes 147603456 | tf_op jit(solution)/shard_map/all_gather | solution.py:19
  7.3 22.2 %collective-permute-start = (bf16[2,512]{1,0:T(2,128)(2,1)S(1)}, bf16[2,512]{1,0:T(2,128)(2,1)S(1)}, u32[]{:S(2)}, u32[]{:S(2)}) collective-permute-start(bf16[2,512]{1,0:T(2,128)(2,1)S(1)} %slice.55), channel_id=1, source_target_pairs={{0,1},{1,2},{2,3},{3,4},{4,5},{5,6},{6,7},{7,8},{8,9},{9,10},{10,1... | collective-permute-start | bytes 6152 | tf_op jit(solution)/shard_map/ppermute | solution.py:14
  11.6 17.8 %collective-permute-start.1 = (bf16[2,512]{1,0:T(2,128)(2,1)S(1)}, bf16[2,512]{1,0:T(2,128)(2,1)S(1)}, u32[]{:S(2)}, u32[]{:S(2)}) collective-permute-start(bf16[2,512]{1,0:T(2,128)(2,1)S(1)} %slice.61), channel_id=1, source_target_pairs={{0,1},{1,2},{2,3},{3,4},{4,5},{5,6},{6,7},{7,8},{8,9},{9,10},{10,1... | collective-permute-start | bytes 6152 | tf_op jit(solution)/shard_map/ppermute | solution.py:14
  14.4 25.1 %collective-permute-start.2 = (bf16[2,4096]{1,0:T(2,128)(2,1)S(1)}, bf16[2,4096]{1,0:T(2,128)(2,1)S(1)}, u32[]{:S(2)}, u32[]{:S(2)}) collective-permute-start(bf16[2,4096]{1,0:T(2,128)(2,1)S(1)} %slice.67), channel_id=1, source_target_pairs={{0,1},{1,2},{2,3},{3,4},{4,5},{5,6},{6,7},{7,8},{8,9},{9,10},{10,1... | collective-permute-start | bytes 49160 | tf_op jit(solution)/shard_map/ppermute | solution.py:14
  32.3 7.2 copy-start
  49.1 52.3 %copy-start.1 = (bf16[512,512]{1,0:T(8,128)(2,1)S(1)}, bf16[512,512]{1,0:T(8,128)(2,1)}, u32[]{:S(2)}) copy-start(bf16[512,512]{1,0:T(8,128)(2,1)} %param.11) | copy-start | bytes 1572868
  49.1 52.6 %copy-start.4 = (f32[3,512]{1,0:T(4,128)S(1)}, f32[3,512]{1,0:T(4,128)}, u32[]{:S(2)}) copy-start(f32[3,512]{1,0:T(4,128)} %param.14) | copy-start | bytes 18436
  54.5 1246.8 %all-gather.4.cloned.1.call-start = ((), (), s32[]{:S(2)}) async-start(), calls=%async_computation | async-start | bytes 34603008 | tf_op jit(solution)/shard_map/all_gather | solution.py:114
  1251.9 18.1 %copy-start.2 = (bf16[32,512,16]{1,2,0:T(8,128)(2,1)S(1)}, bf16[32,512,16]{1,2,0:T(8,128)(2,1)}, u32[]{:S(2)}) copy-start(bf16[32,512,16]{1,2,0:T(8,128)(2,1)} %bitcast_convert_fusion) | copy-start | bytes 1572868
  1270.0 22.6 %copy-start.3 = (f32[4096]{0:T(1024)S(1)}, f32[4096]{0:T(1024)}, u32[]{:S(2)}) copy-start(f32[4096]{0:T(1024)} %param.17) | copy-start | bytes 49156
Sparse Core Ops, SparseCore 0:
  54.6 745.5 all-gather.5
  801.7 193.7 all-gather.3
where the time goes:
time: 1340 us; the launch traced here: 1330 us
  waiting for transfers between devices  679 us (51%)
  other arithmetic  305 us (23%)
  local copies, waits for them, and re-layouts  186 us (14%)
  matrix products  74 us (6%)
  blocking collectives  46.1 us (3%)
  loops' own time  17.8 us (1%)
  between operations  14.9 us (1%)
    all_gather x1, waiting for transfers between devices, entering(): pieces = jax.tree.map(lambda part: lax.all_gather(part, axis), value)  678 us
    select_n x31, other arithmetic, lap(): jnp.where(position < mine, new, old)  263 us
    dynamic_slice x62, local copies, waits for them, and re-layouts, lap(): longer = join(so_far, jax.tree.map(lambda part: part[position], pieces))  170 us
    unnamed x1, blocking collectives  46.1 us
  transfers between devices with their start and end apart: 5, of which 1 were waited for; matrix products, arithmetic and copies ran while one was open for 39% of the time, Pallas kernels for 0%

commit v1 on v0

v1 whole, which is shorter than its diff:
```python
import functools

import jax
import jax.numpy as jnp
from jax import lax
from jax.experimental import pallas as pl
from jax.experimental.pallas import tpu as pltpu
from jax.sharding import PartitionSpec as P

HD = 128
FEAT = 16
GROUP = 8
STATE = 160
BLOCK = 512
VMEM = 56 * 2**20

f32 = jnp.float32
bf16 = jnp.bfloat16


def conv(x_ref, rim_ref, w_ref, pad_ref):
    rows = x_ref.shape[0]
    pad_ref[pl.ds(8, rows), :] = x_ref[...].astype(f32)
    pad_ref[6:8, :] = rim_ref[...]
    return (
        w_ref[0:1] * pad_ref[pl.ds(6, rows), :]
        + w_ref[1:2] * pad_ref[pl.ds(7, rows), :]
        + w_ref[2:3] * pad_ref[pl.ds(8, rows), :]
    ).astype(bf16)


def state_kernel(k_ref, v_ref, rk_ref, rv_ref, ck_ref, cv_ref, kc_ref, vc_ref, kv_ref, kpad, vpad):
    kc = conv(k_ref, rk_ref, ck_ref, kpad)
    kc_ref[...] = kc
    vc_ref[...] = conv(v_ref, rv_ref, cv_ref, vpad)
    kt = (kc.astype(f32) * 0.5).T
    rows = kt.shape[1]
    place = lax.broadcasted_iota(jnp.int32, (FEAT, rows), 0)
    for h in range(GROUP):
        a = kt[FEAT * h : FEAT * (h + 1)]
        parts = [a, a * a] + [a * pltpu.roll(a, d, 0) for d in range(1, 8)]
        last = jnp.where(place >= 8, a * pltpu.roll(a, 8, 0), jnp.where(place == 0, 1.0, 0.0))
        feats = jnp.concatenate([p.astype(bf16) for p in parts + [last]], axis=0)
        kv_ref[h] = jnp.dot(
            feats, vc_ref[:, HD * h : HD * (h + 1)], preferred_element_type=f32
        ).astype(bf16)


def local_kernel(q_ref, rq_ref, cq_ref, kc_ref, vc_ref, qc_ref, loc_ref, qpad):
    qc = conv(q_ref, rq_ref, cq_ref, qpad)
    qc_ref[...] = qc
    rows = qc.shape[0]
    half = rows // 2
    head_of = lax.broadcasted_iota(jnp.int32, qc.shape, 1) // FEAT
    scaled = qc * jnp.asarray(0.25, bf16)
    keys = kc_ref[...]
    causal = lax.broadcasted_iota(jnp.int32, (half, half), 0) >= lax.broadcasted_iota(
        jnp.int32, (half, half), 1
    )
    across = (((1,), (1,)), ((), ()))

    def doubled(s):
        p = s + 1.0
        return p * p + 1.0

    for h in range(GROUP):
        own = jnp.where(head_of == h, scaled, jnp.zeros_like(scaled))
        vh = vc_ref[:, HD * h : HD * (h + 1)]
        s0 = lax.dot_general(own[:half], keys[:half], across, preferred_element_type=f32)
        s1 = lax.dot_general(own[half:], keys, across, preferred_element_type=f32)
        t0 = jnp.where(causal, doubled(s0), 0.0).astype(bf16)
        t10 = doubled(s1[:, :half]).astype(bf16)
        t11 = jnp.where(causal, doubled(s1[:, half:]), 0.0).astype(bf16)
        loc_ref[:half, HD * h : HD * (h + 1)] = 0.5 * jnp.dot(
            t0, vh[:half], preferred_element_type=f32
        )
        loc_ref[half:, HD * h : HD * (h + 1)] = 0.5 * jnp.dot(
            jnp.concatenate([t10, t11], axis=1), vh, preferred_element_type=f32
        )


def hidden_kernel(qc_ref, loc_ref, s_ref, gain_ref, out_ref, wide):
    width = GROUP * FEAT

    @pl.when(pl.program_id(0) == 0)
    def _():
        wide[...] = jnp.zeros_like(wide)

    for h in range(GROUP):
        for d in range(STATE // FEAT):
            wide[width * d + FEAT * h : width * d + FEAT * (h + 1), HD * h : HD * (h + 1)] = s_ref[
                h, FEAT * d : FEAT * (d + 1), :
            ]
    b = qc_ref[...].astype(f32) * 0.5
    place = lax.broadcasted_iota(jnp.int32, b.shape, 1) % FEAT

    def turned(d):
        return jnp.where(place >= d, pltpu.roll(b, d, 1), pltpu.roll(b, width - FEAT + d, 1))

    parts = [b, 0.5 * b * b] + [b * turned(d) for d in range(1, 8)]
    parts.append(jnp.where(place >= 8, b * turned(8), jnp.where(place == 0, 1.0, 0.0)))
    feats = jnp.concatenate([p.astype(bf16) for p in parts], axis=1)
    for h in range(0, GROUP, 2):
        pair = slice(HD * h, HD * (h + 2))
        both = loc_ref[:, pair] + jnp.dot(feats, wide[:, pair], preferred_element_type=f32)
        for e in range(2):
            y = both[:, HD * e : HD * (e + 1)]
            cols = slice(HD * (h + e), HD * (h + e + 1))
            scale = lax.rsqrt(jnp.mean(y * y, axis=-1, keepdims=True) + 1e-05)
            out_ref[:, cols] = (y * scale * gain_ref[:, cols]).astype(bf16)


def params():
    return pltpu.CompilerParams(dimension_semantics=("arbitrary",), vmem_limit_bytes=VMEM)


def flip(x, axis, bit):
    return lax.ppermute(x, axis, [(i, i ^ bit) for i in range(lax.axis_size(axis))])


def after(x, axis, distance):
    n = lax.axis_size(axis)
    return lax.ppermute(x, axis, [(i, i + distance) for i in range(n - distance)])


def entering(kv, ids, axis):
    n, me = lax.axis_size(axis), lax.axis_index(axis)
    half = kv.shape[0] // 2
    core = me % 2
    plane = me - me % 8

    def eq(i, j):
        return (ids[i] == ids[j]).astype(f32)

    first = me - core
    mine = lax.dynamic_slice_in_dim(kv, core * half, half, 0)
    theirs = lax.dynamic_slice_in_dim(kv, (1 - core) * half, half, 0)
    got = flip(theirs, axis, 1)
    kv0 = jnp.where(core == 0, mine, got).astype(f32)
    kv1 = jnp.where(core == 0, got, mine).astype(f32)
    joined = eq(first, first + 1)
    total = (kv1 + joined * kv0).astype(bf16)
    arrived = []
    for bit in (2, 4):
        upper = (me // bit) % 2
        base = me - me % (2 * bit)
        lower_last, upper_last = base + bit - 1, base + 2 * bit - 1
        link = eq(lower_last, upper_last)
        got = flip(total, axis, bit)
        arrived.append((upper * eq(lower_last, first), got))
        total = (
            jnp.where(upper == 1, 1.0, link) * total.astype(f32)
            + jnp.where(upper == 1, link, 1.0) * got.astype(f32)
        ).astype(bf16)
    back = -(-(n // 2 - 1) // 8)
    for step in range(back):
        total = after(total, axis, 8)
        source = plane - 8 * step - 1
        arrived.append(
            ((source >= 0) * eq(jnp.maximum(source, 0), first), total)
        )
    s0 = sum(weight * piece.astype(f32) for weight, piece in arrived)
    s1 = joined * (s0 + kv0)
    keep = jnp.where(core == 0, s0, s1).astype(bf16)
    send = jnp.where(core == 0, s1, s0).astype(bf16)
    got = flip(send, axis, 1)
    low = jnp.where(core == 0, keep, got)
    high = jnp.where(core == 0, got, keep)
    return jnp.concatenate([low, high], axis=0)


def padded(x, width):
    return x if x.shape[-1] == width else jnp.pad(x, ((0, 0), (0, width - x.shape[-1])))


def on_device(
    query_feat,
    key_feat,
    values,
    conv_query,
    conv_key,
    conv_value,
    norm_gain,
    out_weight,
    stream_ids,
):
    rows = query_feat.shape[0]
    width = values.shape[1]
    real = width // HD
    heads = -(-real // GROUP) * GROUP
    groups = heads // GROUP
    fw, vw = GROUP * FEAT, GROUP * HD
    weight = lax.all_gather(out_weight, "seq", axis=1, tiled=True)
    me = lax.axis_index("seq")
    start = jnp.logical_or(me == 0, stream_ids[me] != stream_ids[jnp.maximum(me - 1, 0)])
    keep = 1.0 - start.astype(f32)
    q, k = padded(query_feat, heads * FEAT), padded(key_feat, heads * FEAT)
    v = padded(values, heads * HD)
    cq, ck = padded(conv_query, heads * FEAT), padded(conv_key, heads * FEAT)
    cv = padded(conv_value, heads * HD)
    gain = padded(norm_gain[None], heads * HD)
    rim = after(jnp.concatenate([v[-2:], q[-2:], k[-2:]], axis=1), "seq", 1).astype(f32) * keep

    def cols(n, wide, offset=0):
        return pl.BlockSpec((n, wide), lambda g: (0, offset + g))

    kc, vc, kv = pl.pallas_call(
        state_kernel,
        grid=(groups,),
        in_specs=[
            cols(rows, fw),
            cols(rows, vw),
            cols(2, fw, heads + groups),
            cols(2, vw),
            cols(3, fw),
            cols(3, vw),
        ],
        out_specs=[
            cols(rows, fw),
            cols(rows, vw),
            pl.BlockSpec((GROUP, STATE, HD), lambda g: (g, 0, 0)),
        ],
        out_shape=[
            jax.ShapeDtypeStruct((rows, heads * FEAT), bf16),
            jax.ShapeDtypeStruct((rows, heads * HD), bf16),
            jax.ShapeDtypeStruct((heads, STATE, HD), bf16),
        ],
        scratch_shapes=[pltpu.VMEM((rows + 8, fw), f32), pltpu.VMEM((rows + 8, vw), f32)],
        compiler_params=params(),
        cost_estimate=pl.CostEstimate(
            flops=2 * heads * STATE * rows * HD, bytes_accessed=10 * 2**20, transcendentals=0
        ),
    )(k, v, rim, rim, ck, cv)
    qc, local = pl.pallas_call(
        local_kernel,
        grid=(groups,),
        in_specs=[
            cols(rows, fw),
            cols(2, fw, heads),
            cols(3, fw),
            cols(rows, fw),
            cols(rows, vw),
        ],
        out_specs=[cols(rows, fw), cols(rows, vw)],
        out_shape=[
            jax.ShapeDtypeStruct((rows, heads * FEAT), bf16),
            jax.ShapeDtypeStruct((rows, heads * HD), f32),
        ],
        scratch_shapes=[pltpu.VMEM((rows + 8, fw), f32)],
        compiler_params=params(),
        cost_estimate=pl.CostEstimate(
            flops=2 * heads * rows * rows * 256, bytes_accessed=14 * 2**20, transcendentals=0
        ),
    )(q, rim, cq, kc, vc)
    state = entering(kv, stream_ids, "seq")
    hidden = pl.pallas_call(
        hidden_kernel,
        grid=(groups,),
        in_specs=[
            cols(rows, fw),
            cols(rows, vw),
            pl.BlockSpec((GROUP, STATE, HD), lambda g: (g, 0, 0)),
            cols(1, vw),
        ],
        out_specs=cols(rows, vw),
        out_shape=jax.ShapeDtypeStruct((rows, heads * HD), bf16),
        scratch_shapes=[pltpu.VMEM((STATE * GROUP, vw), bf16)],
        compiler_params=params(),
        cost_estimate=pl.CostEstimate(
            flops=2 * heads * rows * 1280 * HD, bytes_accessed=14 * 2**20, transcendentals=0
        ),
    )(qc, local, state, gain)
    terms = jnp.dot(hidden[:, :width], weight, preferred_element_type=f32)
    return lax.psum_scatter(terms.astype(bf16), "head", scatter_dimension=1, tiled=True)


def solution(mesh):
    placed = (
        P("seq", "head"),
        P("seq", "head"),
        P("seq", "head"),
        P(None, "head"),
        P(None, "head"),
        P(None, "head"),
        P("head"),
        P("head", "seq"),
        P(),
    )
    return jax.shard_map(
        on_device, mesh=mesh, in_specs=placed, out_specs=P("seq", "head"), check_vma=False
    )
```

time: 1340 us -> 278 us (0.21)
  waiting for transfers between devices: 679 us -> 150 us
  other arithmetic: 305 us -> 8.87 us
  local copies, waits for them, and re-layouts: 186 us -> 5.24 us
  matrix products: 74 us -> 23.6 us
  blocking collectives: 46.1 us -> 0 us
  Pallas kernels: 0 us -> 32.7 us
  starting transfers between devices: 9.12 us -> 32.7 us
  loops' own time: 17.8 us -> 0 us
    all_gather x2 -> x1, waiting for transfers between devices: 678 us -> 61.2 us  [on_device(): weight = lax.all_gather(out_weight, 'seq', axis=1, tiled=True)]
    select_n x32 -> x2, other arithmetic: 264 us -> 2.26 us  [the longest x1 2.19 us: entering(): low = jnp.where(core == 0, keep, got)]
    dynamic_slice x63 -> x2, local copies, waits for them, and re-layouts: 171 us -> 2.96 us  [the longest x1 1.73 us: eq(): return (ids[i] == ids[j]).astype(f32)]
    ppermute x3 -> x7, waiting for transfers between devices: 0.01 us -> 87.8 us  [the longest x3 50.5 us: after(): lax.ppermute(x, axis, [(i, i + distance) for i in range(n - distance)])]
    dot_general x4 -> x1, matrix products: 74 us -> 23.6 us  [on_device(): terms = jnp.dot(hidden[:, :width], weight, preferred_element_type=f32)]
    unnamed x1 -> x0, blocking collectives: 46.1 us -> none
    pallas_call x0 -> x3, Pallas kernels: none -> 32.7 us  [the longest x1 12.5 us: on_device(): pl.pallas_call(hidden_kernel, grid=(groups,), in_specs=[cols(rows, fw), c...]
    ppermute x3 -> x7, starting transfers between devices: 9.08 us -> 32.7 us  [the longest x4 19.4 us: flip(): lax.ppermute(x, axis, [(i, i ^ bit) for i in range(lax.axis_size(axis))])]
  transfers between devices with their start and end apart: 5 -> 8, of which waited for: 1 -> 6; matrix products, arithmetic and copies ran while one was open for 39% -> 5% of each run, Pallas kernels for 0% -> 12%
where the time goes in v1:
time: 278 us; the launch traced here: 277 us
  waiting for transfers between devices  150 us (54%)
  starting transfers between devices  32.7 us (12%)
  Pallas kernels  32.7 us (12%)
  between operations  23.9 us (9%)
  matrix products  23.6 us (8%)
  other arithmetic  8.87 us (3%)
  local copies, waits for them, and re-layouts  5.24 us (2%)
    all_gather x1, waiting for transfers between devices, on_device(): weight = lax.all_gather(out_weight, 'seq', axis=1, tiled=True)  61.2 us
    ppermute x3, waiting for transfers between devices, after(): lax.ppermute(x, axis, [(i, i + distance) for i in range(n - distance)])  50.5 us
    ppermute x4, waiting for transfers between devices, flip(): lax.ppermute(x, axis, [(i, i ^ bit) for i in range(lax.axis_size(axis))])  37.3 us
    dot_general x1, matrix products, on_device(): terms = jnp.dot(hidden[:, :width], weight, preferred_element_type=f32)  23.6 us
    ppermute x4, starting transfers between devices, flip(): lax.ppermute(x, axis, [(i, i ^ bit) for i in range(lax.axis_size(axis))])  19.4 us
    ppermute x3, starting transfers between devices, after(): lax.ppermute(x, axis, [(i, i + distance) for i in range(n - distance)])  13.3 us
    pallas_call x1, Pallas kernels, on_device(): pl.pallas_call(hidden_kernel, grid=(groups,), in_specs=[cols(rows, fw), c...  12.5 us
    pallas_call x1, Pallas kernels, on_device(): pl.pallas_call(local_kernel, grid=(groups,), in_specs=[cols(rows, fw), co...  10.9 us
  transfers between devices with their start and end apart: 8, of which 6 were waited for; matrix products, arithmetic and copies ran while one was open for 5% of the time, Pallas kernels for 12%

profile of v1, /device:TPU:11, one launch (start us, length us, event | category | flops | bytes accessed | tf_op | source)
XLA Modules:
  0.0 276.8 jit_solution(13812598558718910133)
XLA Ops:
  6.5 0.7 all-gather.2.cloned.1.call-update
  7.3 0.9 slice.9
  8.1 0.7 slice.10
  8.8 0.7 slice.11
  9.6 3.7 %collective-permute-start = (bf16[2,5120]{1,0:T(2,128)(2,1)S(1)}, bf16[2,5120]{1,0:T(2,128)(2,1)S(1)}, u32[]{:S(2)}, u32[]{:S(2)}) collective-permute-start(bf16[2,5120]{1,0:T(2,128)(2,1)S(1)} %pad_maximum_fusion.1), channel_id=1, source_target_pairs={{0,1},{1,2},{2,3},{3,4},{4,5},{5,6},{6,7},{7,8},{8,9},{9,10},{10,1... | collective-permute-start | bytes 61448 | tf_op jit(solution)/shard_map/ppermute | solution.py:123
  13.3 1.7 fusion.15
  16.3 0.6 convert_multiply_fusion.5.rk_ref.rv_ref.rq_ref
  16.9 9.4 %shard_map.91 = (bf16[512,512]{1,0:T(8,128)(2,1)}, bf16[512,4096]{1,0:T(8,128)(2,1)}, bf16[32,160,128]{2,1,0:T(8,128)(2,1)}) custom-call(bf16[512,512]{1,0:T(8,128)(2,1)} %k_ref.1, bf16[512,4096]{1,0:T(8,128)(2,1)} %v_ref.1, f32[2,5120]{1,0:T(2,128)} %convert_multiply_fusion.5.rk_ref.rv_ref.rq_ref, f32[2,5120]{1,0:T(2,128)} %convert_multiply_fusion.5.rk_ref.rv_ref.rq_ref, ...), custom_call_target="tpu_custom_call" | custom-call | flops 671088640 | bytes 10485760 | tf_op jit(solution)/shard_map/pallas_call | solution.py:207
  26.3 1.2 constant_dynamic-slice_fusion
  27.5 0.1 collective-permute-start.1
  29.0 0.7 collective-permute-done.1
  29.7 0.3 fusion.1
  30.0 0.7 collective-permute-start.2
  32.0 14.3 %collective-permute-done.2 = bf16[16,160,128]{2,1,0:T(8,128)(2,1)S(1)} collective-permute-done((bf16[16,160,128]{2,1,0:T(8,128)(2,1)S(1)}, bf16[16,160,128]{2,1,0:T(8,128)(2,1)S(1)}, u32[]{:S(2)}, u32[]{:S(2)}) %collective-permute-start.2) | collective-permute-done | bytes 655392 | tf_op jit(solution)/shard_map/ppermute | solution.py:118
  46.3 1.1 fusion.11
  47.3 15.5 %collective-permute-start.3 = (bf16[16,160,128]{2,1,0:T(8,128)(2,1)}, bf16[16,160,128]{2,1,0:T(8,128)(2,1)S(1)}, u32[]{:S(2)}, u32[]{:S(2)}) collective-permute-start(bf16[16,160,128]{2,1,0:T(8,128)(2,1)} %fusion.11), channel_id=1, source_target_pairs={{0,4},{1,5},{2,6},{3,7},{4,0},{5,1},{6,2},{7,3},{8,12},{9,13},{10,... | collective-permute-start | bytes 1966088 | tf_op jit(solution)/shard_map/ppermute | solution.py:118
  64.1 22.3 %collective-permute-done.3 = bf16[16,160,128]{2,1,0:T(8,128)(2,1)S(1)} collective-permute-done((bf16[16,160,128]{2,1,0:T(8,128)(2,1)}, bf16[16,160,128]{2,1,0:T(8,128)(2,1)S(1)}, u32[]{:S(2)}, u32[]{:S(2)}) %collective-permute-start.3) | collective-permute-done | bytes 655392 | tf_op jit(solution)/shard_map/ppermute | solution.py:118
  86.4 1.3 fusion.13
  87.8 5.2 %collective-permute-start.4 = (bf16[16,160,128]{2,1,0:T(8,128)(2,1)S(1)}, bf16[16,160,128]{2,1,0:T(8,128)(2,1)}, u32[]{:S(2)}, u32[]{:S(2)}) collective-permute-start(bf16[16,160,128]{2,1,0:T(8,128)(2,1)S(1)} %fusion.13), channel_id=1, source_target_pairs={{0,8},{1,9},{2,10},{3,11},{4,12},{5,13},{6,14},{7,15},{8,16},{9,17... | collective-permute-start | bytes 1966088 | tf_op jit(solution)/shard_map/ppermute | solution.py:123
  93.0 27.9 %collective-permute-done.4 = bf16[16,160,128]{2,1,0:T(8,128)(2,1)} collective-permute-done((bf16[16,160,128]{2,1,0:T(8,128)(2,1)S(1)}, bf16[16,160,128]{2,1,0:T(8,128)(2,1)}, u32[]{:S(2)}, u32[]{:S(2)}) %collective-permute-start.4) | collective-permute-done | bytes 655392 | tf_op jit(solution)/shard_map/ppermute | solution.py:123
  120.9 4.4 %collective-permute-start.5 = (bf16[16,160,128]{2,1,0:T(8,128)(2,1)}, bf16[16,160,128]{2,1,0:T(8,128)(2,1)}, u32[]{:S(2)}, u32[]{:S(2)}) collective-permute-start(bf16[16,160,128]{2,1,0:T(8,128)(2,1)} %collective-permute-done.4), channel_id=1, source_target_pairs={{0,8},{1,9},{2,10},{3,11},{4,12},{5,13},{6,14},{7,15},{8,16},{9,17... | collective-permute-start | bytes 1966088 | tf_op jit(solution)/shard_map/ppermute | solution.py:123
  130.5 22.6 %collective-permute-done.5 = bf16[16,160,128]{2,1,0:T(8,128)(2,1)} collective-permute-done((bf16[16,160,128]{2,1,0:T(8,128)(2,1)}, bf16[16,160,128]{2,1,0:T(8,128)(2,1)}, u32[]{:S(2)}, u32[]{:S(2)}) %collective-permute-start.5) | collective-permute-done | bytes 655392 | tf_op jit(solution)/shard_map/ppermute | solution.py:123
  153.1 2.1 fusion.6
  155.1 3.2 %collective-permute-start.6 = (bf16[16,160,128]{2,1,0:T(8,128)(2,1)S(1)}, bf16[16,160,128]{2,1,0:T(8,128)(2,1)S(1)}, u32[]{:S(2)}, u32[]{:S(2)}) collective-permute-start(bf16[16,160,128]{2,1,0:T(8,128)(2,1)S(1)} %fusion.6), channel_id=1, source_target_pairs={{0,1},{1,0},{2,3},{3,2},{4,5},{5,4},{6,7},{7,6},{8,9},{9,8},{10,11... | collective-permute-start | bytes 1966088 | tf_op jit(solution)/shard_map/ppermute | solution.py:118
  158.3 10.9 %shard_map.92 = (bf16[512,512]{1,0:T(8,128)(2,1)}, f32[512,4096]{1,0:T(8,128)}) custom-call(bf16[512,512]{1,0:T(8,128)(2,1)} %q_ref.1, f32[2,5120]{1,0:T(2,128)} %convert_multiply_fusion.5.rk_ref.rv_ref.rq_ref, f32[3,512]{1,0:T(4,128)} %cq_ref.1, bf16[512,512]{1,0:T(8,128)(2,1)} %get-tuple-element.10.kc_ref, bf16[512,4096]{1,0:T(8,128)(2,1)} %get-tuple-element.11.vc_ref), custom_call_target="tpu_custom_call" | custom-call | flops 4294967296 | bytes 14680064 | tf_op jit(solution)/shard_map/pallas_call | solution.py:234
  169.2 0.0 collective-permute-done.6
  169.2 2.2 broadcast_select_fusion.1
  171.4 0.1 broadcast_select_fusion
  171.5 1.2 pad_maximum_fusion.s_ref
  172.6 12.5 %shard_map.93 = bf16[512,4096]{1,0:T(8,128)(2,1)} custom-call(bf16[512,512]{1,0:T(8,128)(2,1)} %get-tuple-element.12.qc_ref, f32[512,4096]{1,0:T(8,128)} %get-tuple-element.13.loc_ref, bf16[32,160,128]{2,1,0:T(8,128)(2,1)} %pad_maximum_fusion.s_ref, f32[1,4096]{1,0:T(1,128)} %bitcast.11), custom_call_target="tpu_custom_call" | custom-call | flops 5368709120 | bytes 14680064 | tf_op jit(solution)/shard_map/pallas_call | solution.py:256
  185.1 61.2 %all-gather.2.cloned.1.call-done = bf16[4096,4096]{1,0:T(8,128)(2,1)} async-done(((bf16[4096,128]{1,0:T(8,128)(2,1)}), bf16[4096,4096]{1,0:T(8,128)(2,1)}) %all-gather.2.cloned.1.call-update) | async-done | bytes 33554448 | tf_op jit(solution)/shard_map/all_gather | solution.py:193
  246.3 23.6 %convolution_convert_fusion = bf16[512,4096]{1,0:T(8,128)(2,1)} fusion(bf16[512,4096]{1,0:T(8,128)(2,1)} %shard_map.93, bf16[4096,4096]{1,0:T(8,128)(2,1)} %all-gather.2.cloned.1.call-done), kind=kOutput, calls=%fused_computation | convolution fusion | flops 17181966336 | bytes 41943040 | tf_op jit(solution)/shard_map/dot_general | solution.py:273
  (5 shorter events, 0.0 us)
Async XLA Ops:
  6.5 239.8 %all-gather.2.cloned.1.call-start = ((), (), s32[]{:S(2)}) async-start(), calls=%async_computation | async-start | bytes 34603008 | tf_op jit(solution)/shard_map/all_gather | solution.py:193
  9.6 6.7 %collective-permute-start = (bf16[2,5120]{1,0:T(2,128)(2,1)S(1)}, bf16[2,5120]{1,0:T(2,128)(2,1)S(1)}, u32[]{:S(2)}, u32[]{:S(2)}) collective-permute-start(bf16[2,5120]{1,0:T(2,128)(2,1)S(1)} %pad_maximum_fusion.1), channel_id=1, source_target_pairs={{0,1},{1,2},{2,3},{3,4},{4,5},{5,6},{6,7},{7,8},{8,9},{9,10},{10,1... | collective-permute-start | bytes 61448 | tf_op jit(solution)/shard_map/ppermute | solution.py:123
  26.3 3.4 %copy-start = (bf16[32,160,128]{2,1,0:T(8,128)(2,1)S(1)}, bf16[32,160,128]{2,1,0:T(8,128)(2,1)}, u32[]{:S(2)}) copy-start(bf16[32,160,128]{2,1,0:T(8,128)(2,1)} %get-tuple-element.14) | copy-start | bytes 3932164
  27.5 2.2 collective-permute-start.1
  30.0 16.3 %collective-permute-start.2 = (bf16[16,160,128]{2,1,0:T(8,128)(2,1)S(1)}, bf16[16,160,128]{2,1,0:T(8,128)(2,1)S(1)}, u32[]{:S(2)}, u32[]{:S(2)}) collective-permute-start(bf16[16,160,128]{2,1,0:T(8,128)(2,1)S(1)} %fusion.1), channel_id=1, source_target_pairs={{0,2},{1,3},{2,0},{3,1},{4,6},{5,7},{6,4},{7,5},{8,10},{9,11},{10,... | collective-permute-start | bytes 1966088 | tf_op jit(solution)/shard_map/ppermute | solution.py:118
  47.3 39.1 %collective-permute-start.3 = (bf16[16,160,128]{2,1,0:T(8,128)(2,1)}, bf16[16,160,128]{2,1,0:T(8,128)(2,1)S(1)}, u32[]{:S(2)}, u32[]{:S(2)}) collective-permute-start(bf16[16,160,128]{2,1,0:T(8,128)(2,1)} %fusion.11), channel_id=1, source_target_pairs={{0,4},{1,5},{2,6},{3,7},{4,0},{5,1},{6,2},{7,3},{8,12},{9,13},{10,... | collective-permute-start | bytes 1966088 | tf_op jit(solution)/shard_map/ppermute | solution.py:118
  87.8 33.1 %collective-permute-start.4 = (bf16[16,160,128]{2,1,0:T(8,128)(2,1)S(1)}, bf16[16,160,128]{2,1,0:T(8,128)(2,1)}, u32[]{:S(2)}, u32[]{:S(2)}) collective-permute-start(bf16[16,160,128]{2,1,0:T(8,128)(2,1)S(1)} %fusion.13), channel_id=1, source_target_pairs={{0,8},{1,9},{2,10},{3,11},{4,12},{5,13},{6,14},{7,15},{8,16},{9,17... | collective-permute-start | bytes 1966088 | tf_op jit(solution)/shard_map/ppermute | solution.py:123
  120.9 32.2 %collective-permute-start.5 = (bf16[16,160,128]{2,1,0:T(8,128)(2,1)}, bf16[16,160,128]{2,1,0:T(8,128)(2,1)}, u32[]{:S(2)}, u32[]{:S(2)}) collective-permute-start(bf16[16,160,128]{2,1,0:T(8,128)(2,1)} %collective-permute-done.4), channel_id=1, source_target_pairs={{0,8},{1,9},{2,10},{3,11},{4,12},{5,13},{6,14},{7,15},{8,16},{9,17... | collective-permute-start | bytes 1966088 | tf_op jit(solution)/shard_map/ppermute | solution.py:123
  155.1 14.1 %collective-permute-start.6 = (bf16[16,160,128]{2,1,0:T(8,128)(2,1)S(1)}, bf16[16,160,128]{2,1,0:T(8,128)(2,1)S(1)}, u32[]{:S(2)}, u32[]{:S(2)}) collective-permute-start(bf16[16,160,128]{2,1,0:T(8,128)(2,1)S(1)} %fusion.6), channel_id=1, source_target_pairs={{0,1},{1,0},{2,3},{3,2},{4,5},{5,4},{6,7},{7,6},{8,9},{9,8},{10,11... | collective-permute-start | bytes 1966088 | tf_op jit(solution)/shard_map/ppermute | solution.py:118
Sparse Core Ops, SparseCore 0:
  8.9 237.4 all-gather.1

commit v2 on v1

v2 whole, which is shorter than its diff:
```python
import functools

import jax
import jax.numpy as jnp
from jax import lax
from jax.experimental import pallas as pl
from jax.experimental.pallas import tpu as pltpu
from jax.sharding import PartitionSpec as P

HD = 128
FEAT = 16
GROUP = 8
STATE = 160
BLOCK = 512
VMEM = 56 * 2**20

f32 = jnp.float32
bf16 = jnp.bfloat16


def conv(x_ref, rim_ref, w_ref, pad_ref):
    rows = x_ref.shape[0]
    pad_ref[pl.ds(8, rows), :] = x_ref[...].astype(f32)
    pad_ref[6:8, :] = rim_ref[...]
    return (
        w_ref[0:1] * pad_ref[pl.ds(6, rows), :]
        + w_ref[1:2] * pad_ref[pl.ds(7, rows), :]
        + w_ref[2:3] * pad_ref[pl.ds(8, rows), :]
    ).astype(bf16)


def state_kernel(start_ref, k_ref, v_ref, rk_ref, rv_ref, ck_ref, cv_ref, *refs):
    kc_ref, vc_ref, kv_ref, kpad, vpad = refs[-5:]
    kc = conv(k_ref, rk_ref, ck_ref, kpad)
    kc_ref[...] = kc
    vc_ref[...] = conv(v_ref, rv_ref, cv_ref, vpad)
    kt = (kc.astype(f32) * 0.5).T
    rows = kt.shape[1]
    place = lax.broadcasted_iota(jnp.int32, (FEAT, rows), 0)
    for h in range(GROUP):
        a = kt[FEAT * h : FEAT * (h + 1)]
        parts = [a, a * a] + [a * pltpu.roll(a, d, 0) for d in range(1, 8)]
        last = jnp.where(place >= 8, a * pltpu.roll(a, 8, 0), jnp.where(place == 0, 1.0, 0.0))
        feats = jnp.concatenate([p.astype(bf16) for p in parts + [last]], axis=0)
        kv_ref[h] = jnp.dot(
            feats, vc_ref[:, HD * h : HD * (h + 1)], preferred_element_type=f32
        ).astype(bf16)


def local_kernel(q_ref, rq_ref, cq_ref, kc_ref, vc_ref, *refs):
    qc_ref, loc_ref, qpad = refs[-3:]
    qc = conv(q_ref, rq_ref, cq_ref, qpad)
    qc_ref[...] = qc
    rows = qc.shape[0]
    half = rows // 2
    head_of = lax.broadcasted_iota(jnp.int32, qc.shape, 1) // FEAT
    scaled = qc * jnp.asarray(0.25, bf16)
    keys = kc_ref[...]
    causal = lax.broadcasted_iota(jnp.int32, (half, half), 0) >= lax.broadcasted_iota(
        jnp.int32, (half, half), 1
    )
    across = (((1,), (1,)), ((), ()))

    def doubled(s):
        p = s + 1.0
        return p * p + 1.0

    for h in range(GROUP):
        own = jnp.where(head_of == h, scaled, jnp.zeros_like(scaled))
        vh = vc_ref[:, HD * h : HD * (h + 1)]
        s0 = lax.dot_general(own[:half], keys[:half], across, preferred_element_type=f32)
        s1 = lax.dot_general(own[half:], keys, across, preferred_element_type=f32)
        t0 = jnp.where(causal, doubled(s0), 0.0).astype(bf16)
        t10 = doubled(s1[:, :half]).astype(bf16)
        t11 = jnp.where(causal, doubled(s1[:, half:]), 0.0).astype(bf16)
        loc_ref[:half, HD * h : HD * (h + 1)] = 0.5 * jnp.dot(
            t0, vh[:half], preferred_element_type=f32
        )
        loc_ref[half:, HD * h : HD * (h + 1)] = 0.5 * jnp.dot(
            jnp.concatenate([t10, t11], axis=1), vh, preferred_element_type=f32
        )


def hidden_kernel(start_ref, qc_ref, loc_ref, s_ref, gain_ref, out_ref, wide):
    width = GROUP * FEAT

    @pl.when(pl.program_id(0) == 0)
    def _():
        wide[...] = jnp.zeros_like(wide)

    for h in range(GROUP):
        for d in range(STATE // FEAT):
            wide[width * d + FEAT * h : width * d + FEAT * (h + 1), HD * h : HD * (h + 1)] = s_ref[
                h, FEAT * d : FEAT * (d + 1), :
            ]
    b = qc_ref[...].astype(f32) * 0.5
    place = lax.broadcasted_iota(jnp.int32, b.shape, 1) % FEAT

    def turned(d):
        return jnp.where(place >= d, pltpu.roll(b, d, 1), pltpu.roll(b, width - FEAT + d, 1))

    parts = [b, 0.5 * b * b] + [b * turned(d) for d in range(1, 8)]
    parts.append(jnp.where(place >= 8, b * turned(8), jnp.where(place == 0, 1.0, 0.0)))
    feats = jnp.concatenate([p.astype(bf16) for p in parts], axis=1)
    for h in range(0, GROUP, 2):
        pair = slice(HD * h, HD * (h + 2))
        both = loc_ref[:, pair] + jnp.dot(feats, wide[:, pair], preferred_element_type=f32)
        for e in range(2):
            y = both[:, HD * e : HD * (e + 1)]
            cols = slice(HD * (h + e), HD * (h + e + 1))
            scale = lax.rsqrt(jnp.mean(y * y, axis=-1, keepdims=True) + 1e-05)
            out_ref[:, cols] = (y * scale * gain_ref[:, cols]).astype(bf16)


def project_kernel(pieces, own, far, first_ref, place_ref, *refs):
    sides = own + far
    hidden, weights = refs[: 2 * sides], refs[2 * sides : 2 * sides + pieces]
    rows_in, held, done, hid_sems, sems, out_sems = refs[-6:]
    outs = refs[-6 - sides : -6]
    depth = hidden[0].shape[1]
    loads = []
    for p in range(2 * sides):
        turned = p + (0 if own and p < 2 else 1)
        at = pl.multiple_of((first_ref[0] + turned) % 2 * depth, depth)
        loads.append(
            pltpu.make_async_copy(
                hidden[p], rows_in.at[p // 2, :, pl.ds(at, depth)], hid_sems.at[p]
            )
        )
    copies = [
        pltpu.make_async_copy(weights[i], held.at[:, HD * i : HD * (i + 1)], sems.at[i])
        for i in range(pieces)
    ]
    groups = [range(c, min(c + 4, pieces)) for c in range(0, pieces, 4)]
    for copy in loads[:2] + copies[:4] + loads[2:] + copies[4:8]:
        copy.start()
    for copy in loads[:2]:
        copy.wait()
    stores = []
    for at, group in enumerate(groups):
        for copy in copies[4 * at : 4 * (at + 1)]:
            copy.wait()
        for copy in copies[4 * (at + 2) : 4 * (at + 3)]:
            copy.start()
        cols = slice(HD * group[0], HD * (group[-1] + 1))
        if own:
            mine = jnp.dot(rows_in[0], held[:, cols], preferred_element_type=f32).astype(bf16)
            for j, i in enumerate(group):
                done[i] = mine[:, HD * j : HD * (j + 1)]
                where = pl.multiple_of(place_ref[i] * HD, HD)
                store = pltpu.make_async_copy(
                    done.at[i], outs[0].at[:, pl.ds(where, HD)], out_sems.at[i]
                )
                store.start()
                stores.append(store)
        if at == 0:
            for copy in loads[2:]:
                copy.wait()
        if far:
            theirs = jnp.dot(rows_in[sides - 1], held[:, cols], preferred_element_type=f32)
            for j, i in enumerate(group):
                outs[-1][i] = theirs[:, HD * j : HD * (j + 1)].astype(bf16)
    for store in stores:
        store.wait()


def project(own, far, first, width, pieces, places, before=()):
    rows, half = (own + far)[0].shape
    count, depth = len(pieces), pieces[0].shape[0]
    smem, vmem, anywhere = (pl.BlockSpec(memory_space=m) for m in (pltpu.SMEM, pltpu.VMEM, pl.ANY))
    sides = [bool(own), bool(far)]
    outs = [
        (anywhere, jax.ShapeDtypeStruct((rows, width), bf16)),
        (vmem, jax.ShapeDtypeStruct((count, rows, HD), bf16)),
    ]
    outs = [o for o, wanted in zip(outs, sides) if wanted]
    return pl.pallas_call(
        functools.partial(project_kernel, count, *sides),
        in_specs=[smem] * 2 + [anywhere] * (2 * sum(sides) + count + len(before)),
        out_specs=[o[0] for o in outs],
        out_shape=[o[1] for o in outs],
        scratch_shapes=[
            pltpu.VMEM((sum(sides), rows, 2 * half), bf16),
            pltpu.VMEM((depth, HD * count), bf16),
            pltpu.VMEM((count, rows, HD), bf16),
            pltpu.SemaphoreType.DMA((4,)),
            pltpu.SemaphoreType.DMA((count,)),
            pltpu.SemaphoreType.DMA((count,)),
        ],
        input_output_aliases={2 + 2 * sum(sides) + count: 0} if before else {},
        compiler_params=pltpu.CompilerParams(vmem_limit_bytes=VMEM),
        cost_estimate=cost(count),
    )(first, places, *own, *far, *pieces, *before)


def place_kernel(counts, place_ref, *refs):
    blocks, out_ref, sems = refs[: len(counts)], refs[-2], refs[-1]
    copies = []
    for ref, count in zip(blocks, counts):
        for i in range(count):
            at = len(copies)
            where = pl.multiple_of(place_ref[at] * HD, HD)
            copy = pltpu.make_async_copy(ref.at[i], out_ref.at[:, pl.ds(where, HD)], sems.at[at])
            copy.start()
            copies.append(copy)
    for copy in copies:
        copy.wait()


def place(blocks, places, out):
    counts = [b.shape[0] for b in blocks]
    smem, vmem, anywhere = (pl.BlockSpec(memory_space=m) for m in (pltpu.SMEM, pltpu.VMEM, pl.ANY))
    return pl.pallas_call(
        functools.partial(place_kernel, counts),
        in_specs=[smem] + [vmem] * len(blocks) + [anywhere],
        out_specs=anywhere,
        out_shape=jax.ShapeDtypeStruct(out.shape, bf16),
        scratch_shapes=[pltpu.SemaphoreType.DMA((sum(counts),))],
        input_output_aliases={1 + len(blocks): 0},
        compiler_params=pltpu.CompilerParams(vmem_limit_bytes=VMEM),
        cost_estimate=cost(3),
    )(places, *blocks, out)


def ring(n):
    order = list(range(n))
    return order[:1] + order[1::2] + order[2::2][::-1]


def turn(x, axis):
    order = ring(lax.axis_size(axis) // 8)
    route = []
    for at, plane in enumerate(order):
        onto = order[(at + 1) % len(order)]
        route += [(plane * 8 + i, onto * 8 + i) for i in range(8)]
    return lax.ppermute(x, axis, route)


def flip(x, axis, bit):
    return lax.ppermute(x, axis, [(i, i ^ bit) for i in range(lax.axis_size(axis))])


def after(x, axis, distance):
    n = lax.axis_size(axis)
    return lax.ppermute(x, axis, [(i, i + distance) for i in range(n - distance)])


def tie(x, *others):
    return lax.optimization_barrier((x, *others))[0]


def cost(micros):
    return pl.CostEstimate(flops=micros * 2 * 10**10, bytes_accessed=2**20, transcendentals=0)


def params():
    return pltpu.CompilerParams(dimension_semantics=("arbitrary",), vmem_limit_bytes=VMEM)


class Scan:
    def __init__(self, ids, axis):
        self.ids, self.axis = ids, axis
        self.n, self.me = lax.axis_size(axis), lax.axis_index(axis)
        self.core = self.me % 2
        self.first = self.me - self.core
        self.plane = self.me - self.me % 8
        self.sums = 0.0

    def eq(self, i, j):
        return (self.ids[i] == self.ids[j]).astype(f32)

    def chip(self, mine, got):
        self.kv0 = jnp.where(self.core == 0, mine, got)
        kv1 = jnp.where(self.core == 0, got, mine)
        self.joined = self.eq(self.first, self.first + 1)
        self.total = (kv1.astype(f32) + self.joined * self.kv0.astype(f32)).astype(bf16)

    def hop(self, bit):
        return flip(self.total, self.axis, bit)

    def merge(self, bit, got):
        upper = (self.me // bit) % 2
        base = self.me - self.me % (2 * bit)
        lower_last, upper_last = base + bit - 1, base + 2 * bit - 1
        link = self.eq(lower_last, upper_last)
        got = got.astype(f32)
        self.sums = self.sums + upper * self.eq(lower_last, self.first) * got
        self.total = (
            jnp.where(upper == 1, 1.0, link) * self.total.astype(f32)
            + jnp.where(upper == 1, link, 1.0) * got
        ).astype(bf16)

    def climbs(self):
        return -(-(self.n // 2 - 1) // 8)

    def cut(self):
        part = self.total.shape[0] // 4
        spot = self.me // 2 % 4
        self.total = lax.dynamic_slice_in_dim(self.total, spot * part, part, 0)
        self.below = 0.0

    def climb(self, step):
        self.total = after(self.total, self.axis, 8)
        source = self.plane - 8 * step - 1
        same = (source >= 0) * self.eq(jnp.maximum(source, 0), self.plane)
        self.below = self.below + same * self.total.astype(f32)
        return self.total

    def gather_hop(self, bit):
        self.below = self.below.astype(bf16)
        return flip(self.below, self.axis, bit)

    def gather(self, bit, got):
        below = self.below
        upper = (self.me // bit) % 2 == 1
        self.below = jnp.concatenate(
            [jnp.where(upper, got, below), jnp.where(upper, below, got)], axis=0
        )

    def finish(self):
        s0 = self.sums + self.eq(self.plane, self.first) * self.below.astype(f32)
        s1 = self.joined * (s0 + self.kv0.astype(f32))
        keep = jnp.where(self.core == 0, s0, s1).astype(bf16)
        send = jnp.where(self.core == 0, s1, s0).astype(bf16)
        return keep, flip(send, self.axis, 1)


def padded(x, width):
    return x if x.shape[-1] == width else jnp.pad(x, ((0, 0), (0, width - x.shape[-1])))


def state_call(start, groups, k, v, rim, ck, cv, before=()):
    rows, heads = v.shape[0], v.shape[1] // HD
    fw, vw = GROUP * FEAT, GROUP * HD

    def cols(n, wide, offset=0):
        return pl.BlockSpec((n, wide), lambda g, s: (0, offset + s[0] + g))

    return pl.pallas_call(
        state_kernel,
        grid_spec=pltpu.PrefetchScalarGridSpec(
            num_scalar_prefetch=1,
            grid=(groups,),
            in_specs=[
                cols(rows, fw),
                cols(rows, vw),
                cols(2, fw, heads + heads // GROUP),
                cols(2, vw),
                cols(3, fw),
                cols(3, vw),
            ]
            + [pl.BlockSpec(memory_space=pl.ANY)] * len(before),
            out_specs=[
                cols(rows, fw),
                cols(rows, vw),
                pl.BlockSpec((GROUP, STATE, HD), lambda g, s: (g, 0, 0)),
            ],
            scratch_shapes=[pltpu.VMEM((rows + 8, fw), f32), pltpu.VMEM((rows + 8, vw), f32)],
        ),
        out_shape=[
            jax.ShapeDtypeStruct((rows, heads * FEAT), bf16),
            jax.ShapeDtypeStruct((rows, heads * HD), bf16),
            jax.ShapeDtypeStruct((groups * GROUP, STATE, HD), bf16),
        ],
        input_output_aliases={7 + i: i for i in range(len(before))},
        compiler_params=params(),
        cost_estimate=cost(3 * groups),
    )(start, k, v, rim, rim, ck, cv, *before)


def local_call(q, rim, cq, kc, vc, start, groups, before=()):
    rows, heads = vc.shape[0], vc.shape[1] // HD
    fw, vw = GROUP * FEAT, GROUP * HD

    def cols(n, wide, offset=0):
        return pl.BlockSpec((n, wide), lambda g: (0, offset + g))

    return pl.pallas_call(
        local_kernel,
        grid=(groups,),
        in_specs=[
            cols(rows, fw, start),
            cols(2, fw, heads + start),
            cols(3, fw, start),
            cols(rows, fw, start),
            cols(rows, vw, start),
        ]
        + [pl.BlockSpec(memory_space=pl.ANY)] * len(before),
        out_specs=[cols(rows, fw, start), cols(rows, vw, start)],
        out_shape=[
            jax.ShapeDtypeStruct((rows, heads * FEAT), bf16),
            jax.ShapeDtypeStruct((rows, heads * HD), f32),
        ],
        scratch_shapes=[pltpu.VMEM((rows + 8, fw), f32)],
        input_output_aliases={5 + i: i for i in range(len(before))},
        compiler_params=params(),
        cost_estimate=cost(3 * groups),
    )(q, rim, cq, kc, vc, *before)


def hidden_call(start, qc, local, state, gain):
    rows, fw, vw = qc.shape[0], GROUP * FEAT, GROUP * HD
    groups = state.shape[0] // GROUP

    def cols(n, wide):
        return pl.BlockSpec((n, wide), lambda g, s: (0, s[0] + g))

    return pl.pallas_call(
        hidden_kernel,
        grid_spec=pltpu.PrefetchScalarGridSpec(
            num_scalar_prefetch=1,
            grid=(groups,),
            in_specs=[
                cols(rows, fw),
                cols(rows, vw),
                pl.BlockSpec((GROUP, STATE, HD), lambda g, s: (g, 0, 0)),
                cols(1, vw),
            ],
            out_specs=pl.BlockSpec((rows, vw), lambda g, s: (0, g)),
            scratch_shapes=[pltpu.VMEM((STATE * GROUP, vw), bf16)],
        ),
        out_shape=jax.ShapeDtypeStruct((rows, groups * vw), bf16),
        compiler_params=params(),
        cost_estimate=cost(4 * groups),
    )(start, qc, local, state, gain)


def by_gather(q, k, v, cq, ck, cv, gain, rim, weight, ids, width):
    weight = lax.all_gather(weight, "seq", axis=1, tiled=True)
    groups = v.shape[1] // (GROUP * HD)
    zero = jnp.zeros((1,), jnp.int32)
    kc, vc, kv = state_call(zero, groups, k, v, rim, ck, cv)
    qc, local = local_call(q, rim, cq, kc, vc, 0, groups)
    scan = Scan(ids, "seq")
    half = kv.shape[0] // 2
    mine = lax.dynamic_slice_in_dim(kv, scan.core * half, half, 0)
    theirs = lax.dynamic_slice_in_dim(kv, (1 - scan.core) * half, half, 0)
    scan.chip(mine, flip(theirs, "seq", 1))
    for bit in (2, 4):
        scan.merge(bit, scan.hop(bit))
    scan.cut()
    for step in range(scan.climbs()):
        scan.climb(step)
    for bit in (2, 4):
        scan.gather(bit, scan.gather_hop(bit))
    keep, got = scan.finish()
    low = jnp.where(scan.core == 0, keep, got)
    high = jnp.where(scan.core == 0, got, keep)
    state = jnp.concatenate([low, high], axis=0)
    hidden = hidden_call(zero, qc, local, state, gain)
    return jnp.dot(hidden[:, :width], weight, preferred_element_type=f32).astype(bf16)


def by_tree(q, k, v, cq, ck, cv, gain, rim, weight, ids):
    axis = "seq"
    n, me = lax.axis_size(axis), lax.axis_index(axis)
    core = jnp.reshape(me % 2, (1,)).astype(jnp.int32)
    half = v.shape[1] // (GROUP * HD) // 2
    ties = lax.optimization_barrier

    def over_x(piece):
        return flip(piece, axis, 2)

    def over_y(piece):
        return flip(piece, axis, 4)

    def over_z(piece):
        return turn(piece, axis)

    def share(piece):
        return flip(piece, axis, 1)

    own0, width = weight, n * weight.shape[1]
    scan = Scan(ids, axis)
    *kept, theirs = state_call((1 - core) * half, half, k, v, rim, ck, cv)
    got = share(theirs)
    x0, y0, own1 = over_x(own0), over_y(own0), over_z(own0)
    kc, vc, mine = state_call(core * half, half, k, v, rim, ck, cv, kept)
    got = tie(got, mine)
    scan.chip(mine, got)
    hop_x = scan.hop(2)
    before = local_call(tie(q, scan.total), rim, cq, kc, vc, 0, half)
    y0, own1 = ties((y0, own1, before[1]))[:2]

    own2, d0 = over_z(own1), over_x(y0)
    hop_x, x0 = ties((hop_x, x0, before[1]))[:2]
    scan.merge(2, hop_x)
    hop_y = scan.hop(4)
    qc, local = local_call(tie(q, scan.total), rim, cq, kc, vc, half, half, before)
    y1 = over_y(tie(own1, local))
    hop_y = tie(hop_y, local)
    scan.merge(4, hop_y)
    scan.cut()

    for step in range(scan.climbs()):
        hop_z = scan.climb(step)
    scan.below, own2 = ties((scan.below, own2))
    own3 = over_z(tie(own2, scan.below))
    hop_x = scan.gather_hop(2)
    hop_x, d0 = ties((hop_x, d0))
    x1 = over_x(tie(own1, hop_x))
    scan.gather(2, hop_x)
    hop_y = scan.gather_hop(4)
    hop_y, y1 = ties((hop_y, y1))
    y2 = over_y(tie(own2, hop_y))
    d1 = over_z(tie(d0, hop_y))
    scan.gather(4, hop_y)
    keep, got = scan.finish()
    keep, own3 = ties((keep, own3))
    x3 = over_x(own3)
    hid_a = hidden_call(core * half, qc, local, keep, gain)
    got, x1 = ties((got, x1, hid_a))[:2]
    y3 = over_y(tie(own3, got))
    far_a = share(hid_a)
    hid_b = hidden_call((1 - core) * half, qc, local, got, gain)
    far_a, d1, y2 = ties((far_a, d1, y2, hid_b))[:3]
    d2, x2 = over_z(d1), over_x(tie(own2, y2))
    far_b = share(hid_b)
    soon = [
        (own0, 0, 0), (own1, 1, 0), (own2, 2, 0), (own3, 3, 0), (y0, 0, 4), (y1, 1, 4),
        (y2, 2, 4), (x0, 0, 2), (x1, 1, 2), (d0, 0, 6), (d1, 1, 6),
    ]
    late = [(None, 3, 4), (None, 3, 2), (None, 2, 6), (None, 2, 2), (None, 3, 6)]
    order = ring(n // 8)
    home = jnp.asarray(order, jnp.int32)
    spot = jnp.asarray([order.index(p) for p in range(n // 8)], jnp.int32)[me // 8]
    shift = jnp.asarray([p[1] for p in soon + late], jnp.int32)
    bits = jnp.asarray([p[2] for p in soon + late], jnp.int32)
    places = (home[(spot - shift) % (n // 8)] * 8 + (me % 8 ^ bits)).astype(jnp.int32)
    pieces, early = [p[0] for p in soon], places[: len(soon)]
    (out,) = project((hid_a, hid_b), (), core, width, pieces, early)
    far_b, x3, y3, d2, out = ties((far_b, x3, y3, d2, out))
    mid = x3.shape[0] // 2
    d3y, d3z = over_y(x3[:mid]), over_z(d2[mid:])
    (back_a,) = project((), (far_a, far_b), core, width, pieces, early)
    d3y, d3z, x2, out = ties((d3y, d3z, x2, out, back_a))[:4]
    pieces = [y3, x3, d2, x2, jnp.concatenate([d3y, d3z], axis=0)]
    out, back_b = project(
        (hid_a, hid_b), (far_a, far_b), core, width, pieces, places[len(soon) :], (out,)
    )
    back_a, back_b = share(back_a), share(back_b)
    return place([back_a, back_b], places ^ 1, out)


def on_device(
    query_feat,
    key_feat,
    values,
    conv_query,
    conv_key,
    conv_value,
    norm_gain,
    out_weight,
    stream_ids,
):
    width = values.shape[1]
    heads = -(-width // (HD * GROUP)) * GROUP
    me = lax.axis_index("seq")
    start = jnp.logical_or(me == 0, stream_ids[me] != stream_ids[jnp.maximum(me - 1, 0)])
    keep = 1.0 - start.astype(f32)
    q, k = padded(query_feat, heads * FEAT), padded(key_feat, heads * FEAT)
    v = padded(values, heads * HD)
    cq, ck = padded(conv_query, heads * FEAT), padded(conv_key, heads * FEAT)
    cv = padded(conv_value, heads * HD)
    gain = padded(norm_gain[None], heads * HD)
    rim = after(jnp.concatenate([v[-2:], q[-2:], k[-2:]], axis=1), "seq", 1).astype(f32) * keep
    n, cut = lax.axis_size("seq"), lax.axis_size("head")
    if n == 32 and cut == 1 and out_weight.shape[1] == HD and heads % (2 * GROUP) == 0:
        return by_tree(q, k, v, cq, ck, cv, gain, rim, out_weight, stream_ids)
    terms = by_gather(q, k, v, cq, ck, cv, gain, rim, out_weight, stream_ids, width)
    return lax.psum_scatter(terms, "head", scatter_dimension=1, tiled=True)


def solution(mesh):
    placed = (
        P("seq", "head"),
        P("seq", "head"),
        P("seq", "head"),
        P(None, "head"),
        P(None, "head"),
        P(None, "head"),
        P("head"),
        P("head", "seq"),
        P(),
    )
    return jax.shard_map(
        on_device, mesh=mesh, in_specs=placed, out_specs=P("seq", "head"), check_vma=False
    )
```

time: 278 us -> 207 us (0.74)
  waiting for transfers between devices: 150 us -> 51.1 us
  Pallas kernels: 32.7 us -> 82.8 us
  matrix products: 23.6 us -> 0 us
  between operations: 23.9 us -> 12.2 us
  local copies, waits for them, and re-layouts: 5.24 us -> 12.1 us
  starting transfers between devices: 32.7 us -> 36.7 us
    all_gather x1 -> x0, waiting for transfers between devices: 61.2 us -> none  [on_device(): weight = lax.all_gather(out_weight, 'seq', axis=1, tiled=True)]
    pallas_call x3 -> x10, Pallas kernels: 32.7 us -> 82.8 us  [the longest x3 39.8 us: project(): pl.pallas_call(functools.partial(project_kernel, count, *sides), in_specs...]
    ppermute x3, waiting for transfers between devices: 50.5 us -> 3.48 us  [after(): lax.ppermute(x, axis, [(i, i + distance) for i in range(n - distance)])]
    dot_general x1 -> x0, matrix products: 23.6 us -> none  [on_device(): terms = jnp.dot(hidden[:, :width], weight, preferred_element_type=f32)]
    ppermute x4 -> x20, waiting for transfers between devices: 37.3 us -> 46.1 us  [flip(): lax.ppermute(x, axis, [(i, i ^ bit) for i in range(lax.axis_size(axis))])]
    ppermute x0 -> x6, starting transfers between devices: none -> 6.98 us  [turn(): return lax.ppermute(x, axis, route)]
    slice x0 -> x3, local copies, waits for them, and re-layouts: none -> 4.43 us  [the longest x2 3.79 us: by_tree(): d3y, d3z = (over_y(x3[:mid]), over_z(d2[mid:]))]
    ppermute x3, starting transfers between devices: 13.3 us -> 9.69 us  [after(): lax.ppermute(x, axis, [(i, i + distance) for i in range(n - distance)])]
  transfers between devices with their start and end apart: 8 -> 29, of which waited for: 6 -> 9; matrix products, arithmetic and copies ran while one was open for 5% -> 8% of each run, Pallas kernels for 12% -> 39%
where the time goes in v2:
time: 207 us; the launch traced here: 204 us
  Pallas kernels  82.8 us (40%)
  waiting for transfers between devices  51.1 us (25%)
  starting transfers between devices  36.7 us (18%)
  between operations  12.2 us (6%)
  local copies, waits for them, and re-layouts  12.1 us (6%)
  other arithmetic  9.19 us (4%)
    ppermute x20, waiting for transfers between devices, flip(): lax.ppermute(x, axis, [(i, i ^ bit) for i in range(lax.axis_size(axis))])  46.1 us
    pallas_call x3, Pallas kernels, project(): pl.pallas_call(functools.partial(project_kernel, count, *sides), in_specs...  39.8 us
    ppermute x20, starting transfers between devices, flip(): lax.ppermute(x, axis, [(i, i ^ bit) for i in range(lax.axis_size(axis))])  20 us
    pallas_call x2, Pallas kernels, hidden_call(): pl.pallas_call(hidden_kernel, grid_spec=pltpu.PrefetchScalarGridSpec(num_...  15.1 us
    pallas_call x2, Pallas kernels, local_call(): pl.pallas_call(local_kernel, grid=(groups,), in_specs=[cols(rows, fw, sta...  13.4 us
    pallas_call x2, Pallas kernels, state_call(): pl.pallas_call(state_kernel, grid_spec=pltpu.PrefetchScalarGridSpec(num_s...  11.5 us
    ppermute x3, starting transfers between devices, after(): lax.ppermute(x, axis, [(i, i + distance) for i in range(n - distance)])  9.69 us
    ppermute x6, starting transfers between devices, turn(): return lax.ppermute(x, axis, route)  6.98 us
  transfers between devices with their start and end apart: 29, of which 9 were waited for; matrix products, arithmetic and copies ran while one was open for 8% of the time, Pallas kernels for 39%

profile of v2, /device:TPU:11, one launch (start us, length us, event | category | flops | bytes accessed | tf_op | source)
XLA Modules:
  0.0 204.0 jit_solution(17390900214773853360)
XLA Ops:
  2.3 3.7 %collective-permute-start = (bf16[2,5120]{1,0:T(2,128)(2,1)S(1)}, bf16[2,5120]{1,0:T(2,128)(2,1)S(1)}, u32[]{:S(2)}, u32[]{:S(2)}) collective-permute-start(bf16[2,5120]{1,0:T(2,128)(2,1)S(1)} %pad_maximum_fusion.2), channel_id=1, source_target_pairs={{0,1},{1,2},{2,3},{3,4},{4,5},{5,6},{6,7},{7,8},{8,9},{9,10},{10,1... | collective-permute-start | bytes 61448 | tf_op jit(solution)/shard_map/ppermute | solution.py:245
  9.9 1.8 fusion.14
  17.4 5.7 %shard_map.127 = (bf16[512,512]{1,0:T(8,128)(2,1)}, bf16[512,4096]{1,0:T(8,128)(2,1)}, bf16[16,160,128]{2,1,0:T(8,128)(2,1)}) custom-call(s32[1]{0:T(128)S(6)} %mul.99.start_ref, bf16[512,512]{1,0:T(8,128)(2,1)} %k_ref.3, bf16[512,4096]{1,0:T(8,128)(2,1)} %v_ref.3, f32[2,5120]{1,0:T(2,128)} %convert_multiply_fusion.3.rk_ref.rv_ref.rq_ref, ...), custom_call_target="tpu_custom_call" | custom-call | flops 120000004096 | bytes 1048576 | tf_op jit(solution)/shard_map/pallas_call | solution.py:339
  23.1 5.8 %shard_map.128 = (bf16[512,512]{1,0:T(8,128)(2,1)}, bf16[512,4096]{1,0:T(8,128)(2,1)}, bf16[16,160,128]{2,1,0:T(8,128)(2,1)}) custom-call(s32[1]{0:T(128)S(6)} %mul.97.start_ref, bf16[512,512]{1,0:T(8,128)(2,1)} %k_ref.3, bf16[512,4096]{1,0:T(8,128)(2,1)} %v_ref.3, ...), custom_call_target="tpu_custom_call", output_to_operand_aliasing={{0}: (7, {}), {1}: (8, {})} | custom-call | flops 120000004096 | bytes 1048576 | tf_op jit(solution)/shard_map/pallas_call | solution.py:339
  28.9 1.6 fusion.1
  31.5 6.7 %shard_map.129 = (bf16[512,512]{1,0:T(8,128)(2,1)}, f32[512,4096]{1,0:T(8,128)}) custom-call(bf16[512,512]{1,0:T(8,128)(2,1)} %q_ref.1, f32[2,5120]{1,0:T(2,128)} %convert_multiply_fusion.3.rk_ref.rv_ref.rq_ref, f32[3,512]{1,0:T(4,128)} %cq_ref.3, bf16[512,512]{1,0:T(8,128)(2,1)} %get-tuple-element.60.kc_ref, bf16[512,4096]{1,0:T(8,128)(2,1)} %get-tuple-element.61.vc_ref), custom_call_target="tpu_custom_call" | custom-call | flops 120000004096 | bytes 1048576 | tf_op jit(solution)/shard_map/pallas_call | solution.py:378
  39.0 8.5 %collective-permute-done.2 = bf16[16,160,128]{2,1,0:T(8,128)(2,1)S(1)} collective-permute-done((bf16[16,160,128]{2,1,0:T(8,128)(2,1)S(1)}, bf16[16,160,128]{2,1,0:T(8,128)(2,1)S(1)}, u32[]{:S(2)}, u32[]{:S(2)}) %collective-permute-start.2) | collective-permute-done | bytes 655392 | tf_op jit(solution)/shard_map/ppermute | solution.py:240
  47.8 1.9 collective-permute-start.4
  49.7 6.7 %shard_map.130 = (bf16[512,512]{1,0:T(8,128)(2,1)}, f32[512,4096]{1,0:T(8,128)}) custom-call(bf16[512,512]{1,0:T(8,128)(2,1)} %q_ref.1, f32[2,5120]{1,0:T(2,128)} %convert_multiply_fusion.3.rk_ref.rv_ref.rq_ref, f32[3,512]{1,0:T(4,128)} %cq_ref.3, bf16[512,512]{1,0:T(8,128)(2,1)} %get-tuple-element.60.kc_ref, ...), custom_call_target="tpu_custom_call", output_to_operand_aliasing={{0}: (5, {}), {1}: (6, {})} | custom-call | flops 120000004096 | bytes 1048576 | tf_op jit(solution)/shard_map/pallas_call | solution.py:378
  56.4 7.3 %collective-permute-done.4 = bf16[16,160,128]{2,1,0:T(8,128)(2,1)S(1)} collective-permute-done((bf16[16,160,128]{2,1,0:T(8,128)(2,1)S(1)}, bf16[16,160,128]{2,1,0:T(8,128)(2,1)S(1)}, u32[]{:S(2)}, u32[]{:S(2)}) %collective-permute-start.4) | collective-permute-done | bytes 655392 | tf_op jit(solution)/shard_map/ppermute | solution.py:240
  63.9 2.9 %collective-permute-start.5 = (bf16[4,160,128]{2,1,0:T(8,128)(2,1)S(1)}, bf16[4,160,128]{2,1,0:T(8,128)(2,1)S(1)}, u32[]{:S(2)}, u32[]{:S(2)}) collective-permute-start(bf16[4,160,128]{2,1,0:T(8,128)(2,1)S(1)} %fusion.12), channel_id=1, source_target_pairs={{0,8},{1,9},{2,10},{3,11},{4,12},{5,13},{6,14},{7,15},{8,16},{9,17... | collective-permute-start | bytes 491528 | tf_op jit(solution)/shard_map/ppermute | solution.py:245
  66.8 3.5 %collective-permute-done.5 = bf16[4,160,128]{2,1,0:T(8,128)(2,1)S(1)} collective-permute-done((bf16[4,160,128]{2,1,0:T(8,128)(2,1)S(1)}, bf16[4,160,128]{2,1,0:T(8,128)(2,1)S(1)}, u32[]{:S(2)}, u32[]{:S(2)}) %collective-permute-start.5) | collective-permute-done | bytes 163872 | tf_op jit(solution)/shard_map/ppermute | solution.py:245
  70.3 3.1 %collective-permute-start.6 = (bf16[4,160,128]{2,1,0:T(8,128)(2,1)S(1)}, bf16[4,160,128]{2,1,0:T(8,128)(2,1)S(1)}, u32[]{:S(2)}, u32[]{:S(2)}) collective-permute-start(bf16[4,160,128]{2,1,0:T(8,128)(2,1)S(1)} %collective-permute-done.5), channel_id=1, source_target_pairs={{0,8},{1,9},{2,10},{3,11},{4,12},{5,13},{6,14},{7,15},{8,16},{9,17... | collective-permute-start | bytes 491528 | tf_op jit(solution)/shard_map/ppermute | solution.py:245
  80.7 1.5 collective-permute-start.13
  84.1 2.8 %collective-permute-done.10 = bf16[4,160,128]{2,1,0:T(8,128)(2,1)S(1)} collective-permute-done((bf16[4,160,128]{2,1,0:T(8,128)(2,1)S(1)}, bf16[4,160,128]{2,1,0:T(8,128)(2,1)S(1)}, u32[]{:S(2)}, u32[]{:S(2)}) %collective-permute-start.10) | collective-permute-done | bytes 163872 | tf_op jit(solution)/shard_map/ppermute | solution.py:240
  90.5 13.1 %collective-permute-done.13.refs_7_ = bf16[4096,128]{1,0:T(8,128)(2,1)} collective-permute-done((bf16[4096,128]{1,0:T(8,128)(2,1)}, bf16[4096,128]{1,0:T(8,128)(2,1)}, u32[]{:S(2)}, u32[]{:S(2)}) %collective-permute-start.13) | collective-permute-done | bytes 1048608 | tf_op jit(solution)/shard_map/ppermute | solution.py:240
  103.6 7.0 %collective-permute-done.12 = bf16[8,160,128]{2,1,0:T(8,128)(2,1)} collective-permute-done((bf16[8,160,128]{2,1,0:T(8,128)(2,1)S(1)}, bf16[8,160,128]{2,1,0:T(8,128)(2,1)}, u32[]{:S(2)}, u32[]{:S(2)}) %collective-permute-start.12) | collective-permute-done | bytes 327712 | tf_op jit(solution)/shard_map/ppermute | solution.py:240
  113.4 1.8 fusion.6
  115.2 3.0 %collective-permute-start.18 = (bf16[16,160,128]{2,1,0:T(8,128)(2,1)}, bf16[16,160,128]{2,1,0:T(8,128)(2,1)}, u32[]{:S(2)}, u32[]{:S(2)}) collective-permute-start(bf16[16,160,128]{2,1,0:T(8,128)(2,1)} %get-tuple-element.105), channel_id=1, source_target_pairs={{0,1},{1,0},{2,3},{3,2},{4,5},{5,4},{6,7},{7,6},{8,9},{9,8},{10,11... | collective-permute-start | bytes 1966088 | tf_op jit(solution)/shard_map/ppermute | solution.py:240
  118.3 7.6 %shard_map.131.refs_0_ = bf16[512,2048]{1,0:T(8,128)(2,1)} custom-call(s32[1]{0:T(128)S(6)} %mul.97.start_ref, bf16[512,512]{1,0:T(8,128)(2,1)} %get-tuple-element.66.qc_ref, f32[512,4096]{1,0:T(8,128)} %get-tuple-element.67.loc_ref, bf16[16,160,128]{2,1,0:T(8,128)(2,1)} %get-tuple-element.77.s_ref, f32[1,4096]{1,0:T(1,128)} %bitcast.15), custom_call_target="tpu_custom_call" | custom-call | flops 160000000000 | bytes 1048576 | tf_op jit(solution)/shard_map/pallas_call | solution.py:408
  126.0 7.6 %shard_map.132.refs_1_ = bf16[512,2048]{1,0:T(8,128)(2,1)} custom-call(s32[1]{0:T(128)S(6)} %mul.99.start_ref, bf16[512,512]{1,0:T(8,128)(2,1)} %get-tuple-element.66.qc_ref, f32[512,4096]{1,0:T(8,128)} %get-tuple-element.67.loc_ref, bf16[16,160,128]{2,1,0:T(8,128)(2,1)} %collective-permute-done.18.s_ref, f32[1,4096]{1,0:T(1,128)} %bitcast.16), custom_call_target="tpu_custom_call" | custom-call | flops 160000000000 | bytes 1048576 | tf_op jit(solution)/shard_map/pallas_call | solution.py:408
  138.5 13.4 %shard_map.133.refs_9_ = bf16[512,4096]{1,0:T(8,128)(2,1)} custom-call(s32[1]{0:T(128)} %bitcast.1.first_ref, s32[11]{0:T(128)} %bitcast.13, bf16[512,2048]{1,0:T(8,128)(2,1)} %shard_map.131.refs_0_, bf16[512,2048]{1,0:T(8,128)(2,1)} %shard_map.132.refs_1_, bf16[4096,128]{1,0:T(8,128)(2,1)} %refs_2_.3, bf16[4096,128]{1,0:T(8,128)(2,1)} %collective-permute-done.8.refs_3_, ...), custom_call_target="tpu_custom_call" | custom-call | flops 219999993856 | bytes 1048576 | tf_op jit(solution)/shard_map/pallas_call | solution.py:177
  151.9 5.0 %collective-permute-done.22.refs_4_ = bf16[4096,128]{1,0:T(8,128)(2,1)} collective-permute-done((bf16[4096,128]{1,0:T(8,128)(2,1)}, bf16[4096,128]{1,0:T(8,128)(2,1)}, u32[]{:S(2)}, u32[]{:S(2)}) %collective-permute-start.22) | collective-permute-done | bytes 1048608 | tf_op jit(solution)/shard_map/ppermute | solution.py:240
  158.4 1.9 slice.26
  160.2 1.9 slice.27
  162.2 3.1 %collective-permute-start.26 = (bf16[2048,128]{1,0:T(8,128)(2,1)}, bf16[2048,128]{1,0:T(8,128)(2,1)}, u32[]{:S(2)}, u32[]{:S(2)}) collective-permute-start(bf16[2048,128]{1,0:T(8,128)(2,1)} %slice.27), channel_id=1, source_target_pairs={{0,8},{1,9},{2,10},{3,11},{4,12},{5,13},{6,14},{7,15},{8,24},{9,25... | collective-permute-start | bytes 1572872 | tf_op jit(solution)/shard_map/ppermute | solution.py:236
  165.3 13.7 %shard_map.134 = bf16[11,512,128]{2,1,0:T(8,128)(2,1)} custom-call(s32[1]{0:T(128)} %bitcast.1.first_ref, s32[11]{0:T(128)} %bitcast.14, bf16[512,2048]{1,0:T(8,128)(2,1)} %collective-permute-done.15.refs_0_.refs_2_, bf16[512,2048]{1,0:T(8,128)(2,1)} %collective-permute-done.20.refs_1_.refs_3_, bf16[4096,128]{1,0:T(8,128)(2,1)} %refs_2_.3, ...), custom_call_target="tpu_custom_call" | custom-call | flops 219999993856 | bytes 1048576 | tf_op jit(solution)/shard_map/pallas_call | solution.py:177
  179.0 3.2 %collective-permute-start.24 = (bf16[11,512,128]{2,1,0:T(8,128)(2,1)}, bf16[11,512,128]{2,1,0:T(8,128)(2,1)S(1)}, u32[]{:S(2)}, u32[]{:S(2)}) collective-permute-start(bf16[11,512,128]{2,1,0:T(8,128)(2,1)} %shard_map.134), channel_id=1, source_target_pairs={{0,1},{1,0},{2,3},{3,2},{4,5},{5,4},{6,7},{7,6},{8,9},{9,8},{10,11... | collective-permute-start | bytes 4325384 | tf_op jit(solution)/shard_map/ppermute | solution.py:240
  182.1 2.3 %pad_maximum_fusion.refs_8_ = bf16[4096,128]{1,0:T(8,128)(2,1)} fusion(bf16[2048,128]{1,0:T(8,128)(2,1)} %collective-permute-done.26, bf16[2048,128]{1,0:T(8,128)(2,1)} %collective-permute-done.25), kind=kLoop, calls=%fused_computation.16 | loop fusion | flops 2097152 | bytes 2097152 | tf_op jit(solution)/shard_map/concatenate | solution.py:537
  184.4 12.7 %shard_map.135 = (bf16[512,4096]{1,0:T(8,128)(2,1)}, bf16[5,512,128]{2,1,0:T(8,128)(2,1)}) custom-call(s32[1]{0:T(128)} %bitcast.1.first_ref, s32[5]{0:T(128)} %slice.25.place_ref, bf16[512,2048]{1,0:T(8,128)(2,1)} %shard_map.131.refs_0_, bf16[512,2048]{1,0:T(8,128)(2,1)} %shard_map.132.refs_1_, ...), custom_call_target="tpu_custom_call", output_to_operand_aliasing={{0}: (11, {})} | custom-call | flops 99999997952 | bytes 1048576 | tf_op jit(solution)/shard_map/pallas_call | solution.py:177
  197.3 2.3 %collective-permute-done.28.refs_1_ = bf16[5,512,128]{2,1,0:T(8,128)(2,1)S(1)} collective-permute-done((bf16[5,512,128]{2,1,0:T(8,128)(2,1)}, bf16[5,512,128]{2,1,0:T(8,128)(2,1)S(1)}, u32[]{:S(2)}, u32[]{:S(2)}) %collective-permute-start.28) | collective-permute-done | bytes 655392 | tf_op jit(solution)/shard_map/ppermute | solution.py:240
  200.9 3.0 %shard_map.136 = bf16[512,4096]{1,0:T(8,128)(2,1)} custom-call(s32[16]{0:T(128)} %get-tuple-element.103.place_ref, bf16[11,512,128]{2,1,0:T(8,128)(2,1)} %copy-done.6, bf16[5,512,128]{2,1,0:T(8,128)(2,1)} %copy-done.8, bf16[512,4096]{1,0:T(8,128)(2,1)} %get-tuple-element.102.refs_2_), custom_call_target="tpu_custom_call", output_to_operand_aliasing={{}: (3, {})} | custom-call | flops 60000002048 | bytes 1048576 | tf_op jit(solution)/shard_map/pallas_call | solution.py:213
  (80 shorter events, 25.7 us)
Async XLA Ops:
  2.3 14.4 %collective-permute-start = (bf16[2,5120]{1,0:T(2,128)(2,1)S(1)}, bf16[2,5120]{1,0:T(2,128)(2,1)S(1)}, u32[]{:S(2)}, u32[]{:S(2)}) collective-permute-start(bf16[2,5120]{1,0:T(2,128)(2,1)S(1)} %pad_maximum_fusion.2), channel_id=1, source_target_pairs={{0,1},{1,2},{2,3},{3,4},{4,5},{5,6},{6,7},{7,8},{8,9},{9,10},{10,1... | collective-permute-start | bytes 61448 | tf_op jit(solution)/shard_map/ppermute | solution.py:245
  6.0 32.2 %collective-permute-start.7 = (bf16[4096,128]{1,0:T(8,128)(2,1)}, bf16[4096,128]{1,0:T(8,128)(2,1)}, u32[]{:S(2)}, u32[]{:S(2)}) collective-permute-start(bf16[4096,128]{1,0:T(8,128)(2,1)} %refs_2_.3), channel_id=1, source_target_pairs={{0,4},{1,5},{2,6},{3,7},{4,0},{5,1},{6,2},{7,3},{8,12},{9,13},{10,... | collective-permute-start | bytes 3145736 | tf_op jit(solution)/shard_map/ppermute | solution.py:240
  7.3 30.9 %collective-permute-start.8 = (bf16[4096,128]{1,0:T(8,128)(2,1)}, bf16[4096,128]{1,0:T(8,128)(2,1)}, u32[]{:S(2)}, u32[]{:S(2)}) collective-permute-start(bf16[4096,128]{1,0:T(8,128)(2,1)} %refs_2_.3), channel_id=1, source_target_pairs={{0,8},{1,9},{2,10},{3,11},{4,12},{5,13},{6,14},{7,15},{8,24},{9,25... | collective-permute-start | bytes 3145736 | tf_op jit(solution)/shard_map/ppermute | solution.py:236
  8.4 30.6 %collective-permute-start.3 = (bf16[4096,128]{1,0:T(8,128)(2,1)}, bf16[4096,128]{1,0:T(8,128)(2,1)}, u32[]{:S(2)}, u32[]{:S(2)}) collective-permute-start(bf16[4096,128]{1,0:T(8,128)(2,1)} %refs_2_.3), channel_id=1, source_target_pairs={{0,2},{1,3},{2,0},{3,1},{4,6},{5,7},{6,4},{7,5},{8,10},{9,11},{10,... | collective-permute-start | bytes 3145736 | tf_op jit(solution)/shard_map/ppermute | solution.py:240
  23.1 5.8 %collective-permute-start.1 = (bf16[16,160,128]{2,1,0:T(8,128)(2,1)}, bf16[16,160,128]{2,1,0:T(8,128)(2,1)S(1)}, u32[]{:S(2)}, u32[]{:S(2)}) collective-permute-start(bf16[16,160,128]{2,1,0:T(8,128)(2,1)} %get-tuple-element.54), channel_id=1, source_target_pairs={{0,1},{1,0},{2,3},{3,2},{4,5},{5,4},{6,7},{7,6},{8,9},{9,8},{10,11... | collective-permute-start | bytes 1966088 | tf_op jit(solution)/shard_map/ppermute | solution.py:240
  30.5 17.0 %collective-permute-start.2 = (bf16[16,160,128]{2,1,0:T(8,128)(2,1)S(1)}, bf16[16,160,128]{2,1,0:T(8,128)(2,1)S(1)}, u32[]{:S(2)}, u32[]{:S(2)}) collective-permute-start(bf16[16,160,128]{2,1,0:T(8,128)(2,1)S(1)} %fusion.1), channel_id=1, source_target_pairs={{0,2},{1,3},{2,0},{3,1},{4,6},{5,7},{6,4},{7,5},{8,10},{9,11},{10,... | collective-permute-start | bytes 1966088 | tf_op jit(solution)/shard_map/ppermute | solution.py:240
  38.2 44.0 %collective-permute-start.9 = (bf16[4096,128]{1,0:T(8,128)(2,1)}, bf16[4096,128]{1,0:T(8,128)(2,1)}, u32[]{:S(2)}, u32[]{:S(2)}) collective-permute-start(bf16[4096,128]{1,0:T(8,128)(2,1)} %collective-permute-done.8.refs_3_), channel_id=1, source_target_pairs={{0,8},{1,9},{2,10},{3,11},{4,12},{5,13},{6,14},{7,15},{8,24},{9,25... | collective-permute-start | bytes 3145736 | tf_op jit(solution)/shard_map/ppermute | solution.py:236
  38.7 44.4 %collective-permute-start.11 = (bf16[4096,128]{1,0:T(8,128)(2,1)}, bf16[4096,128]{1,0:T(8,128)(2,1)S(1)}, u32[]{:S(2)}, u32[]{:S(2)}) collective-permute-start(bf16[4096,128]{1,0:T(8,128)(2,1)} %collective-permute-done.7.refs_6_), channel_id=1, source_target_pairs={{0,2},{1,3},{2,0},{3,1},{4,6},{5,7},{6,4},{7,5},{8,10},{9,11},{10,... | collective-permute-start | bytes 3145736 | tf_op jit(solution)/shard_map/ppermute | solution.py:240
  47.8 15.9 %collective-permute-start.4 = (bf16[16,160,128]{2,1,0:T(8,128)(2,1)S(1)}, bf16[16,160,128]{2,1,0:T(8,128)(2,1)S(1)}, u32[]{:S(2)}, u32[]{:S(2)}) collective-permute-start(bf16[16,160,128]{2,1,0:T(8,128)(2,1)S(1)} %fusion.8), channel_id=1, source_target_pairs={{0,4},{1,5},{2,6},{3,7},{4,0},{5,1},{6,2},{7,3},{8,12},{9,13},{10,... | collective-permute-start | bytes 1966088 | tf_op jit(solution)/shard_map/ppermute | solution.py:240
  63.9 6.4 %collective-permute-start.5 = (bf16[4,160,128]{2,1,0:T(8,128)(2,1)S(1)}, bf16[4,160,128]{2,1,0:T(8,128)(2,1)S(1)}, u32[]{:S(2)}, u32[]{:S(2)}) collective-permute-start(bf16[4,160,128]{2,1,0:T(8,128)(2,1)S(1)} %fusion.12), channel_id=1, source_target_pairs={{0,8},{1,9},{2,10},{3,11},{4,12},{5,13},{6,14},{7,15},{8,16},{9,17... | collective-permute-start | bytes 491528 | tf_op jit(solution)/shard_map/ppermute | solution.py:245
  70.3 11.9 %collective-permute-start.6 = (bf16[4,160,128]{2,1,0:T(8,128)(2,1)S(1)}, bf16[4,160,128]{2,1,0:T(8,128)(2,1)S(1)}, u32[]{:S(2)}, u32[]{:S(2)}) collective-permute-start(bf16[4,160,128]{2,1,0:T(8,128)(2,1)S(1)} %collective-permute-done.5), channel_id=1, source_target_pairs={{0,8},{1,9},{2,10},{3,11},{4,12},{5,13},{6,14},{7,15},{8,16},{9,17... | collective-permute-start | bytes 491528 | tf_op jit(solution)/shard_map/ppermute | solution.py:245
  80.7 22.9 %collective-permute-start.13 = (bf16[4096,128]{1,0:T(8,128)(2,1)}, bf16[4096,128]{1,0:T(8,128)(2,1)}, u32[]{:S(2)}, u32[]{:S(2)}) collective-permute-start(bf16[4096,128]{1,0:T(8,128)(2,1)} %collective-permute-done.8.refs_3_), channel_id=1, source_target_pairs={{0,4},{1,5},{2,6},{3,7},{4,0},{5,1},{6,2},{7,3},{8,12},{9,13},{10,... | collective-permute-start | bytes 3145736 | tf_op jit(solution)/shard_map/ppermute | solution.py:240
  82.3 4.6 %collective-permute-start.10 = (bf16[4,160,128]{2,1,0:T(8,128)(2,1)S(1)}, bf16[4,160,128]{2,1,0:T(8,128)(2,1)S(1)}, u32[]{:S(2)}, u32[]{:S(2)}) collective-permute-start(bf16[4,160,128]{2,1,0:T(8,128)(2,1)S(1)} %multiply_add_fusion), channel_id=1, source_target_pairs={{0,2},{1,3},{2,0},{3,1},{4,6},{5,7},{6,4},{7,5},{8,10},{9,11},{10,... | collective-permute-start | bytes 491528 | tf_op jit(solution)/shard_map/ppermute | solution.py:240
  83.1 35.2 %collective-permute-start.14 = (bf16[4096,128]{1,0:T(8,128)(2,1)}, bf16[4096,128]{1,0:T(8,128)(2,1)}, u32[]{:S(2)}, u32[]{:S(2)}) collective-permute-start(bf16[4096,128]{1,0:T(8,128)(2,1)} %collective-permute-done.9.refs_4_), channel_id=1, source_target_pairs={{0,8},{1,9},{2,10},{3,11},{4,12},{5,13},{6,14},{7,15},{8,24},{9,25... | collective-permute-start | bytes 3145736 | tf_op jit(solution)/shard_map/ppermute | solution.py:236
  87.0 26.4 %copy-start.2 = (bf16[16,160,128]{2,1,0:T(8,128)(2,1)S(1)}, bf16[16,160,128]{2,1,0:T(8,128)(2,1)}, u32[]{:S(2)}) copy-start(bf16[16,160,128]{2,1,0:T(8,128)(2,1)} %copy-done.1) | copy-start | bytes 1966084
  87.0 26.4 %copy-start.3 = (bf16[16,160,128]{2,1,0:T(8,128)(2,1)S(1)}, bf16[16,160,128]{2,1,0:T(8,128)(2,1)}, u32[]{:S(2)}) copy-start(bf16[16,160,128]{2,1,0:T(8,128)(2,1)} %get-tuple-element.57) | copy-start | bytes 1966084
  87.0 23.6 %collective-permute-start.12 = (bf16[8,160,128]{2,1,0:T(8,128)(2,1)S(1)}, bf16[8,160,128]{2,1,0:T(8,128)(2,1)}, u32[]{:S(2)}, u32[]{:S(2)}) collective-permute-start(bf16[8,160,128]{2,1,0:T(8,128)(2,1)S(1)} %pad_maximum_fusion.1), channel_id=1, source_target_pairs={{0,4},{1,5},{2,6},{3,7},{4,0},{5,1},{6,2},{7,3},{8,12},{9,13},{10,... | collective-permute-start | bytes 983048 | tf_op jit(solution)/shard_map/ppermute | solution.py:240
  88.4 26.9 %copy-start.5 = (s32[16]{0:T(128)}, s32[16]{0:T(128)S(1)}, u32[]{:S(2)}) copy-start(s32[16]{0:T(128)S(1)} %get-tuple-element.104) | copy-start | bytes 196
  89.0 36.9 %collective-permute-start.19 = (bf16[4096,128]{1,0:T(8,128)(2,1)}, bf16[4096,128]{1,0:T(8,128)(2,1)}, u32[]{:S(2)}, u32[]{:S(2)}) collective-permute-start(bf16[4096,128]{1,0:T(8,128)(2,1)} %collective-permute-done.8.refs_3_), channel_id=1, source_target_pairs={{0,2},{1,3},{2,0},{3,1},{4,6},{5,7},{6,4},{7,5},{8,10},{9,11},{10,... | collective-permute-start | bytes 3145736 | tf_op jit(solution)/shard_map/ppermute | solution.py:240
  110.6 23.6 %collective-permute-start.16 = (bf16[4096,128]{1,0:T(8,128)(2,1)}, bf16[4096,128]{1,0:T(8,128)(2,1)}, u32[]{:S(2)}, u32[]{:S(2)}) collective-permute-start(bf16[4096,128]{1,0:T(8,128)(2,1)} %copy-done.7), channel_id=1, source_target_pairs={{0,8},{1,9},{2,10},{3,11},{4,12},{5,13},{6,14},{7,15},{8,24},{9,25... | collective-permute-start | bytes 3145736 | tf_op jit(solution)/shard_map/ppermute | solution.py:236
  111.3 24.4 %collective-permute-start.17 = (bf16[4096,128]{1,0:T(8,128)(2,1)}, bf16[4096,128]{1,0:T(8,128)(2,1)}, u32[]{:S(2)}, u32[]{:S(2)}) collective-permute-start(bf16[4096,128]{1,0:T(8,128)(2,1)} %collective-permute-done.9.refs_4_), channel_id=1, source_target_pairs={{0,4},{1,5},{2,6},{3,7},{4,0},{5,1},{6,2},{7,3},{8,12},{9,13},{10,... | collective-permute-start | bytes 3145736 | tf_op jit(solution)/shard_map/ppermute | solution.py:240
  115.2 10.7 %collective-permute-start.18 = (bf16[16,160,128]{2,1,0:T(8,128)(2,1)}, bf16[16,160,128]{2,1,0:T(8,128)(2,1)}, u32[]{:S(2)}, u32[]{:S(2)}) collective-permute-start(bf16[16,160,128]{2,1,0:T(8,128)(2,1)} %get-tuple-element.105), channel_id=1, source_target_pairs={{0,1},{1,0},{2,3},{3,2},{4,5},{5,4},{6,7},{7,6},{8,9},{9,8},{10,11... | collective-permute-start | bytes 1966088 | tf_op jit(solution)/shard_map/ppermute | solution.py:240
  125.8 9.9 %collective-permute-start.15 = (bf16[512,2048]{1,0:T(8,128)(2,1)}, bf16[512,2048]{1,0:T(8,128)(2,1)}, u32[]{:S(2)}, u32[]{:S(2)}) collective-permute-start(bf16[512,2048]{1,0:T(8,128)(2,1)} %shard_map.131.refs_0_), channel_id=1, source_target_pairs={{0,1},{1,0},{2,3},{3,2},{4,5},{5,4},{6,7},{7,6},{8,9},{9,8},{10,11... | collective-permute-start | bytes 6291464 | tf_op jit(solution)/shard_map/ppermute | solution.py:240
  125.9 26.0 %collective-permute-start.21 = (bf16[4096,128]{1,0:T(8,128)(2,1)}, bf16[4096,128]{1,0:T(8,128)(2,1)}, u32[]{:S(2)}, u32[]{:S(2)}) collective-permute-start(bf16[4096,128]{1,0:T(8,128)(2,1)} %collective-permute-done.14.refs_5_), channel_id=1, source_target_pairs={{0,2},{1,3},{2,0},{3,1},{4,6},{5,7},{6,4},{7,5},{8,10},{9,11},{10,... | collective-permute-start | bytes 3145736 | tf_op jit(solution)/shard_map/ppermute | solution.py:240
  133.5 23.4 %collective-permute-start.20 = (bf16[512,2048]{1,0:T(8,128)(2,1)}, bf16[512,2048]{1,0:T(8,128)(2,1)}, u32[]{:S(2)}, u32[]{:S(2)}) collective-permute-start(bf16[512,2048]{1,0:T(8,128)(2,1)} %shard_map.132.refs_1_), channel_id=1, source_target_pairs={{0,1},{1,0},{2,3},{3,2},{4,5},{5,4},{6,7},{7,6},{8,9},{9,8},{10,11... | collective-permute-start | bytes 6291464 | tf_op jit(solution)/shard_map/ppermute | solution.py:240
  134.2 22.7 %collective-permute-start.22 = (bf16[4096,128]{1,0:T(8,128)(2,1)}, bf16[4096,128]{1,0:T(8,128)(2,1)}, u32[]{:S(2)}, u32[]{:S(2)}) collective-permute-start(bf16[4096,128]{1,0:T(8,128)(2,1)} %collective-permute-done.14.refs_5_), channel_id=1, source_target_pairs={{0,4},{1,5},{2,6},{3,7},{4,0},{5,1},{6,2},{7,3},{8,12},{9,13},{10,... | collective-permute-start | bytes 3145736 | tf_op jit(solution)/shard_map/ppermute | solution.py:240
  135.7 22.7 %collective-permute-start.23 = (bf16[4096,128]{1,0:T(8,128)(2,1)}, bf16[4096,128]{1,0:T(8,128)(2,1)}, u32[]{:S(2)}, u32[]{:S(2)}) collective-permute-start(bf16[4096,128]{1,0:T(8,128)(2,1)} %collective-permute-done.16.refs_12_), channel_id=1, source_target_pairs={{0,8},{1,9},{2,10},{3,11},{4,12},{5,13},{6,14},{7,15},{8,24},{9,25... | collective-permute-start | bytes 3145736 | tf_op jit(solution)/shard_map/ppermute | solution.py:236
  137.2 44.9 %collective-permute-start.27 = (bf16[4096,128]{1,0:T(8,128)(2,1)}, bf16[4096,128]{1,0:T(8,128)(2,1)}, u32[]{:S(2)}, u32[]{:S(2)}) collective-permute-start(bf16[4096,128]{1,0:T(8,128)(2,1)} %collective-permute-done.9.refs_4_), channel_id=1, source_target_pairs={{0,2},{1,3},{2,0},{3,1},{4,6},{5,7},{6,4},{7,5},{8,10},{9,11},{10,... | collective-permute-start | bytes 3145736 | tf_op jit(solution)/shard_map/ppermute | solution.py:240
  160.2 21.9 %collective-permute-start.25 = (bf16[2048,128]{1,0:T(8,128)(2,1)}, bf16[2048,128]{1,0:T(8,128)(2,1)}, u32[]{:S(2)}, u32[]{:S(2)}) collective-permute-start(bf16[2048,128]{1,0:T(8,128)(2,1)} %slice.26), channel_id=1, source_target_pairs={{0,4},{1,5},{2,6},{3,7},{4,0},{5,1},{6,2},{7,3},{8,12},{9,13},{10,... | collective-permute-start | bytes 1572872 | tf_op jit(solution)/shard_map/ppermute | solution.py:240
  162.2 20.0 %collective-permute-start.26 = (bf16[2048,128]{1,0:T(8,128)(2,1)}, bf16[2048,128]{1,0:T(8,128)(2,1)}, u32[]{:S(2)}, u32[]{:S(2)}) collective-permute-start(bf16[2048,128]{1,0:T(8,128)(2,1)} %slice.27), channel_id=1, source_target_pairs={{0,8},{1,9},{2,10},{3,11},{4,12},{5,13},{6,14},{7,15},{8,24},{9,25... | collective-permute-start | bytes 1572872 | tf_op jit(solution)/shard_map/ppermute | solution.py:236
  179.0 20.6 %collective-permute-start.24 = (bf16[11,512,128]{2,1,0:T(8,128)(2,1)}, bf16[11,512,128]{2,1,0:T(8,128)(2,1)S(1)}, u32[]{:S(2)}, u32[]{:S(2)}) collective-permute-start(bf16[11,512,128]{2,1,0:T(8,128)(2,1)} %shard_map.134), channel_id=1, source_target_pairs={{0,1},{1,0},{2,3},{3,2},{4,5},{5,4},{6,7},{7,6},{8,9},{9,8},{10,11... | collective-permute-start | bytes 4325384 | tf_op jit(solution)/shard_map/ppermute | solution.py:240
  197.2 2.4 %collective-permute-start.28 = (bf16[5,512,128]{2,1,0:T(8,128)(2,1)}, bf16[5,512,128]{2,1,0:T(8,128)(2,1)S(1)}, u32[]{:S(2)}, u32[]{:S(2)}) collective-permute-start(bf16[5,512,128]{2,1,0:T(8,128)(2,1)} %get-tuple-element.101), channel_id=1, source_target_pairs={{0,1},{1,0},{2,3},{3,2},{4,5},{5,4},{6,7},{7,6},{8,9},{9,8},{10,11... | collective-permute-start | bytes 1966088 | tf_op jit(solution)/shard_map/ppermute | solution.py:240
  (7 other events, 71.4 us)

commit v3 on v2

--- a/solution.py
+++ b/solution.py
@@ -112,7 +112,7 @@
             out_ref[:, cols] = (y * scale * gain_ref[:, cols]).astype(bf16)
 
 
-def project_kernel(pieces, own, far, first_ref, place_ref, *refs):
+def project_kernel(pieces, own, far, skip, first_ref, place_ref, *refs):
     sides = own + far
     hidden, weights = refs[: 2 * sides], refs[2 * sides : 2 * sides + pieces]
     rows_in, held, done, hid_sems, sems, out_sems = refs[-6:]
@@ -131,40 +131,58 @@
         pltpu.make_async_copy(weights[i], held.at[:, HD * i : HD * (i + 1)], sems.at[i])
         for i in range(pieces)
     ]
-    groups = [range(c, min(c + 4, pieces)) for c in range(0, pieces, 4)]
-    for copy in loads[:2] + copies[:4] + loads[2:] + copies[4:8]:
+    near = 2 * own
+    if skip:
+        loads = loads[near:] + loads[:near]
+        near = 2 * far
+    bounds = [0, min(2, pieces)] + list(range(6, pieces, 4)) + [pieces] * (pieces > 2)
+    groups = [range(c, e) for c, e in zip(bounds, bounds[1:])]
+    ahead = [copies[g[0] : g[-1] + 1] for g in groups] + [[], []]
+    for copy in loads[:near] + ahead[0]:
         copy.start()
-    for copy in loads[:2]:
-        copy.wait()
     stores = []
     for at, group in enumerate(groups):
-        for copy in copies[4 * at : 4 * (at + 1)]:
+        if at == 0:
+            for copy in loads[:near]:
+                copy.wait()
+        for copy in ahead[at]:
             copy.wait()
-        for copy in copies[4 * (at + 2) : 4 * (at + 3)]:
+        for copy in (loads[near:] if at == 0 else []) + ahead[at + 1]:
             copy.start()
         cols = slice(HD * group[0], HD * (group[-1] + 1))
-        if own:
-            mine = jnp.dot(rows_in[0], held[:, cols], preferred_element_type=f32).astype(bf16)
+
+        def mine():
+            total = jnp.dot(rows_in[0], held[:, cols], preferred_element_type=f32).astype(bf16)
             for j, i in enumerate(group):
-                done[i] = mine[:, HD * j : HD * (j + 1)]
+                done[i] = total[:, HD * j : HD * (j + 1)]
                 where = pl.multiple_of(place_ref[i] * HD, HD)
                 store = pltpu.make_async_copy(
                     done.at[i], outs[0].at[:, pl.ds(where, HD)], out_sems.at[i]
                 )
                 store.start()
                 stores.append(store)
+
+        def theirs():
+            total = jnp.dot(rows_in[sides - 1], held[:, cols], preferred_element_type=f32)
+            for j, i in enumerate(group):
+                outs[-1][i] = total[:, HD * j : HD * (j + 1)].astype(bf16)
+
+        if skip:
+            theirs()
+        elif own:
+            mine()
         if at == 0:
-            for copy in loads[2:]:
+            for copy in loads[near:]:
                 copy.wait()
-        if far:
-            theirs = jnp.dot(rows_in[sides - 1], held[:, cols], preferred_element_type=f32)
-            for j, i in enumerate(group):
-                outs[-1][i] = theirs[:, HD * j : HD * (j + 1)].astype(bf16)
+        if skip and group[0] >= skip:
+            mine()
+        elif far and not skip:
+            theirs()
     for store in stores:
         store.wait()
 
 
-def project(own, far, first, width, pieces, places, before=()):
+def project(own, far, first, width, pieces, places, before=(), skip=0, micros=5):
     rows, half = (own + far)[0].shape
     count, depth = len(pieces), pieces[0].shape[0]
     smem, vmem, anywhere = (pl.BlockSpec(memory_space=m) for m in (pltpu.SMEM, pltpu.VMEM, pl.ANY))
@@ -175,7 +193,7 @@
     ]
     outs = [o for o, wanted in zip(outs, sides) if wanted]
     return pl.pallas_call(
-        functools.partial(project_kernel, count, *sides),
+        functools.partial(project_kernel, count, *sides, skip),
         in_specs=[smem] * 2 + [anywhere] * (2 * sum(sides) + count + len(before)),
         out_specs=[o[0] for o in outs],
         out_shape=[o[1] for o in outs],
@@ -189,8 +207,24 @@
         ],
         input_output_aliases={2 + 2 * sum(sides) + count: 0} if before else {},
         compiler_params=pltpu.CompilerParams(vmem_limit_bytes=VMEM),
-        cost_estimate=cost(count),
+        cost_estimate=cost(micros),
     )(first, places, *own, *far, *pieces, *before)
+
+
+def beat_kernel(in_ref, out_ref):
+    for i in range(in_ref.shape[0]):
+        out_ref[i] = in_ref[i]
+
+
+def beat(x):
+    smem = pl.BlockSpec(memory_space=pltpu.SMEM)
+    return pl.pallas_call(
+        beat_kernel,
+        in_specs=[smem],
+        out_specs=smem,
+        out_shape=jax.ShapeDtypeStruct(x.shape, x.dtype),
+        cost_estimate=cost(5),
+    )(x)
 
 
 def place_kernel(counts, place_ref, *refs):
@@ -245,12 +279,17 @@
     return lax.ppermute(x, axis, [(i, i + distance) for i in range(n - distance)])
 
 
+def rotate(x, axis, distance):
+    n = lax.axis_size(axis)
+    return lax.ppermute(x, axis, [(i, (i + distance) % n) for i in range(n)])
+
+
 def tie(x, *others):
     return lax.optimization_barrier((x, *others))[0]
 
 
 def cost(micros):
-    return pl.CostEstimate(flops=micros * 2 * 10**10, bytes_accessed=2**20, transcendentals=0)
+    return pl.CostEstimate(flops=int(micros * 2 * 10**10), bytes_accessed=2**20, transcendentals=0)
 
 
 def params():
@@ -300,11 +339,10 @@
         self.below = 0.0
 
     def climb(self, step):
-        self.total = after(self.total, self.axis, 8)
+        got = rotate(self.total, self.axis, 8 * (step + 1))
         source = self.plane - 8 * step - 1
         same = (source >= 0) * self.eq(jnp.maximum(source, 0), self.plane)
-        self.below = self.below + same * self.total.astype(f32)
-        return self.total
+        self.below = self.below + same * got.astype(f32)
 
     def gather_hop(self, bit):
         self.below = self.below.astype(bf16)
@@ -398,7 +436,7 @@
     )(q, rim, cq, kc, vc, *before)
 
 
-def hidden_call(start, qc, local, state, gain):
+def hidden_call(start, qc, local, state, gain, micros=5):
     rows, fw, vw = qc.shape[0], GROUP * FEAT, GROUP * HD
     groups = state.shape[0] // GROUP
 
@@ -421,7 +459,7 @@
         ),
         out_shape=jax.ShapeDtypeStruct((rows, groups * vw), bf16),
         compiler_params=params(),
-        cost_estimate=cost(4 * groups),
+        cost_estimate=cost(micros),
     )(start, qc, local, state, gain)
 
 
@@ -471,6 +509,7 @@
         return flip(piece, axis, 1)
 
     own0, width = weight, n * weight.shape[1]
+    mid = weight.shape[0] // 2
     scan = Scan(ids, axis)
     *kept, theirs = state_call((1 - core) * half, half, k, v, rim, ck, cv)
     got = share(theirs)
@@ -483,63 +522,61 @@
     y0, own1 = ties((y0, own1, before[1]))[:2]
 
     own2, d0 = over_z(own1), over_x(y0)
-    hop_x, x0 = ties((hop_x, x0, before[1]))[:2]
+    own1u, own1l = own1[:mid], own1[mid:]
+    hop_x, x0, own1u, own1l = ties((hop_x, x0, own1u, own1l, before[1]))[:4]
     scan.merge(2, hop_x)
     hop_y = scan.hop(4)
     qc, local = local_call(tie(q, scan.total), rim, cq, kc, vc, half, half, before)
-    y1 = over_y(tie(own1, local))
-    hop_y = tie(hop_y, local)
+    y1, x1u = over_y(tie(own1, local)), over_x(tie(own1u, local))
+    hop_y, own2 = ties((hop_y, own2, local))[:2]
     scan.merge(4, hop_y)
     scan.cut()
 
     for step in range(scan.climbs()):
-        hop_z = scan.climb(step)
-    scan.below, own2 = ties((scan.below, own2))
+        scan.climb(step)
+    scan.below, d0 = ties((scan.below, d0))
     own3 = over_z(tie(own2, scan.below))
     hop_x = scan.gather_hop(2)
-    hop_x, d0 = ties((hop_x, d0))
-    x1 = over_x(tie(own1, hop_x))
+    hop_x, y1, x1u = ties((hop_x, y1, x1u))
+    x1l = over_x(tie(own1l, hop_x))
+    x2 = over_x(tie(own2, hop_x))
     scan.gather(2, hop_x)
     hop_y = scan.gather_hop(4)
-    hop_y, y1 = ties((hop_y, y1))
     y2 = over_y(tie(own2, hop_y))
     d1 = over_z(tie(d0, hop_y))
     scan.gather(4, hop_y)
     keep, got = scan.finish()
     keep, own3 = ties((keep, own3))
-    x3 = over_x(own3)
     hid_a = hidden_call(core * half, qc, local, keep, gain)
-    got, x1 = ties((got, x1, hid_a))[:2]
-    y3 = over_y(tie(own3, got))
+    got, x1l = ties((got, x1l, hid_a))[:2]
+    x1 = jnp.concatenate([x1u, x1l], axis=0)
+    x3, y3 = over_x(tie(own3, got)), over_y(tie(own3, got))
     far_a = share(hid_a)
-    hid_b = hidden_call((1 - core) * half, qc, local, got, gain)
-    far_a, d1, y2 = ties((far_a, d1, y2, hid_b))[:3]
-    d2, x2 = over_z(d1), over_x(tie(own2, y2))
+    hid_b = hidden_call((1 - core) * half, qc, local, got, gain, 0.02)
+    y2, d1, x2 = ties((y2, d1, x2, hid_b))[:3]
+    d2 = over_z(d1)
     far_b = share(hid_b)
-    soon = [
-        (own0, 0, 0), (own1, 1, 0), (own2, 2, 0), (own3, 3, 0), (y0, 0, 4), (y1, 1, 4),
-        (y2, 2, 4), (x0, 0, 2), (x1, 1, 2), (d0, 0, 6), (d1, 1, 6),
+    where = [
+        (0, 0), (1, 0), (2, 0), (3, 0), (0, 4), (1, 4), (2, 4), (0, 2), (1, 2), (2, 2),
+        (0, 6), (1, 6), (3, 2), (3, 4), (2, 6), (3, 6),
     ]
-    late = [(None, 3, 4), (None, 3, 2), (None, 2, 6), (None, 2, 2), (None, 3, 6)]
     order = ring(n // 8)
     home = jnp.asarray(order, jnp.int32)
     spot = jnp.asarray([order.index(p) for p in range(n // 8)], jnp.int32)[me // 8]
-    shift = jnp.asarray([p[1] for p in soon + late], jnp.int32)
-    bits = jnp.asarray([p[2] for p in soon + late], jnp.int32)
+    shift = jnp.asarray([p[0] for p in where], jnp.int32)
+    bits = jnp.asarray([p[1] for p in where], jnp.int32)
     places = (home[(spot - shift) % (n // 8)] * 8 + (me % 8 ^ bits)).astype(jnp.int32)
-    pieces, early = [p[0] for p in soon], places[: len(soon)]
-    (out,) = project((hid_a, hid_b), (), core, width, pieces, early)
-    far_b, x3, y3, d2, out = ties((far_b, x3, y3, d2, out))
-    mid = x3.shape[0] // 2
+    mark = beat(tie(places, hid_b))
+    far_a, far_b, mark = ties((far_a, far_b, mark))
+    own, far = (hid_a, hid_b), (far_a, far_b)
+    pieces = [own0, own1, own2, own3, y0, y1, y2, x0, x1, x2, d0, d1]
+    out, back_a = project(own, far, core, width, pieces, mark[:12])
+    x3, y3, d2, out = ties((x3, y3, d2, out))
     d3y, d3z = over_y(x3[:mid]), over_z(d2[mid:])
-    (back_a,) = project((), (far_a, far_b), core, width, pieces, early)
-    d3y, d3z, x2, out = ties((d3y, d3z, x2, out, back_a))[:4]
-    pieces = [y3, x3, d2, x2, jnp.concatenate([d3y, d3z], axis=0)]
-    out, back_b = project(
-        (hid_a, hid_b), (far_a, far_b), core, width, pieces, places[len(soon) :], (out,)
-    )
-    back_a, back_b = share(back_a), share(back_b)
-    return place([back_a, back_b], places ^ 1, out)
+    d3 = jnp.concatenate([d3y, d3z], axis=0)
+    out, back_c = project(own, far, core, width, [x3, y3, d2, d3], places[12:], (out,))
+    backs = [share(b) for b in (back_a, back_c)]
+    return place(backs, places ^ 1, out)
 
 
 def on_device(

time: 207 us -> 193 us (0.932)
  waiting for transfers between devices: 51.1 us -> 34.3 us
  starting transfers between devices: 36.7 us -> 41 us
  Pallas kernels: 82.8 us -> 79.9 us
    ppermute x20 -> x21, waiting for transfers between devices: 46.1 us -> 20.9 us  [flip(): lax.ppermute(x, axis, [(i, i ^ bit) for i in range(lax.axis_size(axis))])]
    ppermute x6, waiting for transfers between devices: 1.47 us -> 11.6 us  [turn(): return lax.ppermute(x, axis, route)]
    ppermute x3 -> x1, starting transfers between devices: 9.69 us -> 3.68 us  [after(): lax.ppermute(x, axis, [(i, i + distance) for i in range(n - distance)])]
    ppermute x6, starting transfers between devices: 6.98 us -> 12.9 us  [turn(): return lax.ppermute(x, axis, route)]
    ppermute x0 -> x2, starting transfers between devices: none -> 4.69 us  [rotate(): return lax.ppermute(x, axis, [(i, (i + distance) % n) for i in range(n)])]
    slice x2, local copies, waits for them, and re-layouts: 3.79 us -> 0.07 us  [by_tree(): d3y, d3z = (over_y(x3[:mid]), over_z(d2[mid:]))]
    ppermute x3 -> x1, waiting for transfers between devices: 3.48 us -> 0.01 us  [after(): lax.ppermute(x, axis, [(i, i + distance) for i in range(n - distance)])]
    pallas_call x3, Pallas kernels: 39.8 us -> 36.9 us  [the longest x2 35.6 us: project(): pl.pallas_call(functools.partial(project_kernel, count, *sides, skip), in...]
  transfers between devices with their start and end apart: 29 -> 30, of which waited for: 9 -> 9; matrix products, arithmetic and copies ran while one was open for 8% -> 8% of each run, Pallas kernels for 39% -> 41%
where the time goes in v3:
time: 193 us; the launch traced here: 189 us
  Pallas kernels  79.9 us (41%)
  starting transfers between devices  41 us (21%)
  waiting for transfers between devices  34.3 us (18%)
  between operations  12.1 us (6%)
  local copies, waits for them, and re-layouts  11.6 us (6%)
  other arithmetic  10.5 us (5%)
    pallas_call x2, Pallas kernels, project(): pl.pallas_call(functools.partial(project_kernel, count, *sides, skip), in...  35.6 us
    ppermute x21, waiting for transfers between devices, flip(): lax.ppermute(x, axis, [(i, i ^ bit) for i in range(lax.axis_size(axis))])  20.9 us
    ppermute x21, starting transfers between devices, flip(): lax.ppermute(x, axis, [(i, i ^ bit) for i in range(lax.axis_size(axis))])  19.7 us
    pallas_call x2, Pallas kernels, hidden_call(): pl.pallas_call(hidden_kernel, grid_spec=pltpu.PrefetchScalarGridSpec(num_...  15.2 us
    pallas_call x2, Pallas kernels, local_call(): pl.pallas_call(local_kernel, grid=(groups,), in_specs=[cols(rows, fw, sta...  13.4 us
    ppermute x6, starting transfers between devices, turn(): return lax.ppermute(x, axis, route)  12.9 us
    ppermute x6, waiting for transfers between devices, turn(): return lax.ppermute(x, axis, route)  11.6 us
    pallas_call x2, Pallas kernels, state_call(): pl.pallas_call(state_kernel, grid_spec=pltpu.PrefetchScalarGridSpec(num_s...  11.5 us
  transfers between devices with their start and end apart: 30, of which 9 were waited for; matrix products, arithmetic and copies ran while one was open for 8% of the time, Pallas kernels for 41%

profile of v3, /device:TPU:11, one launch (start us, length us, event | category | flops | bytes accessed | tf_op | source)
XLA Modules:
  0.0 189.5 jit_solution(13167617563136130731)
XLA Ops:
  2.3 3.7 %collective-permute-start = (bf16[2,5120]{1,0:T(2,128)(2,1)S(1)}, bf16[2,5120]{1,0:T(2,128)(2,1)S(1)}, u32[]{:S(2)}, u32[]{:S(2)}) collective-permute-start(bf16[2,5120]{1,0:T(2,128)(2,1)S(1)} %pad_maximum_fusion.3), channel_id=1, source_target_pairs={{0,1},{1,2},{2,3},{3,4},{4,5},{5,6},{6,7},{7,8},{8,9},{9,10},{10,1... | collective-permute-start | bytes 61448 | tf_op jit(solution)/shard_map/ppermute | solution.py:279
  7.5 2.3 %collective-permute-start.5 = (bf16[4096,128]{1,0:T(8,128)(2,1)}, bf16[4096,128]{1,0:T(8,128)(2,1)}, u32[]{:S(2)}, u32[]{:S(2)}) collective-permute-start(bf16[4096,128]{1,0:T(8,128)(2,1)} %refs_4_.1), channel_id=1, source_target_pairs={{0,8},{1,9},{2,10},{3,11},{4,12},{5,13},{6,14},{7,15},{8,24},{9,25... | collective-permute-start | bytes 3145736 | tf_op jit(solution)/shard_map/ppermute | solution.py:270
  9.9 1.8 fusion.15
  16.2 5.7 %shard_map.127 = (bf16[512,512]{1,0:T(8,128)(2,1)}, bf16[512,4096]{1,0:T(8,128)(2,1)}, bf16[16,160,128]{2,1,0:T(8,128)(2,1)}) custom-call(s32[1]{0:T(128)S(6)} %mul.99.start_ref, bf16[512,512]{1,0:T(8,128)(2,1)} %k_ref.3, bf16[512,4096]{1,0:T(8,128)(2,1)} %v_ref.3, f32[2,5120]{1,0:T(2,128)} %convert_multiply_fusion.3.rk_ref.rv_ref.rq_ref, ...), custom_call_target="tpu_custom_call" | custom-call | flops 120000004096 | bytes 1048576 | tf_op jit(solution)/shard_map/pallas_call | solution.py:377
  21.9 5.8 %shard_map.128 = (bf16[512,512]{1,0:T(8,128)(2,1)}, bf16[512,4096]{1,0:T(8,128)(2,1)}, bf16[16,160,128]{2,1,0:T(8,128)(2,1)}) custom-call(s32[1]{0:T(128)S(6)} %mul.97.start_ref, bf16[512,512]{1,0:T(8,128)(2,1)} %k_ref.3, bf16[512,4096]{1,0:T(8,128)(2,1)} %v_ref.3, ...), custom_call_target="tpu_custom_call", output_to_operand_aliasing={{0}: (7, {}), {1}: (8, {})} | custom-call | flops 120000004096 | bytes 1048576 | tf_op jit(solution)/shard_map/pallas_call | solution.py:377
  27.7 1.6 fusion.1
  30.3 6.7 %shard_map.129 = (bf16[512,512]{1,0:T(8,128)(2,1)}, f32[512,4096]{1,0:T(8,128)}) custom-call(bf16[512,512]{1,0:T(8,128)(2,1)} %q_ref.1, f32[2,5120]{1,0:T(2,128)} %convert_multiply_fusion.3.rk_ref.rv_ref.rq_ref, f32[3,512]{1,0:T(4,128)} %cq_ref.3, bf16[512,512]{1,0:T(8,128)(2,1)} %get-tuple-element.64.kc_ref, bf16[512,4096]{1,0:T(8,128)(2,1)} %get-tuple-element.65.vc_ref), custom_call_target="tpu_custom_call" | custom-call | flops 120000004096 | bytes 1048576 | tf_op jit(solution)/shard_map/pallas_call | solution.py:416
  39.1 6.7 %collective-permute-done.2 = bf16[16,160,128]{2,1,0:T(8,128)(2,1)S(1)} collective-permute-done((bf16[16,160,128]{2,1,0:T(8,128)(2,1)S(1)}, bf16[16,160,128]{2,1,0:T(8,128)(2,1)S(1)}, u32[]{:S(2)}, u32[]{:S(2)}) %collective-permute-start.2) | collective-permute-done | bytes 655392 | tf_op jit(solution)/shard_map/ppermute | solution.py:274
  46.3 6.7 %shard_map.130 = (bf16[512,512]{1,0:T(8,128)(2,1)}, f32[512,4096]{1,0:T(8,128)}) custom-call(bf16[512,512]{1,0:T(8,128)(2,1)} %q_ref.1, f32[2,5120]{1,0:T(2,128)} %convert_multiply_fusion.3.rk_ref.rv_ref.rq_ref, f32[3,512]{1,0:T(4,128)} %cq_ref.3, bf16[512,512]{1,0:T(8,128)(2,1)} %get-tuple-element.64.kc_ref, ...), custom_call_target="tpu_custom_call", output_to_operand_aliasing={{0}: (5, {}), {1}: (6, {})} | custom-call | flops 120000004096 | bytes 1048576 | tf_op jit(solution)/shard_map/pallas_call | solution.py:416
  55.5 5.2 %collective-permute-done.6 = bf16[16,160,128]{2,1,0:T(8,128)(2,1)S(1)} collective-permute-done((bf16[16,160,128]{2,1,0:T(8,128)(2,1)S(1)}, bf16[16,160,128]{2,1,0:T(8,128)(2,1)S(1)}, u32[]{:S(2)}, u32[]{:S(2)}) %collective-permute-start.6) | collective-permute-done | bytes 655392 | tf_op jit(solution)/shard_map/ppermute | solution.py:274
  61.8 3.7 %collective-permute-start.8 = (bf16[4,160,128]{2,1,0:T(8,128)(2,1)S(1)}, bf16[4,160,128]{2,1,0:T(8,128)(2,1)S(1)}, u32[]{:S(2)}, u32[]{:S(2)}) collective-permute-start(bf16[4,160,128]{2,1,0:T(8,128)(2,1)S(1)} %fusion.12), channel_id=1, source_target_pairs={{0,8},{1,9},{2,10},{3,11},{4,12},{5,13},{6,14},{7,15},{8,16},{9,17... | collective-permute-start | bytes 491528 | tf_op jit(solution)/shard_map/ppermute | solution.py:284
  73.9 1.8 collective-permute-done.9
  76.8 3.2 %collective-permute-start.15 = (bf16[4096,128]{1,0:T(8,128)(2,1)}, bf16[4096,128]{1,0:T(8,128)(2,1)}, u32[]{:S(2)}, u32[]{:S(2)}) collective-permute-start(bf16[4096,128]{1,0:T(8,128)(2,1)} %collective-permute-done.7.refs_6_), channel_id=1, source_target_pairs={{0,8},{1,9},{2,10},{3,11},{4,12},{5,13},{6,14},{7,15},{8,24},{9,25... | collective-permute-start | bytes 3145736 | tf_op jit(solution)/shard_map/ppermute | solution.py:270
  79.9 3.3 %collective-permute-done.12.refs_9_ = bf16[4096,128]{1,0:T(8,128)(2,1)} collective-permute-done((bf16[4096,128]{1,0:T(8,128)(2,1)}, bf16[4096,128]{1,0:T(8,128)(2,1)}, u32[]{:S(2)}, u32[]{:S(2)}) %collective-permute-start.12) | collective-permute-done | bytes 1048608 | tf_op jit(solution)/shard_map/ppermute | solution.py:274
  86.9 4.0 %collective-permute-done.14 = bf16[8,160,128]{2,1,0:T(8,128)(2,1)} collective-permute-done((bf16[8,160,128]{2,1,0:T(8,128)(2,1)}, bf16[8,160,128]{2,1,0:T(8,128)(2,1)}, u32[]{:S(2)}, u32[]{:S(2)}) %collective-permute-start.14) | collective-permute-done | bytes 327712 | tf_op jit(solution)/shard_map/ppermute | solution.py:274
  91.9 1.6 fusion.6
  93.5 3.6 %collective-permute-start.17 = (bf16[16,160,128]{2,1,0:T(8,128)(2,1)S(1)}, bf16[16,160,128]{2,1,0:T(8,128)(2,1)S(1)}, u32[]{:S(2)}, u32[]{:S(2)}) collective-permute-start(bf16[16,160,128]{2,1,0:T(8,128)(2,1)S(1)} %get-tuple-element.113), channel_id=1, source_target_pairs={{0,1},{1,0},{2,3},{3,2},{4,5},{5,4},{6,7},{7,6},{8,9},{9,8},{10,11... | collective-permute-start | bytes 1966088 | tf_op jit(solution)/shard_map/ppermute | solution.py:274
  97.0 4.3 %collective-permute-start.21 = (bf16[4096,128]{1,0:T(8,128)(2,1)}, bf16[4096,128]{1,0:T(8,128)(2,1)}, u32[]{:S(2)}, u32[]{:S(2)}) collective-permute-start(bf16[4096,128]{1,0:T(8,128)(2,1)} %collective-permute-done.10.refs_14_), channel_id=1, source_target_pairs={{0,8},{1,9},{2,10},{3,11},{4,12},{5,13},{6,14},{7,15},{8,24},{9,25... | collective-permute-start | bytes 3145736 | tf_op jit(solution)/shard_map/ppermute | solution.py:270
  101.3 2.3 %collective-permute-done.15.refs_7_ = bf16[4096,128]{1,0:T(8,128)(2,1)} collective-permute-done((bf16[4096,128]{1,0:T(8,128)(2,1)}, bf16[4096,128]{1,0:T(8,128)(2,1)}, u32[]{:S(2)}, u32[]{:S(2)}) %collective-permute-start.15) | collective-permute-done | bytes 1048608 | tf_op jit(solution)/shard_map/ppermute | solution.py:270
  103.8 7.6 %shard_map.131.refs_0_ = bf16[512,2048]{1,0:T(8,128)(2,1)} custom-call(s32[1]{0:T(128)S(6)} %mul.97.start_ref, bf16[512,512]{1,0:T(8,128)(2,1)} %get-tuple-element.71.qc_ref, f32[512,4096]{1,0:T(8,128)} %get-tuple-element.72.loc_ref, bf16[16,160,128]{2,1,0:T(8,128)(2,1)} %get-tuple-element.82.s_ref, f32[1,4096]{1,0:T(1,128)} %bitcast.13), custom_call_target="tpu_custom_call" | custom-call | flops 99999997952 | bytes 1048576 | tf_op jit(solution)/shard_map/pallas_call | solution.py:446
  111.4 2.6 %collective-permute-start.16 = (bf16[512,2048]{1,0:T(8,128)(2,1)}, bf16[512,2048]{1,0:T(8,128)(2,1)S(1)}, u32[]{:S(2)}, u32[]{:S(2)}) collective-permute-start(bf16[512,2048]{1,0:T(8,128)(2,1)} %shard_map.131.refs_0_), channel_id=1, source_target_pairs={{0,1},{1,0},{2,3},{3,2},{4,5},{5,4},{6,7},{7,6},{8,9},{9,8},{10,11... | collective-permute-start | bytes 6291464 | tf_op jit(solution)/shard_map/ppermute | solution.py:274
  114.9 7.6 %shard_map.132.refs_1_ = bf16[512,2048]{1,0:T(8,128)(2,1)} custom-call(s32[1]{0:T(128)S(6)} %mul.99.start_ref, bf16[512,512]{1,0:T(8,128)(2,1)} %get-tuple-element.71.qc_ref, f32[512,4096]{1,0:T(8,128)} %get-tuple-element.72.loc_ref, bf16[16,160,128]{2,1,0:T(8,128)(2,1)} %copy-done.4, f32[1,4096]{1,0:T(1,128)} %bitcast.14), custom_call_target="tpu_custom_call" | custom-call | flops 400000000 | bytes 1048576 | tf_op jit(solution)/shard_map/pallas_call | solution.py:446
  123.9 2.1 %pad_maximum_fusion.refs_12_ = bf16[4096,128]{1,0:T(8,128)(2,1)} fusion(bf16[2048,128]{1,0:T(8,128)(2,1)S(1)} %copy-done.6, bf16[2048,128]{1,0:T(8,128)(2,1)} %collective-permute-done.13), kind=kLoop, calls=%fused_computation.16 | loop fusion | flops 2097152 | bytes 2097152 | tf_op jit(solution)/shard_map/concatenate | solution.py:552
  127.6 2.4 %collective-permute-start.26 = (bf16[4096,128]{1,0:T(8,128)(2,1)}, bf16[4096,128]{1,0:T(8,128)(2,1)S(1)}, u32[]{:S(2)}, u32[]{:S(2)}) collective-permute-start(bf16[4096,128]{1,0:T(8,128)(2,1)} %collective-permute-done.21.refs_15_), channel_id=1, source_target_pairs={{0,8},{1,9},{2,10},{3,11},{4,12},{5,13},{6,14},{7,15},{8,24},{9,25... | collective-permute-start | bytes 3145736 | tf_op jit(solution)/shard_map/ppermute | solution.py:270
  130.0 1.4 copy-done.11
  131.3 23.0 %shard_map.134 = (bf16[512,4096]{1,0:T(8,128)(2,1)}, bf16[12,512,128]{2,1,0:T(8,128)(2,1)}) custom-call(s32[1]{0:T(128)} %bitcast.1.first_ref, s32[12]{0:T(128)} %bitcast.15, bf16[512,2048]{1,0:T(8,128)(2,1)} %shard_map.131.refs_0_, bf16[512,2048]{1,0:T(8,128)(2,1)} %shard_map.132.refs_1_, bf16[512,2048]{1,0:T(8,128)(2,1)} %copy-done.11, ...), custom_call_target="tpu_custom_call" | custom-call | flops 99999997952 | bytes 1048576 | tf_op jit(solution)/shard_map/pallas_call | solution.py:195
  156.8 1.7 collective-permute-start.23
  158.5 8.4 %collective-permute-done.28 = bf16[2048,128]{1,0:T(8,128)(2,1)S(1)} collective-permute-done((bf16[2048,128]{1,0:T(8,128)(2,1)S(1)}, bf16[2048,128]{1,0:T(8,128)(2,1)S(1)}, u32[]{:S(2)}, u32[]{:S(2)}) %collective-permute-start.28) | collective-permute-done | bytes 524320 | tf_op jit(solution)/shard_map/ppermute | solution.py:270
  168.0 12.6 %shard_map.135 = (bf16[512,4096]{1,0:T(8,128)(2,1)}, bf16[4,512,128]{2,1,0:T(8,128)(2,1)}) custom-call(s32[1]{0:T(128)} %bitcast.1.first_ref, s32[4]{0:T(128)} %slice.33.place_ref, bf16[512,2048]{1,0:T(8,128)(2,1)} %shard_map.131.refs_0_, bf16[512,2048]{1,0:T(8,128)(2,1)} %shard_map.132.refs_1_, ...), custom_call_target="tpu_custom_call", output_to_operand_aliasing={{0}: (10, {})} | custom-call | flops 99999997952 | bytes 1048576 | tf_op jit(solution)/shard_map/pallas_call | solution.py:195
  180.6 2.6 %collective-permute-start.29 = (bf16[4,512,128]{2,1,0:T(8,128)(2,1)}, bf16[4,512,128]{2,1,0:T(8,128)(2,1)S(1)}, u32[]{:S(2)}, u32[]{:S(2)}) collective-permute-start(bf16[4,512,128]{2,1,0:T(8,128)(2,1)} %get-tuple-element.109), channel_id=1, source_target_pairs={{0,1},{1,0},{2,3},{3,2},{4,5},{5,4},{6,7},{7,6},{8,9},{9,8},{10,11... | collective-permute-start | bytes 1572872 | tf_op jit(solution)/shard_map/ppermute | solution.py:274
  183.3 1.7 collective-permute-done.29.refs_1_
  186.3 3.0 %shard_map.136 = bf16[512,4096]{1,0:T(8,128)(2,1)} custom-call(s32[16]{0:T(128)} %get-tuple-element.111.place_ref, bf16[12,512,128]{2,1,0:T(8,128)(2,1)} %copy-done.13, bf16[4,512,128]{2,1,0:T(8,128)(2,1)} %copy-done.15, bf16[512,4096]{1,0:T(8,128)(2,1)} %get-tuple-element.110.refs_2_), custom_call_target="tpu_custom_call", output_to_operand_aliasing={{}: (3, {})} | custom-call | flops 60000002048 | bytes 1048576 | tf_op jit(solution)/shard_map/pallas_call | solution.py:247
  (98 shorter events, 27.0 us)
Async XLA Ops:
  2.3 13.2 %collective-permute-start = (bf16[2,5120]{1,0:T(2,128)(2,1)S(1)}, bf16[2,5120]{1,0:T(2,128)(2,1)S(1)}, u32[]{:S(2)}, u32[]{:S(2)}) collective-permute-start(bf16[2,5120]{1,0:T(2,128)(2,1)S(1)} %pad_maximum_fusion.3), channel_id=1, source_target_pairs={{0,1},{1,2},{2,3},{3,4},{4,5},{5,6},{6,7},{7,8},{8,9},{9,10},{10,1... | collective-permute-start | bytes 61448 | tf_op jit(solution)/shard_map/ppermute | solution.py:279
  6.0 31.0 %collective-permute-start.4 = (bf16[4096,128]{1,0:T(8,128)(2,1)}, bf16[4096,128]{1,0:T(8,128)(2,1)}, u32[]{:S(2)}, u32[]{:S(2)}) collective-permute-start(bf16[4096,128]{1,0:T(8,128)(2,1)} %refs_4_.1), channel_id=1, source_target_pairs={{0,4},{1,5},{2,6},{3,7},{4,0},{5,1},{6,2},{7,3},{8,12},{9,13},{10,... | collective-permute-start | bytes 3145736 | tf_op jit(solution)/shard_map/ppermute | solution.py:274
  7.3 31.8 %collective-permute-start.3 = (bf16[4096,128]{1,0:T(8,128)(2,1)}, bf16[4096,128]{1,0:T(8,128)(2,1)}, u32[]{:S(2)}, u32[]{:S(2)}) collective-permute-start(bf16[4096,128]{1,0:T(8,128)(2,1)} %refs_4_.1), channel_id=1, source_target_pairs={{0,2},{1,3},{2,0},{3,1},{4,6},{5,7},{6,4},{7,5},{8,10},{9,11},{10,... | collective-permute-start | bytes 3145736 | tf_op jit(solution)/shard_map/ppermute | solution.py:274
  7.5 29.4 %collective-permute-start.5 = (bf16[4096,128]{1,0:T(8,128)(2,1)}, bf16[4096,128]{1,0:T(8,128)(2,1)}, u32[]{:S(2)}, u32[]{:S(2)}) collective-permute-start(bf16[4096,128]{1,0:T(8,128)(2,1)} %refs_4_.1), channel_id=1, source_target_pairs={{0,8},{1,9},{2,10},{3,11},{4,12},{5,13},{6,14},{7,15},{8,24},{9,25... | collective-permute-start | bytes 3145736 | tf_op jit(solution)/shard_map/ppermute | solution.py:270
  21.9 5.8 %collective-permute-start.1 = (bf16[16,160,128]{2,1,0:T(8,128)(2,1)}, bf16[16,160,128]{2,1,0:T(8,128)(2,1)S(1)}, u32[]{:S(2)}, u32[]{:S(2)}) collective-permute-start(bf16[16,160,128]{2,1,0:T(8,128)(2,1)} %get-tuple-element.58), channel_id=1, source_target_pairs={{0,1},{1,0},{2,3},{3,2},{4,5},{5,4},{6,7},{7,6},{8,9},{9,8},{10,11... | collective-permute-start | bytes 1966088 | tf_op jit(solution)/shard_map/ppermute | solution.py:274
  29.3 16.5 %collective-permute-start.2 = (bf16[16,160,128]{2,1,0:T(8,128)(2,1)S(1)}, bf16[16,160,128]{2,1,0:T(8,128)(2,1)S(1)}, u32[]{:S(2)}, u32[]{:S(2)}) collective-permute-start(bf16[16,160,128]{2,1,0:T(8,128)(2,1)S(1)} %fusion.1), channel_id=1, source_target_pairs={{0,2},{1,3},{2,0},{3,1},{4,6},{5,7},{6,4},{7,5},{8,10},{9,11},{10,... | collective-permute-start | bytes 1966088 | tf_op jit(solution)/shard_map/ppermute | solution.py:274
  37.0 38.8 %collective-permute-start.10 = (bf16[4096,128]{1,0:T(8,128)(2,1)}, bf16[4096,128]{1,0:T(8,128)(2,1)}, u32[]{:S(2)}, u32[]{:S(2)}) collective-permute-start(bf16[4096,128]{1,0:T(8,128)(2,1)} %collective-permute-done.4.refs_8_), channel_id=1, source_target_pairs={{0,2},{1,3},{2,0},{3,1},{4,6},{5,7},{6,4},{7,5},{8,10},{9,11},{10,... | collective-permute-start | bytes 3145736 | tf_op jit(solution)/shard_map/ppermute | solution.py:274
  37.6 24.0 %collective-permute-start.7 = (bf16[4096,128]{1,0:T(8,128)(2,1)}, bf16[4096,128]{1,0:T(8,128)(2,1)}, u32[]{:S(2)}, u32[]{:S(2)}) collective-permute-start(bf16[4096,128]{1,0:T(8,128)(2,1)} %collective-permute-done.5.refs_5_), channel_id=1, source_target_pairs={{0,8},{1,9},{2,10},{3,11},{4,12},{5,13},{6,14},{7,15},{8,24},{9,25... | collective-permute-start | bytes 3145736 | tf_op jit(solution)/shard_map/ppermute | solution.py:270
  46.0 14.7 %collective-permute-start.6 = (bf16[16,160,128]{2,1,0:T(8,128)(2,1)S(1)}, bf16[16,160,128]{2,1,0:T(8,128)(2,1)S(1)}, u32[]{:S(2)}, u32[]{:S(2)}) collective-permute-start(bf16[16,160,128]{2,1,0:T(8,128)(2,1)S(1)} %fusion.8), channel_id=1, source_target_pairs={{0,4},{1,5},{2,6},{3,7},{4,0},{5,1},{6,2},{7,3},{8,12},{9,13},{10,... | collective-permute-start | bytes 1966088 | tf_op jit(solution)/shard_map/ppermute | solution.py:274
  53.0 30.2 %collective-permute-start.12 = (bf16[4096,128]{1,0:T(8,128)(2,1)}, bf16[4096,128]{1,0:T(8,128)(2,1)}, u32[]{:S(2)}, u32[]{:S(2)}) collective-permute-start(bf16[4096,128]{1,0:T(8,128)(2,1)} %collective-permute-done.5.refs_5_), channel_id=1, source_target_pairs={{0,4},{1,5},{2,6},{3,7},{4,0},{5,1},{6,2},{7,3},{8,12},{9,13},{10,... | collective-permute-start | bytes 3145736 | tf_op jit(solution)/shard_map/ppermute | solution.py:274
  55.5 20.6 %copy-start.16 = (s32[16]{0:T(128)S(1)}, s32[16]{0:T(128)}, u32[]{:S(2)}) copy-start(s32[16]{0:T(128)} %constant.155) | copy-start | bytes 196
  61.8 23.1 %copy-start.9 = (s32[16]{0:T(128)S(1)}, s32[16]{0:T(128)}, u32[]{:S(2)}) copy-start(s32[16]{0:T(128)} %constant.154.clone) | copy-start | bytes 196
  61.8 12.1 %collective-permute-start.8 = (bf16[4,160,128]{2,1,0:T(8,128)(2,1)S(1)}, bf16[4,160,128]{2,1,0:T(8,128)(2,1)S(1)}, u32[]{:S(2)}, u32[]{:S(2)}) collective-permute-start(bf16[4,160,128]{2,1,0:T(8,128)(2,1)S(1)} %fusion.12), channel_id=1, source_target_pairs={{0,8},{1,9},{2,10},{3,11},{4,12},{5,13},{6,14},{7,15},{8,16},{9,17... | collective-permute-start | bytes 491528 | tf_op jit(solution)/shard_map/ppermute | solution.py:284
  65.5 10.2 %collective-permute-start.9 = (bf16[4,160,128]{2,1,0:T(8,128)(2,1)S(1)}, bf16[4,160,128]{2,1,0:T(8,128)(2,1)S(1)}, u32[]{:S(2)}, u32[]{:S(2)}) collective-permute-start(bf16[4,160,128]{2,1,0:T(8,128)(2,1)S(1)} %fusion.12), channel_id=1, source_target_pairs={{0,16},{1,17},{2,18},{3,19},{4,20},{5,21},{6,22},{7,23},{8,24},{9,... | collective-permute-start | bytes 491528 | tf_op jit(solution)/shard_map/ppermute | solution.py:284
  66.5 13.4 %collective-permute-start.13 = (bf16[2048,128]{1,0:T(8,128)(2,1)S(1)}, bf16[2048,128]{1,0:T(8,128)(2,1)}, u32[]{:S(2)}, u32[]{:S(2)}) collective-permute-start(bf16[2048,128]{1,0:T(8,128)(2,1)S(1)} %get-tuple-element.78), channel_id=1, source_target_pairs={{0,2},{1,3},{2,0},{3,1},{4,6},{5,7},{6,4},{7,5},{8,10},{9,11},{10,... | collective-permute-start | bytes 1572872 | tf_op jit(solution)/shard_map/ppermute | solution.py:274
  75.8 7.4 %collective-permute-start.11 = (bf16[4,160,128]{2,1,0:T(8,128)(2,1)S(1)}, bf16[4,160,128]{2,1,0:T(8,128)(2,1)S(1)}, u32[]{:S(2)}, u32[]{:S(2)}) collective-permute-start(bf16[4,160,128]{2,1,0:T(8,128)(2,1)S(1)} %multiply_add_fusion), channel_id=1, source_target_pairs={{0,2},{1,3},{2,0},{3,1},{4,6},{5,7},{6,4},{7,5},{8,10},{9,11},{10,... | collective-permute-start | bytes 491528 | tf_op jit(solution)/shard_map/ppermute | solution.py:274
  76.8 26.8 %collective-permute-start.15 = (bf16[4096,128]{1,0:T(8,128)(2,1)}, bf16[4096,128]{1,0:T(8,128)(2,1)}, u32[]{:S(2)}, u32[]{:S(2)}) collective-permute-start(bf16[4096,128]{1,0:T(8,128)(2,1)} %collective-permute-done.7.refs_6_), channel_id=1, source_target_pairs={{0,8},{1,9},{2,10},{3,11},{4,12},{5,13},{6,14},{7,15},{8,24},{9,25... | collective-permute-start | bytes 3145736 | tf_op jit(solution)/shard_map/ppermute | solution.py:270
  84.0 6.9 %collective-permute-start.14 = (bf16[8,160,128]{2,1,0:T(8,128)(2,1)}, bf16[8,160,128]{2,1,0:T(8,128)(2,1)}, u32[]{:S(2)}, u32[]{:S(2)}) collective-permute-start(bf16[8,160,128]{2,1,0:T(8,128)(2,1)} %pad_maximum_fusion.2), channel_id=1, source_target_pairs={{0,4},{1,5},{2,6},{3,7},{4,0},{5,1},{6,2},{7,3},{8,12},{9,13},{10,... | collective-permute-start | bytes 983048 | tf_op jit(solution)/shard_map/ppermute | solution.py:274
  85.4 26.0 %collective-permute-start.18 = (bf16[2048,128]{1,0:T(8,128)(2,1)S(1)}, bf16[2048,128]{1,0:T(8,128)(2,1)S(1)}, u32[]{:S(2)}, u32[]{:S(2)}) collective-permute-start(bf16[2048,128]{1,0:T(8,128)(2,1)S(1)} %get-tuple-element.84), channel_id=1, source_target_pairs={{0,2},{1,3},{2,0},{3,1},{4,6},{5,7},{6,4},{7,5},{8,10},{9,11},{10,... | collective-permute-start | bytes 1572872 | tf_op jit(solution)/shard_map/ppermute | solution.py:274
  86.7 39.3 %collective-permute-start.22 = (bf16[4096,128]{1,0:T(8,128)(2,1)}, bf16[4096,128]{1,0:T(8,128)(2,1)}, u32[]{:S(2)}, u32[]{:S(2)}) collective-permute-start(bf16[4096,128]{1,0:T(8,128)(2,1)} %collective-permute-done.7.refs_6_), channel_id=1, source_target_pairs={{0,2},{1,3},{2,0},{3,1},{4,6},{5,7},{6,4},{7,5},{8,10},{9,11},{10,... | collective-permute-start | bytes 3145736 | tf_op jit(solution)/shard_map/ppermute | solution.py:274
  93.5 20.6 %collective-permute-start.17 = (bf16[16,160,128]{2,1,0:T(8,128)(2,1)S(1)}, bf16[16,160,128]{2,1,0:T(8,128)(2,1)S(1)}, u32[]{:S(2)}, u32[]{:S(2)}) collective-permute-start(bf16[16,160,128]{2,1,0:T(8,128)(2,1)S(1)} %get-tuple-element.113), channel_id=1, source_target_pairs={{0,1},{1,0},{2,3},{3,2},{4,5},{5,4},{6,7},{7,6},{8,9},{9,8},{10,11... | collective-permute-start | bytes 1966088 | tf_op jit(solution)/shard_map/ppermute | solution.py:274
  97.0 30.2 %collective-permute-start.21 = (bf16[4096,128]{1,0:T(8,128)(2,1)}, bf16[4096,128]{1,0:T(8,128)(2,1)}, u32[]{:S(2)}, u32[]{:S(2)}) collective-permute-start(bf16[4096,128]{1,0:T(8,128)(2,1)} %collective-permute-done.10.refs_14_), channel_id=1, source_target_pairs={{0,8},{1,9},{2,10},{3,11},{4,12},{5,13},{6,14},{7,15},{8,24},{9,25... | collective-permute-start | bytes 3145736 | tf_op jit(solution)/shard_map/ppermute | solution.py:270
  103.6 24.0 %collective-permute-start.20 = (bf16[4096,128]{1,0:T(8,128)(2,1)}, bf16[4096,128]{1,0:T(8,128)(2,1)}, u32[]{:S(2)}, u32[]{:S(2)}) collective-permute-start(bf16[4096,128]{1,0:T(8,128)(2,1)} %collective-permute-done.7.refs_6_), channel_id=1, source_target_pairs={{0,4},{1,5},{2,6},{3,7},{4,0},{5,1},{6,2},{7,3},{8,12},{9,13},{10,... | collective-permute-start | bytes 3145736 | tf_op jit(solution)/shard_map/ppermute | solution.py:274
  111.4 18.5 %collective-permute-start.16 = (bf16[512,2048]{1,0:T(8,128)(2,1)}, bf16[512,2048]{1,0:T(8,128)(2,1)S(1)}, u32[]{:S(2)}, u32[]{:S(2)}) collective-permute-start(bf16[512,2048]{1,0:T(8,128)(2,1)} %shard_map.131.refs_0_), channel_id=1, source_target_pairs={{0,1},{1,0},{2,3},{3,2},{4,5},{5,4},{6,7},{7,6},{8,9},{9,8},{10,11... | collective-permute-start | bytes 6291464 | tf_op jit(solution)/shard_map/ppermute | solution.py:274
  122.5 7.5 %collective-permute-start.19 = (bf16[512,2048]{1,0:T(8,128)(2,1)}, bf16[512,2048]{1,0:T(8,128)(2,1)}, u32[]{:S(2)}, u32[]{:S(2)}) collective-permute-start(bf16[512,2048]{1,0:T(8,128)(2,1)} %shard_map.132.refs_1_), channel_id=1, source_target_pairs={{0,1},{1,0},{2,3},{3,2},{4,5},{5,4},{6,7},{7,6},{8,9},{9,8},{10,11... | collective-permute-start | bytes 6291464 | tf_op jit(solution)/shard_map/ppermute | solution.py:274
  126.0 28.3 %collective-permute-start.25 = (bf16[4096,128]{1,0:T(8,128)(2,1)}, bf16[4096,128]{1,0:T(8,128)(2,1)S(1)}, u32[]{:S(2)}, u32[]{:S(2)}) collective-permute-start(bf16[4096,128]{1,0:T(8,128)(2,1)} %collective-permute-done.15.refs_7_), channel_id=1, source_target_pairs={{0,4},{1,5},{2,6},{3,7},{4,0},{5,1},{6,2},{7,3},{8,12},{9,13},{10,... | collective-permute-start | bytes 3145736 | tf_op jit(solution)/shard_map/ppermute | solution.py:274
  127.2 27.1 %collective-permute-start.24 = (bf16[4096,128]{1,0:T(8,128)(2,1)}, bf16[4096,128]{1,0:T(8,128)(2,1)S(1)}, u32[]{:S(2)}, u32[]{:S(2)}) collective-permute-start(bf16[4096,128]{1,0:T(8,128)(2,1)} %collective-permute-done.15.refs_7_), channel_id=1, source_target_pairs={{0,2},{1,3},{2,0},{3,1},{4,6},{5,7},{6,4},{7,5},{8,10},{9,11},{10,... | collective-permute-start | bytes 3145736 | tf_op jit(solution)/shard_map/ppermute | solution.py:274
  127.6 26.8 %collective-permute-start.26 = (bf16[4096,128]{1,0:T(8,128)(2,1)}, bf16[4096,128]{1,0:T(8,128)(2,1)S(1)}, u32[]{:S(2)}, u32[]{:S(2)}) collective-permute-start(bf16[4096,128]{1,0:T(8,128)(2,1)} %collective-permute-done.21.refs_15_), channel_id=1, source_target_pairs={{0,8},{1,9},{2,10},{3,11},{4,12},{5,13},{6,14},{7,15},{8,24},{9,25... | collective-permute-start | bytes 3145736 | tf_op jit(solution)/shard_map/ppermute | solution.py:270
  154.5 12.4 %collective-permute-start.28 = (bf16[2048,128]{1,0:T(8,128)(2,1)S(1)}, bf16[2048,128]{1,0:T(8,128)(2,1)S(1)}, u32[]{:S(2)}, u32[]{:S(2)}) collective-permute-start(bf16[2048,128]{1,0:T(8,128)(2,1)S(1)} %slice.35), channel_id=1, source_target_pairs={{0,8},{1,9},{2,10},{3,11},{4,12},{5,13},{6,14},{7,15},{8,24},{9,25... | collective-permute-start | bytes 1572872 | tf_op jit(solution)/shard_map/ppermute | solution.py:270
  155.1 11.8 %collective-permute-start.27 = (bf16[2048,128]{1,0:T(8,128)(2,1)S(1)}, bf16[2048,128]{1,0:T(8,128)(2,1)S(1)}, u32[]{:S(2)}, u32[]{:S(2)}) collective-permute-start(bf16[2048,128]{1,0:T(8,128)(2,1)S(1)} %slice.34), channel_id=1, source_target_pairs={{0,4},{1,5},{2,6},{3,7},{4,0},{5,1},{6,2},{7,3},{8,12},{9,13},{10,... | collective-permute-start | bytes 1572872 | tf_op jit(solution)/shard_map/ppermute | solution.py:274
  156.8 28.2 %collective-permute-start.23 = (bf16[12,512,128]{2,1,0:T(8,128)(2,1)S(1)}, bf16[12,512,128]{2,1,0:T(8,128)(2,1)S(1)}, u32[]{:S(2)}, u32[]{:S(2)}) collective-permute-start(bf16[12,512,128]{2,1,0:T(8,128)(2,1)S(1)} %copy-done.12), channel_id=1, source_target_pairs={{0,1},{1,0},{2,3},{3,2},{4,5},{5,4},{6,7},{7,6},{8,9},{9,8},{10,11... | collective-permute-start | bytes 4718600 | tf_op jit(solution)/shard_map/ppermute | solution.py:274
  180.6 4.4 %collective-permute-start.29 = (bf16[4,512,128]{2,1,0:T(8,128)(2,1)}, bf16[4,512,128]{2,1,0:T(8,128)(2,1)S(1)}, u32[]{:S(2)}, u32[]{:S(2)}) collective-permute-start(bf16[4,512,128]{2,1,0:T(8,128)(2,1)} %get-tuple-element.109), channel_id=1, source_target_pairs={{0,1},{1,0},{2,3},{3,2},{4,5},{5,4},{6,7},{7,6},{8,9},{9,8},{10,11... | collective-permute-start | bytes 1572872 | tf_op jit(solution)/shard_map/ppermute | solution.py:274
  (15 other events, 93.7 us)

commit v4 on v3

--- a/solution.py
+++ b/solution.py
@@ -112,9 +112,9 @@
             out_ref[:, cols] = (y * scale * gain_ref[:, cols]).astype(bf16)
 
 
-def project_kernel(pieces, own, far, skip, first_ref, place_ref, *refs):
-    sides = own + far
-    hidden, weights = refs[: 2 * sides], refs[2 * sides : 2 * sides + pieces]
+def project_kernel(parts, own, far, first_ref, place_ref, *refs):
+    sides, pieces = own + far, len(parts)
+    hidden, weights = refs[: 2 * sides], list(refs[2 * sides :])
     rows_in, held, done, hid_sems, sems, out_sems = refs[-6:]
     outs = refs[-6 - sides : -6]
     depth = hidden[0].shape[1]
@@ -127,17 +127,19 @@
                 hidden[p], rows_in.at[p // 2, :, pl.ds(at, depth)], hid_sems.at[p]
             )
         )
-    copies = [
-        pltpu.make_async_copy(weights[i], held.at[:, HD * i : HD * (i + 1)], sems.at[i])
-        for i in range(pieces)
-    ]
+    copies = []
+    for i in range(pieces):
+        row, copies_of = 0, []
+        for _ in range(parts[i]):
+            ref = weights.pop(0)
+            to = held.at[row : row + ref.shape[0], HD * i : HD * (i + 1)]
+            copies_of.append(pltpu.make_async_copy(ref, to, sems.at[i, len(copies_of)]))
+            row += ref.shape[0]
+        copies.append(copies_of)
     near = 2 * own
-    if skip:
-        loads = loads[near:] + loads[:near]
-        near = 2 * far
     bounds = [0, min(2, pieces)] + list(range(6, pieces, 4)) + [pieces] * (pieces > 2)
     groups = [range(c, e) for c, e in zip(bounds, bounds[1:])]
-    ahead = [copies[g[0] : g[-1] + 1] for g in groups] + [[], []]
+    ahead = [[c for i in g for c in copies[i]] for g in groups] + [[]]
     for copy in loads[:near] + ahead[0]:
         copy.start()
     stores = []
@@ -167,24 +169,21 @@
             for j, i in enumerate(group):
                 outs[-1][i] = total[:, HD * j : HD * (j + 1)].astype(bf16)
 
-        if skip:
-            theirs()
-        elif own:
+        if own:
             mine()
         if at == 0:
             for copy in loads[near:]:
                 copy.wait()
-        if skip and group[0] >= skip:
-            mine()
-        elif far and not skip:
+        if far:
             theirs()
     for store in stores:
         store.wait()
 
 
-def project(own, far, first, width, pieces, places, before=(), skip=0, micros=5):
+def project(own, far, first, width, pieces, places, before=()):
     rows, half = (own + far)[0].shape
-    count, depth = len(pieces), pieces[0].shape[0]
+    pieces = [p if isinstance(p, tuple) else (p,) for p in pieces]
+    count, depth, parts = len(pieces), 2 * half, [len(p) for p in pieces]
     smem, vmem, anywhere = (pl.BlockSpec(memory_space=m) for m in (pltpu.SMEM, pltpu.VMEM, pl.ANY))
     sides = [bool(own), bool(far)]
     outs = [
@@ -193,8 +192,8 @@
     ]
     outs = [o for o, wanted in zip(outs, sides) if wanted]
     return pl.pallas_call(
-        functools.partial(project_kernel, count, *sides, skip),
-        in_specs=[smem] * 2 + [anywhere] * (2 * sum(sides) + count + len(before)),
+        functools.partial(project_kernel, parts, *sides),
+        in_specs=[smem] * 2 + [anywhere] * (2 * sum(sides) + sum(parts) + len(before)),
         out_specs=[o[0] for o in outs],
         out_shape=[o[1] for o in outs],
         scratch_shapes=[
@@ -202,13 +201,13 @@
             pltpu.VMEM((depth, HD * count), bf16),
             pltpu.VMEM((count, rows, HD), bf16),
             pltpu.SemaphoreType.DMA((4,)),
-            pltpu.SemaphoreType.DMA((count,)),
+            pltpu.SemaphoreType.DMA((count, max(parts))),
             pltpu.SemaphoreType.DMA((count,)),
         ],
-        input_output_aliases={2 + 2 * sum(sides) + count: 0} if before else {},
+        input_output_aliases={2 + 2 * sum(sides) + sum(parts): 0} if before else {},
         compiler_params=pltpu.CompilerParams(vmem_limit_bytes=VMEM),
-        cost_estimate=cost(micros),
-    )(first, places, *own, *far, *pieces, *before)
+        cost_estimate=cost(5),
+    )(first, places, *own, *far, *(a for p in pieces for a in p), *before)
 
 
 def beat_kernel(in_ref, out_ref):
@@ -296,17 +295,21 @@
     return pltpu.CompilerParams(dimension_semantics=("arbitrary",), vmem_limit_bytes=VMEM)
 
 
+def pick(ids, i):
+    return ids.at[i].get(mode="promise_in_bounds", wrap_negative_indices=False)
+
+
 class Scan:
     def __init__(self, ids, axis):
         self.ids, self.axis = ids, axis
         self.n, self.me = lax.axis_size(axis), lax.axis_index(axis)
-        self.core = self.me % 2
+        self.core = self.me & 1
         self.first = self.me - self.core
-        self.plane = self.me - self.me % 8
+        self.plane = self.me & ~7
         self.sums = 0.0
 
     def eq(self, i, j):
-        return (self.ids[i] == self.ids[j]).astype(f32)
+        return (pick(self.ids, i) == pick(self.ids, j)).astype(f32)
 
     def chip(self, mine, got):
         self.kv0 = jnp.where(self.core == 0, mine, got)
@@ -318,8 +321,8 @@
         return flip(self.total, self.axis, bit)
 
     def merge(self, bit, got):
-        upper = (self.me // bit) % 2
-        base = self.me - self.me % (2 * bit)
+        upper = lax.shift_right_logical(self.me & bit, bit // 2)
+        base = self.me & ~(2 * bit - 1)
         lower_last, upper_last = base + bit - 1, base + 2 * bit - 1
         link = self.eq(lower_last, upper_last)
         got = got.astype(f32)
@@ -334,7 +337,7 @@
 
     def cut(self):
         part = self.total.shape[0] // 4
-        spot = self.me // 2 % 4
+        spot = lax.shift_right_logical(self.me & 6, 1)
         self.total = lax.dynamic_slice_in_dim(self.total, spot * part, part, 0)
         self.below = 0.0
 
@@ -350,7 +353,7 @@
 
     def gather(self, bit, got):
         below = self.below
-        upper = (self.me // bit) % 2 == 1
+        upper = (self.me & bit) != 0
         self.below = jnp.concatenate(
             [jnp.where(upper, got, below), jnp.where(upper, below, got)], axis=0
         )
@@ -492,7 +495,7 @@
 def by_tree(q, k, v, cq, ck, cv, gain, rim, weight, ids):
     axis = "seq"
     n, me = lax.axis_size(axis), lax.axis_index(axis)
-    core = jnp.reshape(me % 2, (1,)).astype(jnp.int32)
+    core = jnp.reshape(me & 1, (1,)).astype(jnp.int32)
     half = v.shape[1] // (GROUP * HD) // 2
     ties = lax.optimization_barrier
 
@@ -534,8 +537,9 @@
 
     for step in range(scan.climbs()):
         scan.climb(step)
-    scan.below, d0 = ties((scan.below, d0))
-    own3 = over_z(tie(own2, scan.below))
+    mark = beat(tie(core, scan.total))
+    own3 = over_z(tie(own2, mark))
+    scan.below, d0, mark = ties((scan.below, d0, mark))
     hop_x = scan.gather_hop(2)
     hop_x, y1, x1u = ties((hop_x, y1, x1u))
     x1l = over_x(tie(own1l, hop_x))
@@ -549,7 +553,7 @@
     keep, own3 = ties((keep, own3))
     hid_a = hidden_call(core * half, qc, local, keep, gain)
     got, x1l = ties((got, x1l, hid_a))[:2]
-    x1 = jnp.concatenate([x1u, x1l], axis=0)
+    x1 = (x1u, x1l)
     x3, y3 = over_x(tie(own3, got)), over_y(tie(own3, got))
     far_a = share(hid_a)
     hid_b = hidden_call((1 - core) * half, qc, local, got, gain, 0.02)
@@ -557,25 +561,31 @@
     d2 = over_z(d1)
     far_b = share(hid_b)
     where = [
-        (0, 0), (1, 0), (2, 0), (3, 0), (0, 4), (1, 4), (2, 4), (0, 2), (1, 2), (2, 2),
-        (0, 6), (1, 6), (3, 2), (3, 4), (2, 6), (3, 6),
+        (0, 0), (1, 0), (2, 0), (3, 0), (0, 4), (1, 4), (0, 2), (1, 2), (0, 6), (1, 6),
+        (2, 4), (2, 2), (3, 2), (3, 4), (2, 6), (3, 6),
     ]
     order = ring(n // 8)
-    home = jnp.asarray(order, jnp.int32)
-    spot = jnp.asarray([order.index(p) for p in range(n // 8)], jnp.int32)[me // 8]
+    me = tie(me, hid_a)
+    plane = lax.shift_right_logical(me, 3)
+    spot = sum(jnp.where(plane == p, i, 0) for i, p in enumerate(order))
     shift = jnp.asarray([p[0] for p in where], jnp.int32)
     bits = jnp.asarray([p[1] for p in where], jnp.int32)
-    places = (home[(spot - shift) % (n // 8)] * 8 + (me % 8 ^ bits)).astype(jnp.int32)
+    turned = (spot - shift) & (n // 8 - 1)
+    home = sum(jnp.where(turned == i, p, 0) for i, p in enumerate(order))
+    places = (home * 8 + ((me & 7) ^ bits)).astype(jnp.int32)
     mark = beat(tie(places, hid_b))
     far_a, far_b, mark = ties((far_a, far_b, mark))
     own, far = (hid_a, hid_b), (far_a, far_b)
-    pieces = [own0, own1, own2, own3, y0, y1, y2, x0, x1, x2, d0, d1]
-    out, back_a = project(own, far, core, width, pieces, mark[:12])
-    x3, y3, d2, out = ties((x3, y3, d2, out))
-    d3y, d3z = over_y(x3[:mid]), over_z(d2[mid:])
-    d3 = jnp.concatenate([d3y, d3z], axis=0)
-    out, back_c = project(own, far, core, width, [x3, y3, d2, d3], places[12:], (out,))
-    backs = [share(b) for b in (back_a, back_c)]
+    pieces = [own0, own1, own2, own3, y0, y1, x0, x1, d0, d1, y2]
+    out, back_a = project(own, far, core, width, pieces, mark[:11])
+    x3, d2, out = ties((x3, d2, out))
+    d3 = (over_y(x3[:mid]), over_z(d2[mid:]))
+    y3, out = ties((y3, out))
+    pieces = [x2, x3, y3]
+    out, back_b = project(own, far, core, width, pieces, places[11:14], (out,))
+    *d3, out = ties((*d3, out, back_b))[:3]
+    out, back_c = project(own, far, core, width, [d2, tuple(d3)], places[14:], (out,))
+    backs = [share(b) for b in (back_a, back_b, back_c)]
     return place(backs, places ^ 1, out)
 
 
@@ -593,17 +603,19 @@
     width = values.shape[1]
     heads = -(-width // (HD * GROUP)) * GROUP
     me = lax.axis_index("seq")
-    start = jnp.logical_or(me == 0, stream_ids[me] != stream_ids[jnp.maximum(me - 1, 0)])
+    start = jnp.logical_or(me == 0, pick(stream_ids, me) != pick(stream_ids, jnp.maximum(me - 1, 0)))
     keep = 1.0 - start.astype(f32)
     q, k = padded(query_feat, heads * FEAT), padded(key_feat, heads * FEAT)
     v = padded(values, heads * HD)
     cq, ck = padded(conv_query, heads * FEAT), padded(conv_key, heads * FEAT)
     cv = padded(conv_value, heads * HD)
     gain = padded(norm_gain[None], heads * HD)
-    rim = after(jnp.concatenate([v[-2:], q[-2:], k[-2:]], axis=1), "seq", 1).astype(f32) * keep
+    last = jnp.concatenate([v[-2:], q[-2:], k[-2:]], axis=1)
+    rim = after(last, "seq", 1).astype(f32) * keep
     n, cut = lax.axis_size("seq"), lax.axis_size("head")
     if n == 32 and cut == 1 and out_weight.shape[1] == HD and heads % (2 * GROUP) == 0:
-        return by_tree(q, k, v, cq, ck, cv, gain, rim, out_weight, stream_ids)
+        weight = tie(out_weight, last)
+        return by_tree(q, k, v, cq, ck, cv, gain, rim, weight, stream_ids)
     terms = by_gather(q, k, v, cq, ck, cv, gain, rim, out_weight, stream_ids, width)
     return lax.psum_scatter(terms, "head", scatter_dimension=1, tiled=True)
 

time: 193 us -> 189 us (0.979)
  Pallas kernels: 79.9 us -> 88.4 us
  starting transfers between devices: 41 us -> 34 us
  other arithmetic: 10.5 us -> 6 us
    ppermute x6, starting transfers between devices: 12.9 us -> 4.35 us  [turn(): return lax.ppermute(x, axis, route)]
    pallas_call x2 -> x3, Pallas kernels: 35.6 us -> 44.1 us  [project(): pl.pallas_call(functools.partial(project_kernel, parts, *sides), in_specs...]
    ppermute x6, waiting for transfers between devices: 11.6 us -> 3.48 us  [turn(): return lax.ppermute(x, axis, route)]
    ppermute x2, waiting for transfers between devices: 1.83 us -> 7.24 us  [rotate(): return lax.ppermute(x, axis, [(i, (i + distance) % n) for i in range(n)])]
    ppermute x21 -> x22, starting transfers between devices: 19.7 us -> 24.7 us  [flip(): lax.ppermute(x, axis, [(i, i ^ bit) for i in range(lax.axis_size(axis))])]
    ppermute x2, starting transfers between devices: 4.69 us -> 1.3 us  [rotate(): return lax.ppermute(x, axis, [(i, (i + distance) % n) for i in range(n)])]
    concatenate x3 -> x1, other arithmetic: 3.15 us -> 0.02 us  [on_device(): last = jnp.concatenate([v[-2:], q[-2:], k[-2:]], axis=1)]
    ppermute x21 -> x22, waiting for transfers between devices: 20.9 us -> 23.1 us  [flip(): lax.ppermute(x, axis, [(i, i ^ bit) for i in range(lax.axis_size(axis))])]
  transfers between devices with their start and end apart: 30 -> 31, of which waited for: 9 -> 12; matrix products, arithmetic and copies ran while one was open for 8% -> 6% of each run, Pallas kernels for 41% -> 46%
where the time goes in v4:
time: 189 us; the launch traced here: 186 us
  Pallas kernels  88.4 us (47%)
  starting transfers between devices  34 us (18%)
  waiting for transfers between devices  33.8 us (18%)
  local copies, waits for them, and re-layouts  11.9 us (6%)
  between operations  11.9 us (6%)
  other arithmetic  6 us (3%)
    pallas_call x3, Pallas kernels, project(): pl.pallas_call(functools.partial(project_kernel, parts, *sides), in_specs...  44.1 us
    ppermute x22, starting transfers between devices, flip(): lax.ppermute(x, axis, [(i, i ^ bit) for i in range(lax.axis_size(axis))])  24.7 us
    ppermute x22, waiting for transfers between devices, flip(): lax.ppermute(x, axis, [(i, i ^ bit) for i in range(lax.axis_size(axis))])  23.1 us
    pallas_call x2, Pallas kernels, hidden_call(): pl.pallas_call(hidden_kernel, grid_spec=pltpu.PrefetchScalarGridSpec(num_...  15.2 us
    pallas_call x2, Pallas kernels, local_call(): pl.pallas_call(local_kernel, grid=(groups,), in_specs=[cols(rows, fw, sta...  13.4 us
    pallas_call x2, Pallas kernels, state_call(): pl.pallas_call(state_kernel, grid_spec=pltpu.PrefetchScalarGridSpec(num_s...  11.5 us
    ppermute x2, waiting for transfers between devices, rotate(): return lax.ppermute(x, axis, [(i, (i + distance) % n) for i in range(n)])  7.24 us
    unnamed x34, local copies, waits for them, and re-layouts  4.4 us
  transfers between devices with their start and end apart: 31, of which 12 were waited for; matrix products, arithmetic and copies ran while one was open for 6% of the time, Pallas kernels for 46%

profile of v4, /device:TPU:11, one launch (start us, length us, event | category | flops | bytes accessed | tf_op | source)
XLA Modules:
  0.0 186.0 jit_solution(11454548220681083209)
XLA Ops:
  2.3 3.7 %collective-permute-start = (bf16[2,5120]{1,0:T(2,128)(2,1)S(1)}, bf16[2,5120]{1,0:T(2,128)(2,1)S(1)}, u32[]{:S(2)}, u32[]{:S(2)}) collective-permute-start(bf16[2,5120]{1,0:T(2,128)(2,1)S(1)} %pad_maximum_fusion.1), channel_id=1, source_target_pairs={{0,1},{1,2},{2,3},{3,4},{4,5},{5,6},{6,7},{7,8},{8,9},{9,10},{10,1... | collective-permute-start | bytes 61448 | tf_op jit(solution)/shard_map/ppermute | solution.py:278
  6.0 2.4 %collective-permute-start.5 = (bf16[4096,128]{1,0:T(8,128)(2,1)}, bf16[4096,128]{1,0:T(8,128)(2,1)}, u32[]{:S(2)}, u32[]{:S(2)}) collective-permute-start(bf16[4096,128]{1,0:T(8,128)(2,1)} %refs_4_), channel_id=1, source_target_pairs={{0,8},{1,9},{2,10},{3,11},{4,12},{5,13},{6,14},{7,15},{8,24},{9,25... | collective-permute-start | bytes 3145736 | tf_op jit(solution)/shard_map/ppermute | solution.py:269
  8.3 1.5 collective-permute-start.3
  9.8 1.8 fusion.19
  19.9 5.7 %shard_map.109 = (bf16[512,512]{1,0:T(8,128)(2,1)}, bf16[512,4096]{1,0:T(8,128)(2,1)}, bf16[16,160,128]{2,1,0:T(8,128)(2,1)}) custom-call(s32[1]{0:T(128)S(6)} %mul.98.start_ref, bf16[512,512]{1,0:T(8,128)(2,1)} %k_ref.3, bf16[512,4096]{1,0:T(8,128)(2,1)} %v_ref.3, f32[2,5120]{1,0:T(2,128)} %convert_multiply_fusion.3.rk_ref.rv_ref.rq_ref, ...), custom_call_target="tpu_custom_call" | custom-call | flops 120000004096 | bytes 1048576 | tf_op jit(solution)/shard_map/pallas_call | solution.py:380
  25.7 5.8 %shard_map.110 = (bf16[512,512]{1,0:T(8,128)(2,1)}, bf16[512,4096]{1,0:T(8,128)(2,1)}, bf16[16,160,128]{2,1,0:T(8,128)(2,1)}) custom-call(s32[1]{0:T(128)S(6)} %mul.96.start_ref, bf16[512,512]{1,0:T(8,128)(2,1)} %k_ref.3, bf16[512,4096]{1,0:T(8,128)(2,1)} %v_ref.3, ...), custom_call_target="tpu_custom_call", output_to_operand_aliasing={{0}: (7, {}), {1}: (8, {})} | custom-call | flops 120000004096 | bytes 1048576 | tf_op jit(solution)/shard_map/pallas_call | solution.py:380
  31.5 1.6 fusion.1
  34.1 6.7 %shard_map.111 = (bf16[512,512]{1,0:T(8,128)(2,1)}, f32[512,4096]{1,0:T(8,128)}) custom-call(bf16[512,512]{1,0:T(8,128)(2,1)} %q_ref.1, f32[2,5120]{1,0:T(2,128)} %convert_multiply_fusion.3.rk_ref.rv_ref.rq_ref, f32[3,512]{1,0:T(4,128)} %cq_ref.3, bf16[512,512]{1,0:T(8,128)(2,1)} %get-tuple-element.74.kc_ref, bf16[512,4096]{1,0:T(8,128)(2,1)} %get-tuple-element.75.vc_ref), custom_call_target="tpu_custom_call" | custom-call | flops 120000004096 | bytes 1048576 | tf_op jit(solution)/shard_map/pallas_call | solution.py:419
  41.6 2.2 %fusion.18 = (bf16[2048,128]{1,0:T(8,128)(2,1)}, bf16[2048,128]{1,0:T(8,128)(2,1)}) fusion(bf16[4096,128]{1,0:T(8,128)(2,1)} %collective-permute-done.5.refs_5_), kind=kLoop, calls=%fused_computation.36 | loop fusion | bytes 2097152 | tf_op jit(solution)/shard_map/slice | solution.py:528
  43.9 5.3 %collective-permute-done.2 = bf16[16,160,128]{2,1,0:T(8,128)(2,1)S(1)} collective-permute-done((bf16[16,160,128]{2,1,0:T(8,128)(2,1)S(1)}, bf16[16,160,128]{2,1,0:T(8,128)(2,1)S(1)}, u32[]{:S(2)}, u32[]{:S(2)}) %collective-permute-start.2) | collective-permute-done | bytes 655392 | tf_op jit(solution)/shard_map/ppermute | solution.py:273
  49.7 6.7 %shard_map.112 = (bf16[512,512]{1,0:T(8,128)(2,1)}, f32[512,4096]{1,0:T(8,128)}) custom-call(bf16[512,512]{1,0:T(8,128)(2,1)} %q_ref.1, f32[2,5120]{1,0:T(2,128)} %convert_multiply_fusion.3.rk_ref.rv_ref.rq_ref, f32[3,512]{1,0:T(4,128)} %cq_ref.3, bf16[512,512]{1,0:T(8,128)(2,1)} %get-tuple-element.74.kc_ref, ...), custom_call_target="tpu_custom_call", output_to_operand_aliasing={{0}: (5, {}), {1}: (6, {})} | custom-call | flops 120000004096 | bytes 1048576 | tf_op jit(solution)/shard_map/pallas_call | solution.py:419
  57.6 1.4 collective-permute-start.12
  59.0 4.8 %collective-permute-done.6 = bf16[16,160,128]{2,1,0:T(8,128)(2,1)S(1)} collective-permute-done((bf16[16,160,128]{2,1,0:T(8,128)(2,1)S(1)}, bf16[16,160,128]{2,1,0:T(8,128)(2,1)S(1)}, u32[]{:S(2)}, u32[]{:S(2)}) %collective-permute-start.6) | collective-permute-done | bytes 655392 | tf_op jit(solution)/shard_map/ppermute | solution.py:273
  63.8 1.6 collective-permute-done.7.refs_6_
  67.0 3.9 %collective-permute-done.9 = bf16[4,160,128]{2,1,0:T(8,128)(2,1)S(1)} collective-permute-done((bf16[4,160,128]{2,1,0:T(8,128)(2,1)S(1)}, bf16[4,160,128]{2,1,0:T(8,128)(2,1)S(1)}, u32[]{:S(2)}, u32[]{:S(2)}) %collective-permute-start.9) | collective-permute-done | bytes 163872 | tf_op jit(solution)/shard_map/ppermute | solution.py:283
  70.9 3.3 %collective-permute-done.8 = bf16[4,160,128]{2,1,0:T(8,128)(2,1)S(1)} collective-permute-done((bf16[4,160,128]{2,1,0:T(8,128)(2,1)S(1)}, bf16[4,160,128]{2,1,0:T(8,128)(2,1)S(1)}, u32[]{:S(2)}, u32[]{:S(2)}) %collective-permute-start.8) | collective-permute-done | bytes 163872 | tf_op jit(solution)/shard_map/ppermute | solution.py:283
  75.9 7.0 %collective-permute-done.13.refs_11_ = bf16[2048,128]{1,0:T(8,128)(2,1)} collective-permute-done((bf16[2048,128]{1,0:T(8,128)(2,1)}, bf16[2048,128]{1,0:T(8,128)(2,1)}, u32[]{:S(2)}, u32[]{:S(2)}) %collective-permute-start.13) | collective-permute-done | bytes 524320 | tf_op jit(solution)/shard_map/ppermute | solution.py:273
  82.9 3.4 %collective-permute-done.12.refs_9_ = bf16[4096,128]{1,0:T(8,128)(2,1)} collective-permute-done((bf16[4096,128]{1,0:T(8,128)(2,1)}, bf16[4096,128]{1,0:T(8,128)(2,1)}, u32[]{:S(2)}, u32[]{:S(2)}) %collective-permute-start.12) | collective-permute-done | bytes 1048608 | tf_op jit(solution)/shard_map/ppermute | solution.py:273
  90.5 2.1 %collective-permute-start.18 = (bf16[2048,128]{1,0:T(8,128)(2,1)}, bf16[2048,128]{1,0:T(8,128)(2,1)}, u32[]{:S(2)}, u32[]{:S(2)}) collective-permute-start(bf16[2048,128]{1,0:T(8,128)(2,1)} %get-tuple-element.96), channel_id=1, source_target_pairs={{0,2},{1,3},{2,0},{3,1},{4,6},{5,7},{6,4},{7,5},{8,10},{9,11},{10,... | collective-permute-start | bytes 1572872 | tf_op jit(solution)/shard_map/ppermute | solution.py:273
  94.1 1.6 fusion.6
  95.7 3.8 %collective-permute-start.17 = (bf16[16,160,128]{2,1,0:T(8,128)(2,1)S(1)}, bf16[16,160,128]{2,1,0:T(8,128)(2,1)S(1)}, u32[]{:S(2)}, u32[]{:S(2)}) collective-permute-start(bf16[16,160,128]{2,1,0:T(8,128)(2,1)S(1)} %get-tuple-element.131), channel_id=1, source_target_pairs={{0,1},{1,0},{2,3},{3,2},{4,5},{5,4},{6,7},{7,6},{8,9},{9,8},{10,11... | collective-permute-start | bytes 1966088 | tf_op jit(solution)/shard_map/ppermute | solution.py:273
  99.6 1.8 collective-permute-done.15.refs_7_
  102.0 7.6 %shard_map.113.refs_0_ = bf16[512,2048]{1,0:T(8,128)(2,1)} custom-call(s32[1]{0:T(128)S(6)} %mul.96.start_ref, bf16[512,512]{1,0:T(8,128)(2,1)} %get-tuple-element.81.qc_ref, f32[512,4096]{1,0:T(8,128)} %get-tuple-element.82.loc_ref, bf16[16,160,128]{2,1,0:T(8,128)(2,1)} %get-tuple-element.93.s_ref, f32[1,4096]{1,0:T(1,128)} %bitcast.12), custom_call_target="tpu_custom_call" | custom-call | flops 99999997952 | bytes 1048576 | tf_op jit(solution)/shard_map/pallas_call | solution.py:449
  111.4 4.4 %collective-permute-start.16 = (bf16[512,2048]{1,0:T(8,128)(2,1)}, bf16[512,2048]{1,0:T(8,128)(2,1)}, u32[]{:S(2)}, u32[]{:S(2)}) collective-permute-start(bf16[512,2048]{1,0:T(8,128)(2,1)} %shard_map.113.refs_0_), channel_id=1, source_target_pairs={{0,1},{1,0},{2,3},{3,2},{4,5},{5,4},{6,7},{7,6},{8,9},{9,8},{10,11... | collective-permute-start | bytes 6291464 | tf_op jit(solution)/shard_map/ppermute | solution.py:273
  116.6 7.6 %shard_map.114.refs_1_ = bf16[512,2048]{1,0:T(8,128)(2,1)} custom-call(s32[1]{0:T(128)S(6)} %mul.98.start_ref, bf16[512,512]{1,0:T(8,128)(2,1)} %get-tuple-element.81.qc_ref, f32[512,4096]{1,0:T(8,128)} %get-tuple-element.82.loc_ref, bf16[16,160,128]{2,1,0:T(8,128)(2,1)} %copy-done.3, f32[1,4096]{1,0:T(1,128)} %bitcast.13), custom_call_target="tpu_custom_call" | custom-call | flops 400000000 | bytes 1048576 | tf_op jit(solution)/shard_map/pallas_call | solution.py:449
  126.4 1.5 collective-permute-start.24
  130.0 22.9 %shard_map.116 = (bf16[512,4096]{1,0:T(8,128)(2,1)}, bf16[11,512,128]{2,1,0:T(8,128)(2,1)}) custom-call(s32[1]{0:T(128)} %bitcast.first_ref, s32[11]{0:T(128)} %bitcast.14, bf16[512,2048]{1,0:T(8,128)(2,1)} %shard_map.113.refs_0_, bf16[512,2048]{1,0:T(8,128)(2,1)} %shard_map.114.refs_1_, bf16[512,2048]{1,0:T(8,128)(2,1)} %collective-permute-done.16.refs_2_, ...), custom_call_target="tpu_custom_call" | custom-call | flops 99999997952 | bytes 1048576 | tf_op jit(solution)/shard_map/pallas_call | solution.py:194
  154.6 12.2 %shard_map.117 = (bf16[512,4096]{1,0:T(8,128)(2,1)}, bf16[3,512,128]{2,1,0:T(8,128)(2,1)}) custom-call(s32[1]{0:T(128)} %bitcast.first_ref, s32[3]{0:T(128)} %slice.36.place_ref, bf16[512,2048]{1,0:T(8,128)(2,1)} %shard_map.113.refs_0_, bf16[512,2048]{1,0:T(8,128)(2,1)} %shard_map.114.refs_1_, ...), custom_call_target="tpu_custom_call", output_to_operand_aliasing={{0}: (9, {})} | custom-call | flops 99999997952 | bytes 1048576 | tf_op jit(solution)/shard_map/pallas_call | solution.py:194
  166.8 3.0 %collective-permute-start.27 = (bf16[3,512,128]{2,1,0:T(8,128)(2,1)}, bf16[3,512,128]{2,1,0:T(8,128)(2,1)S(1)}, u32[]{:S(2)}, u32[]{:S(2)}) collective-permute-start(bf16[3,512,128]{2,1,0:T(8,128)(2,1)} %get-tuple-element.121), channel_id=1, source_target_pairs={{0,1},{1,0},{2,3},{3,2},{4,5},{5,4},{6,7},{7,6},{8,9},{9,8},{10,11... | collective-permute-start | bytes 1179656 | tf_op jit(solution)/shard_map/ppermute | solution.py:273
  170.8 9.0 %shard_map.118 = (bf16[512,4096]{1,0:T(8,128)(2,1)}, bf16[2,512,128]{2,1,0:T(8,128)(2,1)}) custom-call(s32[1]{0:T(128)} %bitcast.first_ref, s32[2]{0:T(128)} %slice.37.place_ref, bf16[512,2048]{1,0:T(8,128)(2,1)} %shard_map.113.refs_0_, bf16[512,2048]{1,0:T(8,128)(2,1)} %shard_map.114.refs_1_, ...), custom_call_target="tpu_custom_call", output_to_operand_aliasing={{0}: (9, {})} | custom-call | flops 99999997952 | bytes 1048576 | tf_op jit(solution)/shard_map/pallas_call | solution.py:194
  180.3 1.4 collective-permute-done.30.refs_2_
  182.9 3.0 %shard_map.119 = bf16[512,4096]{1,0:T(8,128)(2,1)} custom-call(s32[16]{0:T(128)} %get-tuple-element.129.place_ref, bf16[11,512,128]{2,1,0:T(8,128)(2,1)} %copy-done.11, bf16[3,512,128]{2,1,0:T(8,128)(2,1)} %copy-done.15, bf16[2,512,128]{2,1,0:T(8,128)(2,1)} %copy-done.16, bf16[512,4096]{1,0:T(8,128)(2,1)} %get-tuple-element.128.refs_3_), custom_call_target="tpu_custom_call", output_to_operand_aliasing={{}: (4, {})} | custom-call | flops 60000002048 | bytes 1048576 | tf_op jit(solution)/shard_map/pallas_call | solution.py:246
  (96 shorter events, 23.5 us)
Async XLA Ops:
  2.3 17.0 %collective-permute-start = (bf16[2,5120]{1,0:T(2,128)(2,1)S(1)}, bf16[2,5120]{1,0:T(2,128)(2,1)S(1)}, u32[]{:S(2)}, u32[]{:S(2)}) collective-permute-start(bf16[2,5120]{1,0:T(2,128)(2,1)S(1)} %pad_maximum_fusion.1), channel_id=1, source_target_pairs={{0,1},{1,2},{2,3},{3,4},{4,5},{5,6},{6,7},{7,8},{8,9},{9,10},{10,1... | collective-permute-start | bytes 61448 | tf_op jit(solution)/shard_map/ppermute | solution.py:278
  6.0 34.9 %collective-permute-start.5 = (bf16[4096,128]{1,0:T(8,128)(2,1)}, bf16[4096,128]{1,0:T(8,128)(2,1)}, u32[]{:S(2)}, u32[]{:S(2)}) collective-permute-start(bf16[4096,128]{1,0:T(8,128)(2,1)} %refs_4_), channel_id=1, source_target_pairs={{0,8},{1,9},{2,10},{3,11},{4,12},{5,13},{6,14},{7,15},{8,24},{9,25... | collective-permute-start | bytes 3145736 | tf_op jit(solution)/shard_map/ppermute | solution.py:269
  8.3 32.5 %collective-permute-start.4 = (bf16[4096,128]{1,0:T(8,128)(2,1)}, bf16[4096,128]{1,0:T(8,128)(2,1)}, u32[]{:S(2)}, u32[]{:S(2)}) collective-permute-start(bf16[4096,128]{1,0:T(8,128)(2,1)} %refs_4_), channel_id=1, source_target_pairs={{0,4},{1,5},{2,6},{3,7},{4,0},{5,1},{6,2},{7,3},{8,12},{9,13},{10,... | collective-permute-start | bytes 3145736 | tf_op jit(solution)/shard_map/ppermute | solution.py:273
  8.3 35.5 %collective-permute-start.3 = (bf16[4096,128]{1,0:T(8,128)(2,1)}, bf16[4096,128]{1,0:T(8,128)(2,1)}, u32[]{:S(2)}, u32[]{:S(2)}) collective-permute-start(bf16[4096,128]{1,0:T(8,128)(2,1)} %refs_4_), channel_id=1, source_target_pairs={{0,2},{1,3},{2,0},{3,1},{4,6},{5,7},{6,4},{7,5},{8,10},{9,11},{10,... | collective-permute-start | bytes 3145736 | tf_op jit(solution)/shard_map/ppermute | solution.py:273
  25.7 5.8 %collective-permute-start.1 = (bf16[16,160,128]{2,1,0:T(8,128)(2,1)}, bf16[16,160,128]{2,1,0:T(8,128)(2,1)S(1)}, u32[]{:S(2)}, u32[]{:S(2)}) collective-permute-start(bf16[16,160,128]{2,1,0:T(8,128)(2,1)} %get-tuple-element.67), channel_id=1, source_target_pairs={{0,1},{1,0},{2,3},{3,2},{4,5},{5,4},{6,7},{7,6},{8,9},{9,8},{10,11... | collective-permute-start | bytes 1966088 | tf_op jit(solution)/shard_map/ppermute | solution.py:273
  33.1 16.1 %collective-permute-start.2 = (bf16[16,160,128]{2,1,0:T(8,128)(2,1)S(1)}, bf16[16,160,128]{2,1,0:T(8,128)(2,1)S(1)}, u32[]{:S(2)}, u32[]{:S(2)}) collective-permute-start(bf16[16,160,128]{2,1,0:T(8,128)(2,1)S(1)} %fusion.1), channel_id=1, source_target_pairs={{0,2},{1,3},{2,0},{3,1},{4,6},{5,7},{6,4},{7,5},{8,10},{9,11},{10,... | collective-permute-start | bytes 1966088 | tf_op jit(solution)/shard_map/ppermute | solution.py:273
  40.9 33.4 %collective-permute-start.10 = (bf16[4096,128]{1,0:T(8,128)(2,1)}, bf16[4096,128]{1,0:T(8,128)(2,1)}, u32[]{:S(2)}, u32[]{:S(2)}) collective-permute-start(bf16[4096,128]{1,0:T(8,128)(2,1)} %collective-permute-done.4.refs_8_), channel_id=1, source_target_pairs={{0,2},{1,3},{2,0},{3,1},{4,6},{5,7},{6,4},{7,5},{8,10},{9,11},{10,... | collective-permute-start | bytes 3145736 | tf_op jit(solution)/shard_map/ppermute | solution.py:273
  41.5 24.0 %collective-permute-start.7 = (bf16[4096,128]{1,0:T(8,128)(2,1)}, bf16[4096,128]{1,0:T(8,128)(2,1)}, u32[]{:S(2)}, u32[]{:S(2)}) collective-permute-start(bf16[4096,128]{1,0:T(8,128)(2,1)} %collective-permute-done.5.refs_5_), channel_id=1, source_target_pairs={{0,8},{1,9},{2,10},{3,11},{4,12},{5,13},{6,14},{7,15},{8,24},{9,25... | collective-permute-start | bytes 3145736 | tf_op jit(solution)/shard_map/ppermute | solution.py:269
  49.5 14.4 %collective-permute-start.6 = (bf16[16,160,128]{2,1,0:T(8,128)(2,1)S(1)}, bf16[16,160,128]{2,1,0:T(8,128)(2,1)S(1)}, u32[]{:S(2)}, u32[]{:S(2)}) collective-permute-start(bf16[16,160,128]{2,1,0:T(8,128)(2,1)S(1)} %fusion.8), channel_id=1, source_target_pairs={{0,4},{1,5},{2,6},{3,7},{4,0},{5,1},{6,2},{7,3},{8,12},{9,13},{10,... | collective-permute-start | bytes 1966088 | tf_op jit(solution)/shard_map/ppermute | solution.py:273
  56.4 26.5 %collective-permute-start.13 = (bf16[2048,128]{1,0:T(8,128)(2,1)}, bf16[2048,128]{1,0:T(8,128)(2,1)}, u32[]{:S(2)}, u32[]{:S(2)}) collective-permute-start(bf16[2048,128]{1,0:T(8,128)(2,1)} %get-tuple-element.89), channel_id=1, source_target_pairs={{0,2},{1,3},{2,0},{3,1},{4,6},{5,7},{6,4},{7,5},{8,10},{9,11},{10,... | collective-permute-start | bytes 1572872 | tf_op jit(solution)/shard_map/ppermute | solution.py:273
  57.6 28.7 %collective-permute-start.12 = (bf16[4096,128]{1,0:T(8,128)(2,1)}, bf16[4096,128]{1,0:T(8,128)(2,1)}, u32[]{:S(2)}, u32[]{:S(2)}) collective-permute-start(bf16[4096,128]{1,0:T(8,128)(2,1)} %collective-permute-done.5.refs_5_), channel_id=1, source_target_pairs={{0,4},{1,5},{2,6},{3,7},{4,0},{5,1},{6,2},{7,3},{8,12},{9,13},{10,... | collective-permute-start | bytes 3145736 | tf_op jit(solution)/shard_map/ppermute | solution.py:273
  65.7 5.2 %collective-permute-start.9 = (bf16[4,160,128]{2,1,0:T(8,128)(2,1)S(1)}, bf16[4,160,128]{2,1,0:T(8,128)(2,1)S(1)}, u32[]{:S(2)}, u32[]{:S(2)}) collective-permute-start(bf16[4,160,128]{2,1,0:T(8,128)(2,1)S(1)} %fusion.12), channel_id=1, source_target_pairs={{0,16},{1,17},{2,18},{3,19},{4,20},{5,21},{6,22},{7,23},{8,24},{9,... | collective-permute-start | bytes 491528 | tf_op jit(solution)/shard_map/ppermute | solution.py:283
  66.8 7.4 %collective-permute-start.8 = (bf16[4,160,128]{2,1,0:T(8,128)(2,1)S(1)}, bf16[4,160,128]{2,1,0:T(8,128)(2,1)S(1)}, u32[]{:S(2)}, u32[]{:S(2)}) collective-permute-start(bf16[4,160,128]{2,1,0:T(8,128)(2,1)S(1)} %fusion.12), channel_id=1, source_target_pairs={{0,8},{1,9},{2,10},{3,11},{4,12},{5,13},{6,14},{7,15},{8,16},{9,17... | collective-permute-start | bytes 491528 | tf_op jit(solution)/shard_map/ppermute | solution.py:283
  74.3 12.1 %collective-permute-start.11 = (bf16[4,160,128]{2,1,0:T(8,128)(2,1)S(1)}, bf16[4,160,128]{2,1,0:T(8,128)(2,1)S(1)}, u32[]{:S(2)}, u32[]{:S(2)}) collective-permute-start(bf16[4,160,128]{2,1,0:T(8,128)(2,1)S(1)} %multiply_add_fusion), channel_id=1, source_target_pairs={{0,2},{1,3},{2,0},{3,1},{4,6},{5,7},{6,4},{7,5},{8,10},{9,11},{10,... | collective-permute-start | bytes 491528 | tf_op jit(solution)/shard_map/ppermute | solution.py:273
  75.6 18.5 %copy-start.2 = (bf16[16,160,128]{2,1,0:T(8,128)(2,1)S(1)}, bf16[16,160,128]{2,1,0:T(8,128)(2,1)}, u32[]{:S(2)}) copy-start(bf16[16,160,128]{2,1,0:T(8,128)(2,1)} %get-tuple-element.70) | copy-start | bytes 1966084
  75.6 25.9 %collective-permute-start.15 = (bf16[4096,128]{1,0:T(8,128)(2,1)}, bf16[4096,128]{1,0:T(8,128)(2,1)}, u32[]{:S(2)}, u32[]{:S(2)}) collective-permute-start(bf16[4096,128]{1,0:T(8,128)(2,1)} %collective-permute-done.7.refs_6_), channel_id=1, source_target_pairs={{0,8},{1,9},{2,10},{3,11},{4,12},{5,13},{6,14},{7,15},{8,24},{9,25... | collective-permute-start | bytes 3145736 | tf_op jit(solution)/shard_map/ppermute | solution.py:269
  86.5 6.5 %collective-permute-start.14 = (bf16[8,160,128]{2,1,0:T(8,128)(2,1)S(1)}, bf16[8,160,128]{2,1,0:T(8,128)(2,1)}, u32[]{:S(2)}, u32[]{:S(2)}) collective-permute-start(bf16[8,160,128]{2,1,0:T(8,128)(2,1)S(1)} %pad_maximum_fusion), channel_id=1, source_target_pairs={{0,4},{1,5},{2,6},{3,7},{4,0},{5,1},{6,2},{7,3},{8,12},{9,13},{10,... | collective-permute-start | bytes 983048 | tf_op jit(solution)/shard_map/ppermute | solution.py:273
  90.5 20.9 %collective-permute-start.18 = (bf16[2048,128]{1,0:T(8,128)(2,1)}, bf16[2048,128]{1,0:T(8,128)(2,1)}, u32[]{:S(2)}, u32[]{:S(2)}) collective-permute-start(bf16[2048,128]{1,0:T(8,128)(2,1)} %get-tuple-element.96), channel_id=1, source_target_pairs={{0,2},{1,3},{2,0},{3,1},{4,6},{5,7},{6,4},{7,5},{8,10},{9,11},{10,... | collective-permute-start | bytes 1572872 | tf_op jit(solution)/shard_map/ppermute | solution.py:273
  92.6 32.9 %collective-permute-start.22 = (bf16[4096,128]{1,0:T(8,128)(2,1)}, bf16[4096,128]{1,0:T(8,128)(2,1)}, u32[]{:S(2)}, u32[]{:S(2)}) collective-permute-start(bf16[4096,128]{1,0:T(8,128)(2,1)} %collective-permute-done.7.refs_6_), channel_id=1, source_target_pairs={{0,2},{1,3},{2,0},{3,1},{4,6},{5,7},{6,4},{7,5},{8,10},{9,11},{10,... | collective-permute-start | bytes 3145736 | tf_op jit(solution)/shard_map/ppermute | solution.py:273
  95.7 20.1 %collective-permute-start.17 = (bf16[16,160,128]{2,1,0:T(8,128)(2,1)S(1)}, bf16[16,160,128]{2,1,0:T(8,128)(2,1)S(1)}, u32[]{:S(2)}, u32[]{:S(2)}) collective-permute-start(bf16[16,160,128]{2,1,0:T(8,128)(2,1)S(1)} %get-tuple-element.131), channel_id=1, source_target_pairs={{0,1},{1,0},{2,3},{3,2},{4,5},{5,4},{6,7},{7,6},{8,9},{9,8},{10,11... | collective-permute-start | bytes 1966088 | tf_op jit(solution)/shard_map/ppermute | solution.py:273
  99.4 27.0 %collective-permute-start.21 = (bf16[4096,128]{1,0:T(8,128)(2,1)}, bf16[4096,128]{1,0:T(8,128)(2,1)}, u32[]{:S(2)}, u32[]{:S(2)}) collective-permute-start(bf16[4096,128]{1,0:T(8,128)(2,1)} %collective-permute-done.10.refs_13_), channel_id=1, source_target_pairs={{0,8},{1,9},{2,10},{3,11},{4,12},{5,13},{6,14},{7,15},{8,24},{9,25... | collective-permute-start | bytes 3145736 | tf_op jit(solution)/shard_map/ppermute | solution.py:269
  101.4 26.5 %collective-permute-start.20 = (bf16[4096,128]{1,0:T(8,128)(2,1)}, bf16[4096,128]{1,0:T(8,128)(2,1)}, u32[]{:S(2)}, u32[]{:S(2)}) collective-permute-start(bf16[4096,128]{1,0:T(8,128)(2,1)} %collective-permute-done.7.refs_6_), channel_id=1, source_target_pairs={{0,4},{1,5},{2,6},{3,7},{4,0},{5,1},{6,2},{7,3},{8,12},{9,13},{10,... | collective-permute-start | bytes 3145736 | tf_op jit(solution)/shard_map/ppermute | solution.py:273
  111.4 16.5 %collective-permute-start.16 = (bf16[512,2048]{1,0:T(8,128)(2,1)}, bf16[512,2048]{1,0:T(8,128)(2,1)}, u32[]{:S(2)}, u32[]{:S(2)}) collective-permute-start(bf16[512,2048]{1,0:T(8,128)(2,1)} %shard_map.113.refs_0_), channel_id=1, source_target_pairs={{0,1},{1,0},{2,3},{3,2},{4,5},{5,4},{6,7},{7,6},{8,9},{9,8},{10,11... | collective-permute-start | bytes 6291464 | tf_op jit(solution)/shard_map/ppermute | solution.py:273
  124.2 4.4 %collective-permute-start.19 = (bf16[512,2048]{1,0:T(8,128)(2,1)}, bf16[512,2048]{1,0:T(8,128)(2,1)S(1)}, u32[]{:S(2)}, u32[]{:S(2)}) collective-permute-start(bf16[512,2048]{1,0:T(8,128)(2,1)} %shard_map.114.refs_1_), channel_id=1, source_target_pairs={{0,1},{1,0},{2,3},{3,2},{4,5},{5,4},{6,7},{7,6},{8,9},{9,8},{10,11... | collective-permute-start | bytes 6291464 | tf_op jit(solution)/shard_map/ppermute | solution.py:273
  125.5 27.5 %collective-permute-start.26 = (bf16[4096,128]{1,0:T(8,128)(2,1)}, bf16[4096,128]{1,0:T(8,128)(2,1)S(1)}, u32[]{:S(2)}, u32[]{:S(2)}) collective-permute-start(bf16[4096,128]{1,0:T(8,128)(2,1)} %collective-permute-done.15.refs_7_), channel_id=1, source_target_pairs={{0,4},{1,5},{2,6},{3,7},{4,0},{5,1},{6,2},{7,3},{8,12},{9,13},{10,... | collective-permute-start | bytes 3145736 | tf_op jit(solution)/shard_map/ppermute | solution.py:273
  126.4 26.5 %collective-permute-start.24 = (bf16[4096,128]{1,0:T(8,128)(2,1)}, bf16[4096,128]{1,0:T(8,128)(2,1)S(1)}, u32[]{:S(2)}, u32[]{:S(2)}) collective-permute-start(bf16[4096,128]{1,0:T(8,128)(2,1)} %collective-permute-done.15.refs_7_), channel_id=1, source_target_pairs={{0,2},{1,3},{2,0},{3,1},{4,6},{5,7},{6,4},{7,5},{8,10},{9,11},{10,... | collective-permute-start | bytes 3145736 | tf_op jit(solution)/shard_map/ppermute | solution.py:273
  127.9 25.0 %collective-permute-start.25 = (bf16[4096,128]{1,0:T(8,128)(2,1)}, bf16[4096,128]{1,0:T(8,128)(2,1)S(1)}, u32[]{:S(2)}, u32[]{:S(2)}) collective-permute-start(bf16[4096,128]{1,0:T(8,128)(2,1)} %collective-permute-done.21.refs_14_), channel_id=1, source_target_pairs={{0,8},{1,9},{2,10},{3,11},{4,12},{5,13},{6,14},{7,15},{8,24},{9,25... | collective-permute-start | bytes 3145736 | tf_op jit(solution)/shard_map/ppermute | solution.py:269
  153.0 16.8 %collective-permute-start.29 = (bf16[2048,128]{1,0:T(8,128)(2,1)S(1)}, bf16[2048,128]{1,0:T(8,128)(2,1)S(1)}, u32[]{:S(2)}, u32[]{:S(2)}) collective-permute-start(bf16[2048,128]{1,0:T(8,128)(2,1)S(1)} %slice.39), channel_id=1, source_target_pairs={{0,8},{1,9},{2,10},{3,11},{4,12},{5,13},{6,14},{7,15},{8,24},{9,25... | collective-permute-start | bytes 1572872 | tf_op jit(solution)/shard_map/ppermute | solution.py:269
  154.3 15.5 %collective-permute-start.28 = (bf16[2048,128]{1,0:T(8,128)(2,1)S(1)}, bf16[2048,128]{1,0:T(8,128)(2,1)S(1)}, u32[]{:S(2)}, u32[]{:S(2)}) collective-permute-start(bf16[2048,128]{1,0:T(8,128)(2,1)S(1)} %slice.38), channel_id=1, source_target_pairs={{0,4},{1,5},{2,6},{3,7},{4,0},{5,1},{6,2},{7,3},{8,12},{9,13},{10,... | collective-permute-start | bytes 1572872 | tf_op jit(solution)/shard_map/ppermute | solution.py:273
  166.8 13.5 %collective-permute-start.27 = (bf16[3,512,128]{2,1,0:T(8,128)(2,1)}, bf16[3,512,128]{2,1,0:T(8,128)(2,1)S(1)}, u32[]{:S(2)}, u32[]{:S(2)}) collective-permute-start(bf16[3,512,128]{2,1,0:T(8,128)(2,1)} %get-tuple-element.121), channel_id=1, source_target_pairs={{0,1},{1,0},{2,3},{3,2},{4,5},{5,4},{6,7},{7,6},{8,9},{9,8},{10,11... | collective-permute-start | bytes 1179656 | tf_op jit(solution)/shard_map/ppermute | solution.py:273
  169.8 11.9 %collective-permute-start.23 = (bf16[11,512,128]{2,1,0:T(8,128)(2,1)S(1)}, bf16[11,512,128]{2,1,0:T(8,128)(2,1)S(1)}, u32[]{:S(2)}, u32[]{:S(2)}) collective-permute-start(bf16[11,512,128]{2,1,0:T(8,128)(2,1)S(1)} %copy-done.10), channel_id=1, source_target_pairs={{0,1},{1,0},{2,3},{3,2},{4,5},{5,4},{6,7},{7,6},{8,9},{9,8},{10,11... | collective-permute-start | bytes 4325384 | tf_op jit(solution)/shard_map/ppermute | solution.py:273
  179.8 1.9 %collective-permute-start.30 = (bf16[2,512,128]{2,1,0:T(8,128)(2,1)}, bf16[2,512,128]{2,1,0:T(8,128)(2,1)S(1)}, u32[]{:S(2)}, u32[]{:S(2)}) collective-permute-start(bf16[2,512,128]{2,1,0:T(8,128)(2,1)} %get-tuple-element.127), channel_id=1, source_target_pairs={{0,1},{1,0},{2,3},{3,2},{4,5},{5,4},{6,7},{7,6},{8,9},{9,8},{10,11... | collective-permute-start | bytes 786440 | tf_op jit(solution)/shard_map/ppermute | solution.py:273
  (16 other events, 98.4 us)
